TPU v7x, 128 devices: a whole 4x4x4 slice. The times are simulated.
128 devices in a mesh: tensor: 4 (over z), island: 8 (over y, core), region: 4 (over x).
Axes of the slice: x: 4, y: 4, z: 4, core: 2. Of those that a mesh axis runs over, the one named last changes fastest.
Arguments:
- global_params: float32 [512, 16384], P(None, 'tensor'), may hold values from -6 to 6
- local_params: bfloat16 [4, 8, 512, 16384], P('region', 'island', None, 'tensor'), may hold values from -6 to 6
- error_buf: float32 [4, 8, 512, 16384], P('region', 'island', None, 'tensor'), may hold values from -6 to 6
- momentum: float32 [512, 16384], P(('island', 'region'), 'tensor'), may hold values from -6 to 6
- kept: int32 [4, 8, 4, 16], P('region', 'island', 'tensor'), may hold values from 0 to 127, as said below
- counts: int32 [4, 8, 4], P('region', 'island', 'tensor'), may hold values from 1 to 16
Outputs:
- new_params: float32 [512, 16384], P(None, 'tensor')
- new_error: float32 [4, 8, 512, 16384], P('region', 'island', None, 'tensor')
- new_momentum: float32 [512, 16384], P(('island', 'region'), 'tensor')
Inputs may be any that keep to these rules, and one draw needn't show every extreme that they name: The first counts[r, i, t] entries of kept[r, i, t] are distinct block numbers; the list of one device is at most 16 long and some device's list is exactly 16 long.
All inputs are finite; a program needn't handle non-finite values.
Results may differ from a plain program's by a relative error of at most 0.00085.
Values may be sent and summed in bfloat16 or wider, within the bound.
No kernel may reach another device: no remote copies, remote signals or barrier semaphores. Data moves between devices by JAX's collectives and lax.ppermute only.
A program may use at most 128 MiB of HBM per device.

v0:
```python
import jax
import jax.numpy as jnp
from jax import lax
from jax.sharding import PartitionSpec as P

BLOCK = 128


def to_blocks(tile, block):
    rows, cols = tile.shape
    return (
        tile.reshape(rows // block, block, cols // block, block)
        .transpose(0, 2, 1, 3)
        .reshape(-1, block, block)
    )


def from_blocks(blocks, rows, cols, block):
    return (
        blocks.reshape(rows // block, cols // block, block, block)
        .transpose(0, 2, 1, 3)
        .reshape(rows, cols)
    )


def per_device(global_params, local_params, error_buf, momentum, kept, counts):
    rows, cols = global_params.shape
    block = BLOCK
    share_rows = momentum.shape[0]
    col_blocks = cols // block
    numbers = rows // block * col_blocks
    acc = 0.95 * error_buf[0, 0] + (global_params - local_params[0, 0].astype(jnp.float32))
    ids = kept.reshape(-1)
    slots = ids.shape[0]
    live = jnp.arange(slots, dtype=jnp.int32) < counts.reshape(())
    onehot = (ids[:, None] == jnp.arange(numbers, dtype=jnp.int32)[None, :]) & live[:, None]
    chosen = jnp.any(onehot, axis=0).reshape(rows // block, col_blocks)
    chosen = jnp.repeat(jnp.repeat(chosen, block, axis=0), block, axis=1)
    rounded_half = acc.astype(jnp.bfloat16)
    rounded = lax.optimization_barrier(rounded_half).astype(jnp.float32)
    message = jnp.where(chosen, rounded, jnp.float32(0.0))
    new_error = (acc - message)[None, None]
    total_islands = lax.axis_size(("island", "region"))
    position = lax.axis_index(("island", "region"))
    picked = to_blocks(rounded_half, block)[ids]
    picked = jnp.where(live[:, None, None], picked, jnp.zeros_like(picked))
    all_vals, all_ids, all_live = (
        lax.all_gather(picked, ("island", "region"), axis=0, tiled=True),
        lax.all_gather(ids, ("island", "region"), axis=0, tiled=True),
        lax.all_gather(live.astype(jnp.int32), ("island", "region"), axis=0, tiled=True),
    )
    table = (
        (all_ids[:, None] == jnp.arange(numbers, dtype=jnp.int32)[None, :])
        & (all_live[:, None] > 0)
    ).astype(jnp.bfloat16)
    summed = jnp.einsum("kn,kab->nab", table, all_vals, preferred_element_type=jnp.float32)
    dense = from_blocks(summed, rows, cols, block)
    share = lax.dynamic_slice_in_dim(dense, position * share_rows, share_rows, 0)
    average = share / total_islands
    new_momentum = 0.9 * momentum + average
    base = lax.dynamic_slice_in_dim(global_params, position * share_rows, share_rows, 0)
    updated = base - 0.7 * (average + 0.9 * new_momentum)
    new_params = lax.all_gather(updated, ("island", "region"), axis=0, tiled=True)
    return (new_params, new_error, new_momentum)


def solution(mesh):
    return jax.shard_map(
        per_device,
        mesh=mesh,
        in_specs=(
            P(None, "tensor"),
            P("region", "island", None, "tensor"),
            P("region", "island", None, "tensor"),
            P(("island", "region"), "tensor"),
            P("region", "island", "tensor", None),
            P("region", "island", "tensor"),
        ),
        out_specs=(
            P(None, "tensor"),
            P("region", "island", None, "tensor"),
            P(("island", "region"), "tensor"),
        ),
        check_vma=False,
    )
```

profile of v0, /device:TPU:1, one launch (start us, length us, event | category | flops | bytes accessed | tf_op | source)
XLA Modules:
  0.0 203.2 jit_solution(1436706892303509801)
XLA Ops:
  7.2 0.0 all-gather.4.cloned.1.call-start
  7.9 11.5 %fusion.1 = bf16[512,4096]{1,0:T(8,128)(2,1)} fusion(f32[512,4096]{1,0:T(8,128)} %param.6, bf16[1,1,512,4096]{3,2,1,0:T(8,128)(2,1)} %param.7, f32[1,1,512,4096]{3,2,1,0:T(8,128)} %param.8), kind=kLoop, calls=%fused_computation.6 | loop fusion | flops 10485760 | bytes 25165824 | tf_op jit(solution)/shard_map/convert_element_type | solution.py:39
  19.3 3.4 %copy.18 = bf16[64,8,32,128]{3,2,1,0:T(8,128)(2,1)S(1)} copy(bf16[64,8,32,128]{3,1,2,0:T(8,128)(2,1)} %bitcast.50) | data formatting | bytes 8388608
  22.8 0.0 copy-start.1
  22.8 0.0 copy-start.2
  22.8 0.9 bitcast_bitcast_fusion
  23.7 3.6 %copy.15 = bf16[4,32,128,128]{3,2,1,0:T(8,128)(2,1)} copy(bf16[4,32,128,128]{3,1,2,0:T(8,128)(2,1)S(1)} %bitcast_bitcast_fusion) | data formatting | bytes 8388608 | tf_op jit(solution)/shard_map/transpose | solution.py:13
  27.3 0.0 copy-done.1
  27.4 2.8 %gather_fusion = bf16[16,128,128]{2,1,0:T(8,128)(2,1)S(1)} fusion(bf16[128,128,128]{2,1,0:T(8,128)(2,1)} %bitcast.55, s32[1024]{0:T(1024)S(1)} %pad_clamp_fusion), kind=kCustom, calls=%fused_computation | custom fusion | bytes 1048640 | tf_op jit(solution)/shard_map/gather | solution.py:45
  30.2 1.1 copy_select_fusion
  31.3 0.0 all-gather.4.cloned.1.call-update
  31.3 0.0 all-gather.6.cloned.1.call-start
  31.4 0.0 copy-done.2
  31.4 0.7 dynamic-slice
  32.8 0.1 convert_dynamic-update-slice_fusion
  32.9 0.1 bitcast_dynamic-update-slice_fusion
  33.0 17.1 %all-reduce.2 = (s32[512]{0:T(512)S(1)}, s32[512]{0:T(512)S(1)}) all-reduce(s32[512]{0:T(512)S(1)} %bitcast_dynamic-update-slice_fusion, s32[512]{0:T(512)S(1)} %convert_dynamic-update-slice_fusion), channel_id=2, replica_groups=mesh['tensor'=4,'island'=8,'region'=4] {'island','region'}, use_global_device_ids=true, to_apply=%add | all-reduce | flops 1024 | bytes 8192
  50.1 66.0 %all-gather.4.cloned.1.call-done = bf16[512,128,128]{2,0,1:T(8,128)(2,1)} async-done(((bf16[16,128,128]{2,0,1:T(8,128)(2,1)}), bf16[512,128,128]{2,0,1:T(8,128)(2,1)}) %all-gather.4.cloned.1.call-update) | async-done | bytes 16777232 | tf_op jit(solution)/shard_map/all_gather | solution.py:48
  116.1 8.1 %fusion.4 = f32[128,128,128]{2,0,1:T(8,128)S(1)} fusion(bf16[512,128,128]{2,0,1:T(8,128)(2,1)} %all-gather.4.cloned.1.call-done, s32[512]{0:T(512)S(1)} %get-tuple-element.3, pred[512]{0:T(512)(128)(4,1)S(1)} %broadcast_compare_fusion), kind=kOutput, calls=%fused_computation.14 | convolution fusion | flops 2147614720 | bytes 25168384 | tf_op jit(solution)/shard_map/kn,kab->nab/dot_general | solution.py:56
  124.2 1.3 copy.17
  125.5 0.0 copy-start
  125.5 8.1 %copy.24 = f32[64,8,32,128]{3,1,2,0:T(8,128)S(1)} copy(f32[64,8,32,128]{3,2,1,0:T(8,128)S(1)} %bitcast.51) | data formatting | bytes 16777216
  133.6 0.0 copy-done
  133.6 1.8 multiply_subtract_fusion
  135.5 0.0 all-gather.6.cloned.1.call-update
  135.5 0.1 fusion.9
  135.6 0.1 reshape.86
  135.7 6.9 %broadcast_in_dim.34 = pred[512,32,128]{2,1,0:T(8,128)(4,1)S(1)} broadcast(pred[512,32]{1,0:T(8,128)(4,1)S(1)} %bitcast.56), dimensions={0,1} | broadcast | bytes 2113536 | tf_op jit(solution)/shard_map/broadcast_in_dim | solution.py:38
  142.6 13.3 %subtract_bitcast_fusion = f32[1,1,512,4096]{3,2,1,0:T(8,128)} fusion(bf16[512,4096]{1,0:T(8,128)(2,1)} %fusion.1, pred[64,8,32,128]{3,2,1,0:T(8,128)(4,1)S(1)} %bitcast.54, f32[512,4096]{1,0:T(8,128)} %param.6, bf16[1,1,512,4096]{3,2,1,0:T(8,128)(2,1)} %param.7, f32[1,1,512,4096]{3,2,1,0:T(8,128)} %param.8), kind=kLoop, calls=%fused_computation.4 | loop fusion | flops 14680064 | bytes 35651584 | tf_op jit(solution)/shard_map/broadcast_in_dim | solution.py:42
  156.0 32.6 %all-gather.6.cloned.1.call-done = f32[512,4096]{1,0:T(8,128)} async-done(((f32[16,4096]{1,0:T(8,128)}), f32[512,4096]{1,0:T(8,128)}) %all-gather.6.cloned.1.call-update) | async-done | bytes 8388624 | tf_op jit(solution)/shard_map/all_gather | solution.py:63
  188.6 7.8 %copy.30 = f32[512,4096]{1,0:T(8,128)} copy(f32[512,4096]{1,0:T(8,128)} %all-gather.6.cloned.1.call-done) | data formatting | bytes 16777216
  (7 shorter events, 0.1 us)
Async XLA Ops:
  7.2 108.9 %all-gather.4.cloned.1.call-start = ((), (), s32[]{:S(2)}) async-start(), calls=%async_computation | async-start | bytes 17301504 | tf_op jit(solution)/shard_map/all_gather | solution.py:48
  22.8 4.6 %copy-start.1 = (s32[1,1,1,16]{3,2,1,0:T(1,128)S(1)}, s32[1,1,1,16]{3,2,1,0:T(1,128)}, u32[]{:S(2)}) copy-start(s32[1,1,1,16]{3,2,1,0:T(1,128)} %param.10) | copy-start | bytes 196
  22.8 8.6 %copy-start.2 = (u32[128]{0:T(128)S(1)}, u32[128]{0:T(128)}, u32[]{:S(2)}) copy-start(u32[128]{0:T(128)} %constant.43) | copy-start | bytes 1540
  31.3 157.3 %all-gather.6.cloned.1.call-start = ((), (), s32[]{:S(2)}) async-start(), calls=%async_computation.1 | async-start | bytes 8650752 | tf_op jit(solution)/shard_map/all_gather | solution.py:63
  125.5 8.1 %copy-start = (f32[16,4096]{1,0:T(8,128)S(1)}, f32[16,4096]{1,0:T(8,128)}, u32[]{:S(2)}) copy-start(f32[16,4096]{1,0:T(8,128)} %param.9) | copy-start | bytes 786436
Sparse Core Ops, SparseCore 0:
  31.4 84.5 all-gather.3
  135.6 52.9 all-gather.5
where the time goes:
time: 204 us; the launch traced here: 203 us
  waiting for transfers between devices  98.7 us (48%)
  local copies, waits for them, and re-layouts  35.8 us (18%)
  other arithmetic  28 us (14%)
  blocking collectives  17.1 us (8%)
  between operations  15.5 us (8%)
  matrix products  8.1 us (4%)
    all_gather x1, waiting for transfers between devices, per_device(): lax.all_gather(picked, ('island', 'region'), axis=0, tiled=True)  66 us
    all_gather x1, waiting for transfers between devices, per_device(): lax.all_gather(updated, ('island', 'region'), axis=0, tiled=True)  32.6 us
    unnamed x13, local copies, waits for them, and re-layouts  20.1 us
    unnamed x1, blocking collectives  17.1 us
    broadcast_in_dim x1, other arithmetic, per_device(): new_error = (acc - message)[None, None]  13.3 us
    convert_element_type x1, other arithmetic, per_device(): rounded_half = acc.astype(jnp.bfloat16)  11.5 us
    dot_general x1, matrix products, per_device(): jnp.einsum('kn,kab->nab', table, all_vals, preferred_element_type=jnp.flo...  8.1 us
    broadcast_in_dim x2, local copies, waits for them, and re-layouts, per_device(): chosen = jnp.repeat(jnp.repeat(chosen, block, axis=0), block, axis=1)  6.93 us
  transfers between devices with their start and end apart: 2, of which 2 were waited for; matrix products, arithmetic and copies ran while one was open for 10% of the time, Pallas kernels for 0%

commit v1 on v0

v1 whole, which is shorter than its diff:
```python
import functools

import jax
import jax.numpy as jnp
from jax import lax
from jax.experimental import pallas as pl
from jax.experimental.pallas import tpu as pltpu
from jax.sharding import PartitionSpec as P

BLOCK = 128
PARTS = 4
DEVICES = 32
EXTRA = 16
AXES = ("island", "region")
SCALE = 2.0**24
MIB = 2**20
F32 = jnp.float32
BF16 = jnp.bfloat16


def place():
    island = lax.axis_index("island")
    return island // 2, island % 2, lax.axis_index("region")


def move(array, step):
    pairs = []
    for p in range(DEVICES):
        y, c, x = p // 8, p // 4 % 2, p % 4
        y, c, x = step(y, c, x)
        pairs.append((p, 8 * (y % 4) + 4 * (c % 2) + x % 4))
    return lax.ppermute(array, AXES, pairs)


def encode(v):
    v = v * SCALE
    s = v * v
    return jnp.where(v < 0, -(s * s), s * s).astype(BF16)


def decode(code):
    w = code.astype(F32)
    v = lax.rsqrt(lax.rsqrt(jnp.abs(w))) * (1.0 / SCALE)
    return jnp.where(w < 0, -v, v)


def pick(index, choices):
    out = choices[-1]
    for i in range(len(choices) - 2, -1, -1):
        out = jnp.where(index == i, choices[i], out)
    return out


def pack_kernel(ids, count, pos, g, l, e, mom, pay, m0, m1, m2, m3, gb, lb, eb, sems):
    y, x = pos[0], pos[2]
    slots = gb.shape[0]
    copies = []
    for k in range(slots):
        rows = pl.ds(pl.multiple_of(ids[k] // 32 * BLOCK, BLOCK), BLOCK)
        cols = pl.ds(pl.multiple_of(ids[k] % 32 * BLOCK, BLOCK), BLOCK)
        copies.append([
            pltpu.make_async_copy(src.at[rows, cols], dst.at[k], sems.at[i, k])
            for i, (src, dst) in enumerate(((g, gb), (l, lb), (e, eb)))
        ])
        for copy in copies[-1]:
            copy.start()
    for d, out in enumerate((m0, m1, m2, m3)):
        out[...] = pick((y + d) % 4, [mom[4 * q : 4 * q + 4, :] for q in range(4)])
    lane = lax.broadcasted_iota(jnp.int32, (EXTRA, BLOCK), 1)
    vec = jnp.zeros((EXTRA, BLOCK), F32)
    for k in range(slots):
        vec = jnp.where(lane % 64 // 4 == k, ids[k].astype(F32), vec)
    vec = jnp.where(lane // 64 == x % 2, vec, 0.0).astype(BF16)
    for p in range(DEVICES):
        pay[p, 64 : 64 + EXTRA, :] = vec
    for group in range(slots // 4):
        for k in range(4 * group, 4 * group + 4):
            for copy in copies[k]:
                copy.wait()
        for r in range(8):
            rows = slice(16 * r, 16 * r + 16)
            tiles = []
            for k in range(4 * group, 4 * group + 4):
                acc = 0.95 * eb[k, rows, :] + (gb[k, rows, :] - lb[k, rows, :].astype(F32))
                tiles.append(jnp.where(k < count[0], acc, 0.0))
            for q in range(4):
                tile = jnp.concatenate([t[4 * q : 4 * q + 4] for t in tiles], axis=0)
                pay[8 * q + r, 16 * group : 16 * group + 16, :] = tile.astype(BF16)


def share_kernel(pos, recv, g, m0, m1, m2, m3, code, n0, n1, n2, n3, gb, mb, nb, sems):
    y, c, x = pos[0], pos[1], pos[2]
    r = 4 * c + x
    copies = []
    for q in range(4):
        rows = pl.ds(pl.multiple_of(q * BLOCK + 16 * r, 16), 16)
        copies.append(pltpu.make_async_copy(g.at[rows, :], gb.at[q], sems.at[q]))
        copies[-1].start()
    for d, m in enumerate((m0, m1, m2, m3)):
        mb[d] = m[...]
    row = lax.broadcasted_iota(jnp.int32, (512, BLOCK), 0)
    lane = lax.broadcasted_iota(jnp.int32, (512, BLOCK), 1)
    want = (row // 4 % 4 * 32 + row // 16) * 4 + row % 4
    want = (want - lane % 4).astype(F32)
    total = jnp.zeros((512, BLOCK), F32)
    for i in range(0, DEVICES, 4):
        halves = []
        for h in (i, i + 2):
            pair = recv[h, 64 : 64 + EXTRA, :].astype(F32) + recv[h + 1, 64 : 64 + EXTRA, :].astype(F32)
            halves.append((want == 4.0 * pair[0:1, :]).astype(F32).astype(BF16))
        table = jnp.concatenate(halves, axis=1)
        values = jnp.concatenate([recv[i + s, 0:64, :] for s in range(4)], axis=0)
        total = total + jnp.dot(table, values, preferred_element_type=F32)
    for copy in copies:
        copy.wait()
    for b in range(32):
        cols = slice(BLOCK * b, BLOCK * b + BLOCK)
        average = total[16 * b : 16 * b + 16, :] * (1.0 / DEVICES)
        mom = jnp.concatenate([mb[(y - q) % 4, :, cols] for q in range(4)], axis=0)
        base = jnp.concatenate(
            [pick(y, [gb[q, 4 * s : 4 * s + 4, cols] for s in range(4)]) for q in range(4)], axis=0
        )
        new_mom = 0.9 * mom + average
        code[:, cols] = encode(base - 0.7 * (average + 0.9 * new_mom))
        for q in range(4):
            nb[q, :, cols] = new_mom[4 * q : 4 * q + 4, :]
    for d, n in enumerate((n0, n1, n2, n3)):
        n[...] = nb[(y + d) % 4]


def error_kernel(ids, count, g, l, e, out, mask):
    i, j = pl.program_id(0), pl.program_id(1)
    wide = g.shape[1] // BLOCK

    @pl.when((i == 0) & (j == 0))
    def _():
        for n in range(mask.shape[0]):
            mask[n] = jnp.int32(0)
        for k in range(ids.shape[0]):

            @pl.when(k < count[0])
            def _():
                mask[ids[k]] = jnp.int32(1)

    for b in range(wide):
        cols = slice(BLOCK * b, BLOCK * b + BLOCK)
        acc = 0.95 * e[:, cols] + (g[:, cols] - l[:, cols].astype(F32))
        kept = mask[i * 32 + j * wide + b] > 0
        out[:, cols] = acc - jnp.where(kept, acc.astype(BF16).astype(F32), 0.0)


def spread_kernel(pos, g0, g1, g2, g3, s0, s1, s2, s3, n0, n1, n2, n3, out, new_mom, buf, nb, sems):
    y, c, x = pos[0], pos[1], pos[2]
    step = pl.program_id(0)
    core, col = step // 4, step % 4
    copies = [
        [
            pltpu.make_async_copy(src, buf.at[slot, d], sems.at[slot, d])
            for d, src in enumerate(group)
        ]
        for slot, group in ((c, (g0, g1, g2, g3)), (1 - c, (s0, s1, s2, s3)))
    ]

    @pl.when(step == 0)
    def _():
        for group in copies:
            for copy in group:
                copy.start()
        for d, n in enumerate((n0, n1, n2, n3)):
            nb[(y - d) % 4] = n[...]
        for q in range(4):
            new_mom[4 * q : 4 * q + 4, :] = nb[q]

    @pl.when(step % 4 == 0)
    def _():
        for d in range(4):
            pltpu.make_async_copy(g0, buf.at[core, d], sems.at[core, d]).wait()

    dx = (x - col) % 4
    places = []
    for q in range(4):
        dy = (y - q) % 4
        first, second = jnp.where(core == 0, dy, dx), jnp.where(core == 0, dx, dy)
        places.append((first, pl.ds(pl.multiple_of(second * 16, 16), 16)))

    width = 256

    def body(i, _):
        cols = pl.ds(pl.multiple_of(i * width, width), width)
        parts = [decode(buf[core, first, rows, cols]) for first, rows in places]
        for q in range(4):
            out[q, :, cols] = jnp.concatenate([p[4 * q : 4 * q + 4, :] for p in parts], axis=0)
        return 0

    lax.fori_loop(0, out.shape[2] // width, body, 0, unroll=2)


def smem():
    return pl.BlockSpec(memory_space=pltpu.SMEM)


def vmem():
    return pl.BlockSpec(memory_space=pltpu.VMEM)


def hbm():
    return pl.BlockSpec(memory_space=pl.ANY)


def params(mib):
    return pltpu.CompilerParams(vmem_limit_bytes=mib * MIB)


def per_device(global_params, local_params, error_buf, momentum, kept, counts):
    rows, cols = global_params.shape
    local, error = local_params.reshape(rows, cols), error_buf.reshape(rows, cols)
    ids, count = kept.reshape(-1), counts.reshape(-1)
    slots = ids.shape[0]
    y, c, x = place()
    pos = jnp.stack([y, c, x]).astype(jnp.int32)
    sds = jax.ShapeDtypeStruct
    quarter = sds((4, cols), F32)

    pay, m0, m1, m2, m3 = pl.pallas_call(
        pack_kernel,
        out_shape=(sds((DEVICES, 64 + EXTRA, BLOCK), BF16),) + (quarter,) * 4,
        in_specs=[smem(), smem(), smem(), hbm(), hbm(), hbm(), vmem()],
        out_specs=(vmem(),) * 5,
        scratch_shapes=[
            pltpu.VMEM((slots, BLOCK, BLOCK), F32),
            pltpu.VMEM((slots, BLOCK, BLOCK), BF16),
            pltpu.VMEM((slots, BLOCK, BLOCK), F32),
            pltpu.SemaphoreType.DMA((3, slots)),
        ],
        compiler_params=params(16),
        cost_estimate=pl.CostEstimate(flops=2 * MIB, bytes_accessed=4 * MIB, transcendentals=0),
        name="pack",
    )(ids, count, pos, global_params, local, error, momentum)

    m1, m2, m3 = [move(m, lambda y, c, x, d=d: (y + d, c, x)) for d, m in ((1, m1), (2, m2), (3, m3))]
    recv = lax.all_to_all(pay, AXES, 0, 0, tiled=True)

    code, n0, n1, n2, n3 = pl.pallas_call(
        share_kernel,
        out_shape=(sds((16, cols), BF16),) + (quarter,) * 4,
        in_specs=[smem(), vmem(), hbm()] + [vmem()] * 4,
        out_specs=(vmem(),) * 5,
        scratch_shapes=[
            pltpu.VMEM((4, 16, cols), F32),
            pltpu.VMEM((4, 4, cols), F32),
            pltpu.VMEM((4, 4, cols), F32),
            pltpu.SemaphoreType.DMA((4,)),
        ],
        compiler_params=params(16),
        cost_estimate=pl.CostEstimate(flops=256 * MIB, bytes_accessed=4 * MIB, transcendentals=0),
        name="share",
    )(pos, recv, global_params, m0, m1, m2, m3)

    first = [
        move(code, lambda y, c, x, d=d: (y, c, x + d) if c == 0 else (y + d, c, x)) for d in (1, 2, 3)
    ]
    group = jnp.concatenate([code] + first, axis=0)
    own = [group] + [
        move(group, lambda y, c, x, d=d: (y + d, c, x) if c == 0 else (y, c, x + d)) for d in (1, 2, 3)
    ]
    other = [move(g, lambda y, c, x: (y, c + 1, x)) for g in own]
    n1, n2, n3 = [move(n, lambda y, c, x, d=d: (y + d, c, x)) for d, n in ((1, n1), (2, n2), (3, n3))]

    wide = 1024
    spec = pl.BlockSpec((BLOCK, wide), lambda i, j, *_: (i, j))
    new_error = pl.pallas_call(
        error_kernel,
        out_shape=sds((rows, cols), F32),
        grid_spec=pltpu.PrefetchScalarGridSpec(
            num_scalar_prefetch=2,
            grid=(rows // BLOCK, cols // wide),
            in_specs=[spec] * 3,
            out_specs=spec,
            scratch_shapes=[pltpu.SMEM((rows // BLOCK * (cols // BLOCK),), jnp.int32)],
        ),
        compiler_params=params(16),
        cost_estimate=pl.CostEstimate(flops=8 * MIB, bytes_accessed=28 * MIB, transcendentals=0),
        name="error",
    )(ids, count, global_params, local, error)

    new_params, new_momentum = pl.pallas_call(
        spread_kernel,
        out_shape=(sds((4, BLOCK, cols), F32), sds((16, cols), F32)),
        grid=(8,),
        in_specs=[smem()] + [hbm()] * 8 + [vmem()] * 4,
        out_specs=(
            pl.BlockSpec((4, 16, cols), lambda i: (0, i, 0)),
            pl.BlockSpec((16, cols), lambda i: (0, 0)),
        ),
        scratch_shapes=[
            pltpu.VMEM((2, 4, 64, cols), BF16),
            pltpu.VMEM((4, 4, cols), F32),
            pltpu.SemaphoreType.DMA((2, 4)),
        ],
        compiler_params=params(24),
        cost_estimate=pl.CostEstimate(flops=16 * MIB, bytes_accessed=12 * MIB, transcendentals=4 * MIB),
        name="spread",
    )(pos, *own, *other, n0, n1, n2, n3)
    return (
        new_params.reshape(rows, cols),
        new_error.reshape(1, 1, rows, cols),
        new_momentum,
    )


def solution(mesh):
    return jax.shard_map(
        per_device,
        mesh=mesh,
        in_specs=(
            P(None, "tensor"),
            P("region", "island", None, "tensor"),
            P("region", "island", None, "tensor"),
            P(("island", "region"), "tensor"),
            P("region", "island", "tensor", None),
            P("region", "island", "tensor"),
        ),
        out_specs=(
            P(None, "tensor"),
            P("region", "island", None, "tensor"),
            P(("island", "region"), "tensor"),
        ),
        check_vma=False,
    )
```

time: 204 us -> 101 us (0.50)
  waiting for transfers between devices: 98.7 us -> 34.6 us
  other arithmetic: 28 us -> 0.08 us
  starting transfers between devices: 0.08 us -> 25.7 us
  Pallas kernels: 0 us -> 21.8 us
  local copies, waits for them, and re-layouts: 35.8 us -> 16.2 us
  blocking collectives: 17.1 us -> 0 us
  between operations: 15.5 us -> 1.42 us
  matrix products: 8.1 us -> 0 us
    all_gather x2 -> x0, waiting for transfers between devices: 98.6 us -> none  [the longest x1 66 us: per_device(): lax.all_gather(picked, ('island', 'region'), axis=0, tiled=True)]
    ppermute x0 -> x16, waiting for transfers between devices: none -> 34.6 us  [move(): return lax.ppermute(array, AXES, pairs)]
    pallas_call x0 -> x4, Pallas kernels: none -> 21.8 us  [the longest x1 9.2 us: per_device(): pl.pallas_call(error_kernel, out_shape=sds((rows, cols), F32), grid_spec=...]
    unnamed x1 -> x0, blocking collectives: 17.1 us -> none
    ppermute x0 -> x16, starting transfers between devices: none -> 17.1 us  [move(): return lax.ppermute(array, AXES, pairs)]
    broadcast_in_dim x1 -> x0, other arithmetic: 13.3 us -> none  [per_device(): new_error = (acc - message)[None, None]]
    convert_element_type x1 -> x0, other arithmetic: 11.5 us -> none  [per_device(): rounded_half = acc.astype(jnp.bfloat16)]
    all_to_all x0 -> x1, starting transfers between devices: none -> 8.6 us  [per_device(): recv = lax.all_to_all(pay, AXES, 0, 0, tiled=True)]
  transfers between devices with their start and end apart: 2 -> 17, of which waited for: 2 -> 7; matrix products, arithmetic and copies ran while one was open for 10% -> 0% of each run, Pallas kernels for 0% -> 9%
where the time goes in v1:
time: 101 us; the launch traced here: 99.7 us
  waiting for transfers between devices  34.6 us (34%)
  starting transfers between devices  25.7 us (25%)
  Pallas kernels  21.8 us (22%)
  local copies, waits for them, and re-layouts  16.2 us (16%)
  between operations  1.42 us (1%)
    ppermute x16, waiting for transfers between devices, move(): return lax.ppermute(array, AXES, pairs)  34.6 us
    ppermute x16, starting transfers between devices, move(): return lax.ppermute(array, AXES, pairs)  17.1 us
    unnamed x21, local copies, waits for them, and re-layouts  16.2 us
    pallas_call x1, Pallas kernels, per_device(): pl.pallas_call(error_kernel, out_shape=sds((rows, cols), F32), grid_spec=...  9.2 us
    all_to_all x1, starting transfers between devices, per_device(): recv = lax.all_to_all(pay, AXES, 0, 0, tiled=True)  8.6 us
    pallas_call x1, Pallas kernels, per_device(): pl.pallas_call(spread_kernel, out_shape=(sds((4, BLOCK, cols), F32), sds(...  7.87 us
    pallas_call x1, Pallas kernels, per_device(): pl.pallas_call(pack_kernel, out_shape=(sds((DEVICES, 64 + EXTRA, BLOCK),...  3.01 us
  transfers between devices with their start and end apart: 17, of which 7 were waited for; matrix products, arithmetic and copies ran while one was open for 0% of the time, Pallas kernels for 9%

profile of v1, /device:TPU:1, one launch (start us, length us, event | category | flops | bytes accessed | tf_op | source)
XLA Modules:
  0.0 99.7 jit_solution(7520247514929354107)
XLA Ops:
  1.3 0.1 pad_add_fusion.pos
  1.4 3.4 %copy-done = f32[512,4096]{1,0:T(8,128)S(1)} copy-done((f32[512,4096]{1,0:T(8,128)S(1)}, f32[512,4096]{1,0:T(8,128)}, u32[]{:S(2)}) %copy-start) | copy-done | bytes 8388632
  4.8 3.4 %copy-done.2 = f32[1,1,512,4096]{3,2,1,0:T(8,128)S(1)} copy-done((f32[1,1,512,4096]{3,2,1,0:T(8,128)S(1)}, f32[1,1,512,4096]{3,2,1,0:T(8,128)}, u32[]{:S(2)}) %copy-start.2) | copy-done | bytes 8388632
  8.1 2.2 %copy-done.4 = bf16[1,1,512,4096]{3,2,1,0:T(8,128)(2,1)S(1)} copy-done((bf16[1,1,512,4096]{3,2,1,0:T(8,128)(2,1)S(1)}, bf16[1,1,512,4096]{3,2,1,0:T(8,128)(2,1)}, u32[]{:S(2)}) %copy-start.4) | copy-done | bytes 4194328
  10.3 0.9 copy-done.6
  11.3 0.7 copy-done.7
  11.9 3.0 %pack.1 = (bf16[32,80,128]{2,1,0:T(8,128)(2,1)}, f32[4,4096]{1,0:T(4,128)S(1)}, f32[4,4096]{1,0:T(4,128)S(1)}, f32[4,4096]{1,0:T(4,128)S(1)}, f32[4,4096]{1,0:T(4,128)S(1)}) custom-call(s32[16]{0:T(128)S(1)} %bitcast.15, s32[1]{0:T(128)} %bitcast.9.count, s32[3]{0:T(128)S(1)} %pad_add_fusion.pos, f32[512,4096]{1,0:T(8,128)S(1)} %copy-done, ...), custom_call_target="tpu_custom_call" | custom-call | flops 2097152 | bytes 4194304 | tf_op jit(solution)/shard_map/pack/pallas_call | solution.py:224
  15.0 8.6 %all-to-all-start = ((bf16[32,80,128]{2,1,0:T(8,128)(2,1)}), bf16[32,80,128]{2,1,0:T(8,128)(2,1)S(1)}, u32[]{:S(2)}, u32[]{:S(2)}) async-start(bf16[32,80,128]{2,1,0:T(8,128)(2,1)} %get-tuple-element.15), calls=%async_computation | async-start | bytes 1310720 | tf_op jit(solution)/shard_map/all_to_all | solution.py:241
  23.6 1.5 %collective-permute-start = (f32[4,4096]{1,0:T(4,128)S(1)}, f32[4,4096]{1,0:T(4,128)S(1)}, u32[]{:S(2)}, u32[]{:S(2)}) collective-permute-start(f32[4,4096]{1,0:T(4,128)S(1)} %get-tuple-element.17), channel_id=1, source_target_pairs={{0,8},{1,9},{2,10},{3,11},{4,12},{5,13},{6,14},{7,15},{8,16},{9,17... | collective-permute-start | bytes 196616 | tf_op jit(solution)/shard_map/ppermute | solution.py:32
  25.0 2.4 %collective-permute-start.1 = (f32[4,4096]{1,0:T(4,128)S(1)}, f32[4,4096]{1,0:T(4,128)S(1)}, u32[]{:S(2)}, u32[]{:S(2)}) collective-permute-start(f32[4,4096]{1,0:T(4,128)S(1)} %get-tuple-element.18), channel_id=1, source_target_pairs={{0,16},{1,17},{2,18},{3,19},{4,20},{5,21},{6,22},{7,23},{8,24},{9,... | collective-permute-start | bytes 196616 | tf_op jit(solution)/shard_map/ppermute | solution.py:32
  27.5 1.1 %collective-permute-start.2 = (f32[4,4096]{1,0:T(4,128)S(1)}, f32[4,4096]{1,0:T(4,128)S(1)}, u32[]{:S(2)}, u32[]{:S(2)}) collective-permute-start(f32[4,4096]{1,0:T(4,128)S(1)} %get-tuple-element.19), channel_id=1, source_target_pairs={{0,24},{1,25},{2,26},{3,27},{4,28},{5,29},{6,30},{7,31},{8,0},{9,1... | collective-permute-start | bytes 196616 | tf_op jit(solution)/shard_map/ppermute | solution.py:32
  28.6 5.4 %collective-permute-done.m1 = f32[4,4096]{1,0:T(4,128)S(1)} collective-permute-done((f32[4,4096]{1,0:T(4,128)S(1)}, f32[4,4096]{1,0:T(4,128)S(1)}, u32[]{:S(2)}, u32[]{:S(2)}) %collective-permute-start) | collective-permute-done | bytes 65568 | tf_op jit(solution)/shard_map/ppermute | solution.py:32
  34.0 3.1 %collective-permute-done.1.m2 = f32[4,4096]{1,0:T(4,128)S(1)} collective-permute-done((f32[4,4096]{1,0:T(4,128)S(1)}, f32[4,4096]{1,0:T(4,128)S(1)}, u32[]{:S(2)}, u32[]{:S(2)}) %collective-permute-start.1) | collective-permute-done | bytes 65568 | tf_op jit(solution)/shard_map/ppermute | solution.py:32
  37.2 3.4 %copy-done.1 = f32[512,4096]{1,0:T(8,128)S(1)} copy-done((f32[512,4096]{1,0:T(8,128)S(1)}, f32[512,4096]{1,0:T(8,128)}, u32[]{:S(2)}) %copy-start.1) | copy-done | bytes 8388632
  40.6 1.7 %share.1 = (bf16[16,4096]{1,0:T(8,128)(2,1)S(1)}, f32[4,4096]{1,0:T(4,128)S(1)}, f32[4,4096]{1,0:T(4,128)S(1)}, f32[4,4096]{1,0:T(4,128)S(1)}, f32[4,4096]{1,0:T(4,128)S(1)}) custom-call(s32[3]{0:T(128)S(1)} %pad_add_fusion.pos, bf16[32,80,128]{2,1,0:T(8,128)(2,1)S(1)} %all-to-all-done.recv, f32[512,4096]{1,0:T(8,128)S(1)} %copy-done.1, ...), custom_call_target="tpu_custom_call" | custom-call | flops 268435456 | bytes 4194304 | tf_op jit(solution)/shard_map/share/pallas_call | solution.py:243
  42.3 1.3 %collective-permute-start.5 = (bf16[16,4096]{1,0:T(8,128)(2,1)S(1)}, bf16[16,4096]{1,0:T(8,128)(2,1)S(1)}, u32[]{:S(2)}, u32[]{:S(2)}) collective-permute-start(bf16[16,4096]{1,0:T(8,128)(2,1)S(1)} %get-tuple-element.20), channel_id=1, source_target_pairs={{0,3},{1,0},{2,1},{3,2},{4,28},{5,29},{6,30},{7,31},{8,11},{9,8},{... | collective-permute-start | bytes 393224 | tf_op jit(solution)/shard_map/ppermute | solution.py:32
  43.6 0.5 collective-permute-start.4
  44.1 0.1 collective-permute-start.3
  44.3 6.3 %collective-permute-done.3 = bf16[16,4096]{1,0:T(8,128)(2,1)S(1)} collective-permute-done((bf16[16,4096]{1,0:T(8,128)(2,1)S(1)}, bf16[16,4096]{1,0:T(8,128)(2,1)S(1)}, u32[]{:S(2)}, u32[]{:S(2)}) %collective-permute-start.3) | collective-permute-done | bytes 131104 | tf_op jit(solution)/shard_map/ppermute | solution.py:32
  50.7 1.7 %collective-permute-start.8 = (bf16[64,4096]{1,0:T(8,128)(2,1)S(1)}, bf16[64,4096]{1,0:T(8,128)(2,1)S(1)}, u32[]{:S(2)}, u32[]{:S(2)}) collective-permute-start(bf16[64,4096]{1,0:T(8,128)(2,1)S(1)} %constant_dynamic-update-slice_fusion.g0), channel_id=1, source_target_pairs={{0,24},{1,25},{2,26},{3,27},{4,7},{5,4},{6,5},{7,6},{8,0},{9,1},{1... | collective-permute-start | bytes 1572872 | tf_op jit(solution)/shard_map/ppermute | solution.py:32
  52.4 0.8 collective-permute-start.7
  53.2 0.5 collective-permute-start.6
  53.7 2.9 %collective-permute-start.9 = (bf16[64,4096]{1,0:T(8,128)(2,1)S(1)}, bf16[64,4096]{1,0:T(8,128)(2,1)S(1)}, u32[]{:S(2)}, u32[]{:S(2)}) collective-permute-start(bf16[64,4096]{1,0:T(8,128)(2,1)S(1)} %constant_dynamic-update-slice_fusion.g0), channel_id=1, source_target_pairs={{0,4},{1,5},{2,6},{3,7},{4,0},{5,1},{6,2},{7,3},{8,12},{9,13},{10,... | collective-permute-start | bytes 1572872 | tf_op jit(solution)/shard_map/ppermute | solution.py:32
  56.5 7.6 %collective-permute-done.8.g3 = bf16[64,4096]{1,0:T(8,128)(2,1)S(1)} collective-permute-done((bf16[64,4096]{1,0:T(8,128)(2,1)S(1)}, bf16[64,4096]{1,0:T(8,128)(2,1)S(1)}, u32[]{:S(2)}, u32[]{:S(2)}) %collective-permute-start.8) | collective-permute-done | bytes 524320 | tf_op jit(solution)/shard_map/ppermute | solution.py:32
  64.1 1.2 %collective-permute-start.11 = (bf16[64,4096]{1,0:T(8,128)(2,1)S(1)}, bf16[64,4096]{1,0:T(8,128)(2,1)S(1)}, u32[]{:S(2)}, u32[]{:S(2)}) collective-permute-start(bf16[64,4096]{1,0:T(8,128)(2,1)S(1)} %collective-permute-done.7.g2), channel_id=1, source_target_pairs={{0,4},{1,5},{2,6},{3,7},{4,0},{5,1},{6,2},{7,3},{8,12},{9,13},{10,... | collective-permute-start | bytes 1572872 | tf_op jit(solution)/shard_map/ppermute | solution.py:32
  65.3 2.5 %collective-permute-done.6.g1 = bf16[64,4096]{1,0:T(8,128)(2,1)S(1)} collective-permute-done((bf16[64,4096]{1,0:T(8,128)(2,1)S(1)}, bf16[64,4096]{1,0:T(8,128)(2,1)S(1)}, u32[]{:S(2)}, u32[]{:S(2)}) %collective-permute-start.6) | collective-permute-done | bytes 524320 | tf_op jit(solution)/shard_map/ppermute | solution.py:32
  67.8 3.0 %collective-permute-start.10 = (bf16[64,4096]{1,0:T(8,128)(2,1)S(1)}, bf16[64,4096]{1,0:T(8,128)(2,1)S(1)}, u32[]{:S(2)}, u32[]{:S(2)}) collective-permute-start(bf16[64,4096]{1,0:T(8,128)(2,1)S(1)} %collective-permute-done.6.g1), channel_id=1, source_target_pairs={{0,4},{1,5},{2,6},{3,7},{4,0},{5,1},{6,2},{7,3},{8,12},{9,13},{10,... | collective-permute-start | bytes 1572872 | tf_op jit(solution)/shard_map/ppermute | solution.py:32
  70.8 4.9 %collective-permute-done.13.n1 = f32[4,4096]{1,0:T(4,128)S(1)} collective-permute-done((f32[4,4096]{1,0:T(4,128)S(1)}, f32[4,4096]{1,0:T(4,128)S(1)}, u32[]{:S(2)}, u32[]{:S(2)}) %collective-permute-start.13) | collective-permute-done | bytes 65568 | tf_op jit(solution)/shard_map/ppermute | solution.py:32
  75.8 4.6 %collective-permute-done.14.n2 = f32[4,4096]{1,0:T(4,128)S(1)} collective-permute-done((f32[4,4096]{1,0:T(4,128)S(1)}, f32[4,4096]{1,0:T(4,128)S(1)}, u32[]{:S(2)}, u32[]{:S(2)}) %collective-permute-start.14) | collective-permute-done | bytes 65568 | tf_op jit(solution)/shard_map/ppermute | solution.py:32
  80.4 2.2 %copy-done.5 = bf16[1,1,512,4096]{3,2,1,0:T(8,128)(2,1)S(1)} copy-done((bf16[1,1,512,4096]{3,2,1,0:T(8,128)(2,1)S(1)}, bf16[1,1,512,4096]{3,2,1,0:T(8,128)(2,1)}, u32[]{:S(2)}) %copy-start.5) | copy-done | bytes 4194328
  82.6 9.2 %error.1 = f32[512,4096]{1,0:T(8,128)} custom-call(s32[16]{0:T(128)S(1)} %bitcast.16, s32[1]{0:T(128)} %bitcast.10.count, f32[512,4096]{1,0:T(8,128)S(1)} %copy-done.1, bf16[512,4096]{1,0:T(8,128)(2,1)S(1)} %bitcast.14, f32[512,4096]{1,0:T(8,128)S(1)} %bitcast.12), custom_call_target="tpu_custom_call" | custom-call | flops 8388608 | bytes 29360128 | tf_op jit(solution)/shard_map/error/pallas_call | solution.py:271
  91.8 7.9 %spread.1 = (f32[4,128,4096]{2,1,0:T(8,128)}, f32[16,4096]{1,0:T(8,128)}) custom-call(s32[3]{0:T(128)S(1)} %pad_add_fusion.pos, bf16[64,4096]{1,0:T(8,128)(2,1)S(1)} %constant_dynamic-update-slice_fusion.g0, bf16[64,4096]{1,0:T(8,128)(2,1)S(1)} %collective-permute-done.6.g1, bf16[64,4096]{1,0:T(8,128)(2,1)S(1)} %collective-permute-done.7.g2, ...), custom_call_target="tpu_custom_call" | custom-call | flops 16777216 | bytes 12582912 | tf_op jit(solution)/shard_map/spread/pallas_call | solution.py:286
  (29 shorter events, 0.1 us)
Async XLA Ops:
  1.4 3.4 %copy-start = (f32[512,4096]{1,0:T(8,128)S(1)}, f32[512,4096]{1,0:T(8,128)}, u32[]{:S(2)}) copy-start(f32[512,4096]{1,0:T(8,128)} %g.5) | copy-start | bytes 25165828
  4.8 3.4 %copy-start.2 = (f32[1,1,512,4096]{3,2,1,0:T(8,128)S(1)}, f32[1,1,512,4096]{3,2,1,0:T(8,128)}, u32[]{:S(2)}) copy-start(f32[1,1,512,4096]{3,2,1,0:T(8,128)} %param.8) | copy-start | bytes 25165828
  8.1 2.2 %copy-start.4 = (bf16[1,1,512,4096]{3,2,1,0:T(8,128)(2,1)S(1)}, bf16[1,1,512,4096]{3,2,1,0:T(8,128)(2,1)}, u32[]{:S(2)}) copy-start(bf16[1,1,512,4096]{3,2,1,0:T(8,128)(2,1)} %param.7) | copy-start | bytes 12582916
  10.3 0.9 copy-start.6
  11.3 0.7 copy-start.7
  15.0 65.4 %copy-start.8 = (s32[1,1,1,16]{3,2,1,0:T(1,128)S(1)}, s32[1,1,1,16]{3,2,1,0:T(1,128)}, u32[]{:S(2)}) copy-start(s32[1,1,1,16]{3,2,1,0:T(1,128)} %param.10) | copy-start | bytes 196
  15.0 22.2 %all-to-all-start = ((bf16[32,80,128]{2,1,0:T(8,128)(2,1)}), bf16[32,80,128]{2,1,0:T(8,128)(2,1)S(1)}, u32[]{:S(2)}, u32[]{:S(2)}) async-start(bf16[32,80,128]{2,1,0:T(8,128)(2,1)} %get-tuple-element.15), calls=%async_computation | async-start | bytes 1310720 | tf_op jit(solution)/shard_map/all_to_all | solution.py:241
  23.6 10.5 %collective-permute-start = (f32[4,4096]{1,0:T(4,128)S(1)}, f32[4,4096]{1,0:T(4,128)S(1)}, u32[]{:S(2)}, u32[]{:S(2)}) collective-permute-start(f32[4,4096]{1,0:T(4,128)S(1)} %get-tuple-element.17), channel_id=1, source_target_pairs={{0,8},{1,9},{2,10},{3,11},{4,12},{5,13},{6,14},{7,15},{8,16},{9,17... | collective-permute-start | bytes 196616 | tf_op jit(solution)/shard_map/ppermute | solution.py:32
  25.0 12.1 %collective-permute-start.1 = (f32[4,4096]{1,0:T(4,128)S(1)}, f32[4,4096]{1,0:T(4,128)S(1)}, u32[]{:S(2)}, u32[]{:S(2)}) collective-permute-start(f32[4,4096]{1,0:T(4,128)S(1)} %get-tuple-element.18), channel_id=1, source_target_pairs={{0,16},{1,17},{2,18},{3,19},{4,20},{5,21},{6,22},{7,23},{8,24},{9,... | collective-permute-start | bytes 196616 | tf_op jit(solution)/shard_map/ppermute | solution.py:32
  27.5 9.7 %collective-permute-start.2 = (f32[4,4096]{1,0:T(4,128)S(1)}, f32[4,4096]{1,0:T(4,128)S(1)}, u32[]{:S(2)}, u32[]{:S(2)}) collective-permute-start(f32[4,4096]{1,0:T(4,128)S(1)} %get-tuple-element.19), channel_id=1, source_target_pairs={{0,24},{1,25},{2,26},{3,27},{4,28},{5,29},{6,30},{7,31},{8,0},{9,1... | collective-permute-start | bytes 196616 | tf_op jit(solution)/shard_map/ppermute | solution.py:32
  37.2 3.4 %copy-start.1 = (f32[512,4096]{1,0:T(8,128)S(1)}, f32[512,4096]{1,0:T(8,128)}, u32[]{:S(2)}) copy-start(f32[512,4096]{1,0:T(8,128)} %g.5) | copy-start | bytes 25165828
  40.6 39.8 %copy-start.3 = (f32[1,1,512,4096]{3,2,1,0:T(8,128)S(1)}, f32[1,1,512,4096]{3,2,1,0:T(8,128)}, u32[]{:S(2)}) copy-start(f32[1,1,512,4096]{3,2,1,0:T(8,128)} %param.8) | copy-start | bytes 25165828
  42.3 8.4 %collective-permute-start.5 = (bf16[16,4096]{1,0:T(8,128)(2,1)S(1)}, bf16[16,4096]{1,0:T(8,128)(2,1)S(1)}, u32[]{:S(2)}, u32[]{:S(2)}) collective-permute-start(bf16[16,4096]{1,0:T(8,128)(2,1)S(1)} %get-tuple-element.20), channel_id=1, source_target_pairs={{0,3},{1,0},{2,1},{3,2},{4,28},{5,29},{6,30},{7,31},{8,11},{9,8},{... | collective-permute-start | bytes 393224 | tf_op jit(solution)/shard_map/ppermute | solution.py:32
  43.6 7.0 %collective-permute-start.4 = (bf16[16,4096]{1,0:T(8,128)(2,1)S(1)}, bf16[16,4096]{1,0:T(8,128)(2,1)S(1)}, u32[]{:S(2)}, u32[]{:S(2)}) collective-permute-start(bf16[16,4096]{1,0:T(8,128)(2,1)S(1)} %get-tuple-element.20), channel_id=1, source_target_pairs={{0,2},{1,3},{2,0},{3,1},{4,20},{5,21},{6,22},{7,23},{8,10},{9,11},... | collective-permute-start | bytes 393224 | tf_op jit(solution)/shard_map/ppermute | solution.py:32
  44.1 6.5 %collective-permute-start.3 = (bf16[16,4096]{1,0:T(8,128)(2,1)S(1)}, bf16[16,4096]{1,0:T(8,128)(2,1)S(1)}, u32[]{:S(2)}, u32[]{:S(2)}) collective-permute-start(bf16[16,4096]{1,0:T(8,128)(2,1)S(1)} %get-tuple-element.20), channel_id=1, source_target_pairs={{0,1},{1,2},{2,3},{3,0},{4,12},{5,13},{6,14},{7,15},{8,9},{9,10},{... | collective-permute-start | bytes 393224 | tf_op jit(solution)/shard_map/ppermute | solution.py:32
  50.7 13.5 %collective-permute-start.8 = (bf16[64,4096]{1,0:T(8,128)(2,1)S(1)}, bf16[64,4096]{1,0:T(8,128)(2,1)S(1)}, u32[]{:S(2)}, u32[]{:S(2)}) collective-permute-start(bf16[64,4096]{1,0:T(8,128)(2,1)S(1)} %constant_dynamic-update-slice_fusion.g0), channel_id=1, source_target_pairs={{0,24},{1,25},{2,26},{3,27},{4,7},{5,4},{6,5},{7,6},{8,0},{9,1},{1... | collective-permute-start | bytes 1572872 | tf_op jit(solution)/shard_map/ppermute | solution.py:32
  52.4 11.8 %collective-permute-start.7 = (bf16[64,4096]{1,0:T(8,128)(2,1)S(1)}, bf16[64,4096]{1,0:T(8,128)(2,1)S(1)}, u32[]{:S(2)}, u32[]{:S(2)}) collective-permute-start(bf16[64,4096]{1,0:T(8,128)(2,1)S(1)} %constant_dynamic-update-slice_fusion.g0), channel_id=1, source_target_pairs={{0,16},{1,17},{2,18},{3,19},{4,6},{5,7},{6,4},{7,5},{8,24},{9,25},... | collective-permute-start | bytes 1572872 | tf_op jit(solution)/shard_map/ppermute | solution.py:32
  53.2 14.6 %collective-permute-start.6 = (bf16[64,4096]{1,0:T(8,128)(2,1)S(1)}, bf16[64,4096]{1,0:T(8,128)(2,1)S(1)}, u32[]{:S(2)}, u32[]{:S(2)}) collective-permute-start(bf16[64,4096]{1,0:T(8,128)(2,1)S(1)} %constant_dynamic-update-slice_fusion.g0), channel_id=1, source_target_pairs={{0,8},{1,9},{2,10},{3,11},{4,5},{5,6},{6,7},{7,4},{8,16},{9,17},{1... | collective-permute-start | bytes 1572872 | tf_op jit(solution)/shard_map/ppermute | solution.py:32
  53.7 38.1 %collective-permute-start.9 = (bf16[64,4096]{1,0:T(8,128)(2,1)S(1)}, bf16[64,4096]{1,0:T(8,128)(2,1)S(1)}, u32[]{:S(2)}, u32[]{:S(2)}) collective-permute-start(bf16[64,4096]{1,0:T(8,128)(2,1)S(1)} %constant_dynamic-update-slice_fusion.g0), channel_id=1, source_target_pairs={{0,4},{1,5},{2,6},{3,7},{4,0},{5,1},{6,2},{7,3},{8,12},{9,13},{10,... | collective-permute-start | bytes 1572872 | tf_op jit(solution)/shard_map/ppermute | solution.py:32
  64.1 27.7 %collective-permute-start.12 = (bf16[64,4096]{1,0:T(8,128)(2,1)S(1)}, bf16[64,4096]{1,0:T(8,128)(2,1)S(1)}, u32[]{:S(2)}, u32[]{:S(2)}) collective-permute-start(bf16[64,4096]{1,0:T(8,128)(2,1)S(1)} %collective-permute-done.8.g3), channel_id=1, source_target_pairs={{0,4},{1,5},{2,6},{3,7},{4,0},{5,1},{6,2},{7,3},{8,12},{9,13},{10,... | collective-permute-start | bytes 1572872 | tf_op jit(solution)/shard_map/ppermute | solution.py:32
  64.1 27.7 %collective-permute-start.11 = (bf16[64,4096]{1,0:T(8,128)(2,1)S(1)}, bf16[64,4096]{1,0:T(8,128)(2,1)S(1)}, u32[]{:S(2)}, u32[]{:S(2)}) collective-permute-start(bf16[64,4096]{1,0:T(8,128)(2,1)S(1)} %collective-permute-done.7.g2), channel_id=1, source_target_pairs={{0,4},{1,5},{2,6},{3,7},{4,0},{5,1},{6,2},{7,3},{8,12},{9,13},{10,... | collective-permute-start | bytes 1572872 | tf_op jit(solution)/shard_map/ppermute | solution.py:32
  67.8 24.0 %collective-permute-start.10 = (bf16[64,4096]{1,0:T(8,128)(2,1)S(1)}, bf16[64,4096]{1,0:T(8,128)(2,1)S(1)}, u32[]{:S(2)}, u32[]{:S(2)}) collective-permute-start(bf16[64,4096]{1,0:T(8,128)(2,1)S(1)} %collective-permute-done.6.g1), channel_id=1, source_target_pairs={{0,4},{1,5},{2,6},{3,7},{4,0},{5,1},{6,2},{7,3},{8,12},{9,13},{10,... | collective-permute-start | bytes 1572872 | tf_op jit(solution)/shard_map/ppermute | solution.py:32
  70.8 4.9 %collective-permute-start.13 = (f32[4,4096]{1,0:T(4,128)S(1)}, f32[4,4096]{1,0:T(4,128)S(1)}, u32[]{:S(2)}, u32[]{:S(2)}) collective-permute-start(f32[4,4096]{1,0:T(4,128)S(1)} %get-tuple-element.22), channel_id=1, source_target_pairs={{0,8},{1,9},{2,10},{3,11},{4,12},{5,13},{6,14},{7,15},{8,16},{9,17... | collective-permute-start | bytes 196616 | tf_op jit(solution)/shard_map/ppermute | solution.py:32
  75.8 4.6 %collective-permute-start.14 = (f32[4,4096]{1,0:T(4,128)S(1)}, f32[4,4096]{1,0:T(4,128)S(1)}, u32[]{:S(2)}, u32[]{:S(2)}) collective-permute-start(f32[4,4096]{1,0:T(4,128)S(1)} %get-tuple-element.23), channel_id=1, source_target_pairs={{0,16},{1,17},{2,18},{3,19},{4,20},{5,21},{6,22},{7,23},{8,24},{9,... | collective-permute-start | bytes 196616 | tf_op jit(solution)/shard_map/ppermute | solution.py:32
  80.4 11.4 %collective-permute-start.15 = (f32[4,4096]{1,0:T(4,128)S(1)}, f32[4,4096]{1,0:T(4,128)S(1)}, u32[]{:S(2)}, u32[]{:S(2)}) collective-permute-start(f32[4,4096]{1,0:T(4,128)S(1)} %get-tuple-element.24), channel_id=1, source_target_pairs={{0,24},{1,25},{2,26},{3,27},{4,28},{5,29},{6,30},{7,31},{8,0},{9,1... | collective-permute-start | bytes 196616 | tf_op jit(solution)/shard_map/ppermute | solution.py:32
  80.4 2.2 %copy-start.5 = (bf16[1,1,512,4096]{3,2,1,0:T(8,128)(2,1)S(1)}, bf16[1,1,512,4096]{3,2,1,0:T(8,128)(2,1)}, u32[]{:S(2)}) copy-start(bf16[1,1,512,4096]{3,2,1,0:T(8,128)(2,1)} %param.7) | copy-start | bytes 12582916

commit v2 on v1

--- a/solution.py
+++ b/solution.py
@@ -88,7 +88,7 @@
                 pay[8 * q + r, 16 * group : 16 * group + 16, :] = tile.astype(BF16)
 
 
-def share_kernel(pos, recv, g, m0, m1, m2, m3, code, n0, n1, n2, n3, gb, mb, nb, sems):
+def share_kernel(pos, recv, g, m0, m1, m2, m3, code, nb, gb, mb, sems):
     y, c, x = pos[0], pos[1], pos[2]
     r = 4 * c + x
     copies = []
@@ -124,75 +124,89 @@
         code[:, cols] = encode(base - 0.7 * (average + 0.9 * new_mom))
         for q in range(4):
             nb[q, :, cols] = new_mom[4 * q : 4 * q + 4, :]
-    for d, n in enumerate((n0, n1, n2, n3)):
-        n[...] = nb[(y + d) % 4]
-
-
-def error_kernel(ids, count, g, l, e, out, mask):
-    i, j = pl.program_id(0), pl.program_id(1)
-    wide = g.shape[1] // BLOCK
-
-    @pl.when((i == 0) & (j == 0))
-    def _():
-        for n in range(mask.shape[0]):
-            mask[n] = jnp.int32(0)
-        for k in range(ids.shape[0]):
-
-            @pl.when(k < count[0])
+
+
+def error_kernel(top, ids, count, g, l, e, *refs):
+    out, gb, lb, eb, mask, sems, done = refs[-7:]
+    chunks, high, _ = gb.shape
+    copies = []
+    for i in range(chunks):
+        rows = pl.ds(top + i * high, high)
+        copies.append([
+            pltpu.make_async_copy(src.at[rows, :], dst.at[i], sems.at[n, i])
+            for n, (src, dst) in enumerate(((g, gb), (l, lb), (e, eb)))
+        ])
+        for copy in copies[-1]:
+            copy.start()
+    for n in range(mask.shape[0]):
+        mask[n] = jnp.int32(0)
+    for k in range(ids.shape[0]):
+
+        @pl.when(k < count[0])
+        def _():
+            mask[ids[k]] = jnp.int32(1)
+
+    back = []
+    for i in range(chunks):
+        for copy in copies[i]:
+            copy.wait()
+        first = (top + i * high) // BLOCK * 32
+
+        def body(b, _):
+            cols = pl.ds(pl.multiple_of(b * BLOCK, BLOCK), BLOCK)
+            acc = 0.95 * eb[i, :, cols] + (gb[i, :, cols] - lb[i, :, cols].astype(F32))
+            kept = mask[first + b] > 0
+            eb[i, :, cols] = acc - jnp.where(kept, acc.astype(BF16).astype(F32), 0.0)
+            return 0
+
+        lax.fori_loop(0, 32, body, 0, unroll=4)
+        back.append(pltpu.make_async_copy(eb.at[i], out.at[pl.ds(top + i * high, high), :], done.at[i]))
+        back[-1].start()
+    for copy in back:
+        copy.wait()
+
+
+def spread_kernel(pos, *refs):
+    own, other, (out, stage, sems) = refs[:4], refs[4:8], refs[8:]
+    y, c, x = pos[0], pos[1], pos[2]
+    width = BLOCK
+
+    def unit(slot, tile, parts_of):
+        def body(i, _):
+            cols = pl.ds(pl.multiple_of(i * width, width), width)
+            parts = [decode(part) for part in parts_of(cols)]
+            for q in range(4):
+                stage[slot, q, :, cols] = jnp.concatenate([p[4 * q : 4 * q + 4, :] for p in parts], axis=0)
+            return 0
+
+        lax.fori_loop(0, stage.shape[3] // width, body, 0, unroll=True)
+        rows = pl.ds(pl.multiple_of(tile * 16, 16), 16)
+        pltpu.make_async_copy(stage.at[slot], out.at[:, rows, :], sems.at[slot]).start()
+
+    def shard(ref, index, cols):
+        return ref[pl.ds(pl.multiple_of(index * 16, 16), 16), cols]
+
+    for core in range(2):
+
+        @pl.when(c == core)
+        def _():
+            groups = own if core == 1 else other
+            for d in range(4):
+                unit(4 + d, 4 + (x - d) % 4, lambda cols: [shard(groups[d], (y - q) % 4, cols) for q in range(4)])
+
+        groups0 = own if core == 0 else other
+        for row in range(4):
+
+            @pl.when((c == core) & (y == row))
             def _():
-                mask[ids[k]] = jnp.int32(1)
-
-    for b in range(wide):
-        cols = slice(BLOCK * b, BLOCK * b + BLOCK)
-        acc = 0.95 * e[:, cols] + (g[:, cols] - l[:, cols].astype(F32))
-        kept = mask[i * 32 + j * wide + b] > 0
-        out[:, cols] = acc - jnp.where(kept, acc.astype(BF16).astype(F32), 0.0)
-
-
-def spread_kernel(pos, g0, g1, g2, g3, s0, s1, s2, s3, n0, n1, n2, n3, out, new_mom, buf, nb, sems):
-    y, c, x = pos[0], pos[1], pos[2]
-    step = pl.program_id(0)
-    core, col = step // 4, step % 4
-    copies = [
-        [
-            pltpu.make_async_copy(src, buf.at[slot, d], sems.at[slot, d])
-            for d, src in enumerate(group)
-        ]
-        for slot, group in ((c, (g0, g1, g2, g3)), (1 - c, (s0, s1, s2, s3)))
-    ]
-
-    @pl.when(step == 0)
-    def _():
-        for group in copies:
-            for copy in group:
-                copy.start()
-        for d, n in enumerate((n0, n1, n2, n3)):
-            nb[(y - d) % 4] = n[...]
-        for q in range(4):
-            new_mom[4 * q : 4 * q + 4, :] = nb[q]
-
-    @pl.when(step % 4 == 0)
-    def _():
-        for d in range(4):
-            pltpu.make_async_copy(g0, buf.at[core, d], sems.at[core, d]).wait()
-
-    dx = (x - col) % 4
-    places = []
-    for q in range(4):
-        dy = (y - q) % 4
-        first, second = jnp.where(core == 0, dy, dx), jnp.where(core == 0, dx, dy)
-        places.append((first, pl.ds(pl.multiple_of(second * 16, 16), 16)))
-
-    width = 256
-
-    def body(i, _):
-        cols = pl.ds(pl.multiple_of(i * width, width), width)
-        parts = [decode(buf[core, first, rows, cols]) for first, rows in places]
-        for q in range(4):
-            out[q, :, cols] = jnp.concatenate([p[4 * q : 4 * q + 4, :] for p in parts], axis=0)
-        return 0
-
-    lax.fori_loop(0, out.shape[2] // width, body, 0, unroll=2)
+                def each(d, _):
+                    unit(d, (x - d) % 4, lambda cols: [shard(groups0[(row - q) % 4], d, cols) for q in range(4)])
+                    return 0
+
+                lax.fori_loop(0, 4, each, 0)
+
+    for slot in range(8):
+        pltpu.make_async_copy(stage.at[slot], out.at[:, pl.ds(0, 16), :], sems.at[slot]).wait()
 
 
 def smem():
@@ -209,6 +223,42 @@
 
 def params(mib):
     return pltpu.CompilerParams(vmem_limit_bytes=mib * MIB)
+
+
+def in_hbm(array):
+    return pltpu.with_memory_space_constraint(array, pltpu.HBM)
+
+
+def error_rows(top, count_rows, high, ids, count, g, l, e, before):
+    rows, cols = g.shape
+    chunks = count_rows // high
+    given = [] if before is None else [before]
+    return pl.pallas_call(
+        functools.partial(error_kernel, top),
+        out_shape=jax.ShapeDtypeStruct((rows, cols), F32),
+        in_specs=[smem(), smem()] + [hbm()] * (3 + len(given)),
+        out_specs=hbm(),
+        input_output_aliases={5: 0} if given else {},
+        scratch_shapes=[
+            pltpu.VMEM((chunks, high, cols), F32),
+            pltpu.VMEM((chunks, high, cols), BF16),
+            pltpu.VMEM((chunks, high, cols), F32),
+            pltpu.SMEM((rows // BLOCK * (cols // BLOCK),), jnp.int32),
+            pltpu.SemaphoreType.DMA((3, chunks)),
+            pltpu.SemaphoreType.DMA((chunks,)),
+        ],
+        compiler_params=params(2 + 10 * count_rows * cols // MIB),
+        cost_estimate=pl.CostEstimate(flops=16 * count_rows * cols, bytes_accessed=14 * count_rows * cols, transcendentals=0),
+        name=f"error{top}",
+    )(ids, count, in_hbm(g), in_hbm(l), in_hbm(e), *given)
+
+
+def over_y(array):
+    return lax.all_to_all(array, "island", 0, 0, axis_index_groups=[[0, 2, 4, 6], [1, 3, 5, 7]], tiled=True)
+
+
+CUTS = (0, 192, 320, 512)
+HIGH = 64
 
 
 def per_device(global_params, local_params, error_buf, momentum, kept, counts):
@@ -219,8 +269,8 @@
     y, c, x = place()
     pos = jnp.stack([y, c, x]).astype(jnp.int32)
     sds = jax.ShapeDtypeStruct
+
     quarter = sds((4, cols), F32)
-
     pay, m0, m1, m2, m3 = pl.pallas_call(
         pack_kernel,
         out_shape=(sds((DEVICES, 64 + EXTRA, BLOCK), BF16),) + (quarter,) * 4,
@@ -235,76 +285,59 @@
         compiler_params=params(16),
         cost_estimate=pl.CostEstimate(flops=2 * MIB, bytes_accessed=4 * MIB, transcendentals=0),
         name="pack",
-    )(ids, count, pos, global_params, local, error, momentum)
+    )(ids, count, pos, in_hbm(global_params), in_hbm(local), in_hbm(error), momentum)
 
     m1, m2, m3 = [move(m, lambda y, c, x, d=d: (y + d, c, x)) for d, m in ((1, m1), (2, m2), (3, m3))]
     recv = lax.all_to_all(pay, AXES, 0, 0, tiled=True)
-
-    code, n0, n1, n2, n3 = pl.pallas_call(
+    def part(n, local, before):
+        return error_rows(CUTS[n], CUTS[n + 1] - CUTS[n], HIGH, ids, count, global_params, local, error, before)
+
+    pay, local = lax.optimization_barrier((pay, local))
+    new_error = part(0, local, None)
+    recv, new_error = lax.optimization_barrier((recv, new_error))
+
+    code, new_mom = pl.pallas_call(
         share_kernel,
-        out_shape=(sds((16, cols), BF16),) + (quarter,) * 4,
+        out_shape=(sds((16, cols), BF16), sds((4, 4, cols), F32)),
         in_specs=[smem(), vmem(), hbm()] + [vmem()] * 4,
-        out_specs=(vmem(),) * 5,
-        scratch_shapes=[
-            pltpu.VMEM((4, 16, cols), F32),
-            pltpu.VMEM((4, 4, cols), F32),
-            pltpu.VMEM((4, 4, cols), F32),
-            pltpu.SemaphoreType.DMA((4,)),
-        ],
+        out_specs=(vmem(),) * 2,
+        scratch_shapes=[pltpu.VMEM((4, 16, cols), F32), pltpu.VMEM((4, 4, cols), F32), pltpu.SemaphoreType.DMA((4,))],
         compiler_params=params(16),
         cost_estimate=pl.CostEstimate(flops=256 * MIB, bytes_accessed=4 * MIB, transcendentals=0),
         name="share",
-    )(pos, recv, global_params, m0, m1, m2, m3)
-
+    )(pos, recv, in_hbm(global_params), m0, m1, m2, m3)
+
+    code, local = lax.optimization_barrier((code, local))
+    new_error = part(1, local, new_error)
     first = [
         move(code, lambda y, c, x, d=d: (y, c, x + d) if c == 0 else (y + d, c, x)) for d in (1, 2, 3)
     ]
+    first, new_error = lax.optimization_barrier((first, new_error))
     group = jnp.concatenate([code] + first, axis=0)
-    own = [group] + [
+    group, new_mom, local = lax.optimization_barrier((group, new_mom, local))
+    own = [
         move(group, lambda y, c, x, d=d: (y + d, c, x) if c == 0 else (y, c, x + d)) for d in (1, 2, 3)
     ]
-    other = [move(g, lambda y, c, x: (y, c + 1, x)) for g in own]
-    n1, n2, n3 = [move(n, lambda y, c, x, d=d: (y + d, c, x)) for d, n in ((1, n1), (2, n2), (3, n3))]
-
-    wide = 1024
-    spec = pl.BlockSpec((BLOCK, wide), lambda i, j, *_: (i, j))
-    new_error = pl.pallas_call(
-        error_kernel,
-        out_shape=sds((rows, cols), F32),
-        grid_spec=pltpu.PrefetchScalarGridSpec(
-            num_scalar_prefetch=2,
-            grid=(rows // BLOCK, cols // wide),
-            in_specs=[spec] * 3,
-            out_specs=spec,
-            scratch_shapes=[pltpu.SMEM((rows // BLOCK * (cols // BLOCK),), jnp.int32)],
-        ),
-        compiler_params=params(16),
-        cost_estimate=pl.CostEstimate(flops=8 * MIB, bytes_accessed=28 * MIB, transcendentals=0),
-        name="error",
-    )(ids, count, global_params, local, error)
-
-    new_params, new_momentum = pl.pallas_call(
+    new_mom = over_y(new_mom)
+    other0 = move(group, lambda y, c, x: (y, c + 1, x))
+    new_error = part(2, local, new_error)
+    own[0], new_mom, other0, new_error = lax.optimization_barrier((own[0], new_mom, other0, new_error))
+    other = [other0] + [move(g, lambda y, c, x: (y, c + 1, x)) for g in own]
+
+    new_params = pl.pallas_call(
         spread_kernel,
-        out_shape=(sds((4, BLOCK, cols), F32), sds((16, cols), F32)),
-        grid=(8,),
-        in_specs=[smem()] + [hbm()] * 8 + [vmem()] * 4,
-        out_specs=(
-            pl.BlockSpec((4, 16, cols), lambda i: (0, i, 0)),
-            pl.BlockSpec((16, cols), lambda i: (0, 0)),
-        ),
-        scratch_shapes=[
-            pltpu.VMEM((2, 4, 64, cols), BF16),
-            pltpu.VMEM((4, 4, cols), F32),
-            pltpu.SemaphoreType.DMA((2, 4)),
-        ],
+        out_shape=sds((4, BLOCK, cols), F32),
+        in_specs=[smem()] + [vmem()] * 8,
+        out_specs=hbm(),
+        scratch_shapes=[pltpu.VMEM((8, 4, 16, cols), F32), pltpu.SemaphoreType.DMA((8,))],
         compiler_params=params(24),
         cost_estimate=pl.CostEstimate(flops=16 * MIB, bytes_accessed=12 * MIB, transcendentals=4 * MIB),
         name="spread",
-    )(pos, *own, *other, n0, n1, n2, n3)
+    )(pos, group, *own, *other)
     return (
         new_params.reshape(rows, cols),
         new_error.reshape(1, 1, rows, cols),
-        new_momentum,
+        new_mom.reshape(16, cols),
     )
 
 

time: 101 us -> 71.6 us (0.71)
  waiting for transfers between devices: 34.6 us -> 12.3 us
  local copies, waits for them, and re-layouts: 16.2 us -> 2.4 us
  Pallas kernels: 21.8 us -> 27.9 us
  starting transfers between devices: 25.7 us -> 26.9 us
    ppermute x16 -> x13, waiting for transfers between devices: 34.6 us -> 4.73 us  [move(): return lax.ppermute(array, AXES, pairs)]
    unnamed x21 -> x6, local copies, waits for them, and re-layouts: 16.2 us -> 1.61 us
    all_to_all x0 -> x1, waiting for transfers between devices: none -> 5.75 us  [over_y(): lax.all_to_all(array, 'island', 0, 0, axis_index_groups=[[0, 2, 4, 6], [1...]
    pallas_call x3 -> x5, Pallas kernels: 18.8 us -> 24.2 us  [the longest x3 15.9 us: error_rows(): pl.pallas_call(functools.partial(error_kernel, top), out_shape=jax.ShapeD...]
    all_to_all x0 -> x1, starting transfers between devices: none -> 3.41 us  [over_y(): lax.all_to_all(array, 'island', 0, 0, axis_index_groups=[[0, 2, 4, 6], [1...]
    ppermute x16 -> x13, starting transfers between devices: 17.1 us -> 14.9 us  [move(): return lax.ppermute(array, AXES, pairs)]
    all_to_all x1, waiting for transfers between devices: 0.01 us -> 1.81 us  [per_device(): recv = lax.all_to_all(pay, AXES, 0, 0, tiled=True)]
  transfers between devices with their start and end apart: 17 -> 15, of which waited for: 7 -> 8; matrix products, arithmetic and copies ran while one was open for 0% -> 1% of each run, Pallas kernels for 9% -> 22%
where the time goes in v2:
time: 71.6 us; the launch traced here: 71.1 us
  Pallas kernels  27.9 us (39%)
  starting transfers between devices  26.9 us (38%)
  waiting for transfers between devices  12.3 us (17%)
  local copies, waits for them, and re-layouts  2.4 us (3%)
  between operations  1.54 us (2%)
    pallas_call x3, Pallas kernels, error_rows(): pl.pallas_call(functools.partial(error_kernel, top), out_shape=jax.ShapeD...  15.9 us
    ppermute x13, starting transfers between devices, move(): return lax.ppermute(array, AXES, pairs)  14.9 us
    all_to_all x1, starting transfers between devices, per_device(): recv = lax.all_to_all(pay, AXES, 0, 0, tiled=True)  8.6 us
    all_to_all x1, waiting for transfers between devices, over_y(): lax.all_to_all(array, 'island', 0, 0, axis_index_groups=[[0, 2, 4, 6], [1...  5.75 us
    pallas_call x1, Pallas kernels, per_device(): pl.pallas_call(spread_kernel, out_shape=sds((4, BLOCK, cols), F32), in_sp...  5.32 us
    ppermute x13, waiting for transfers between devices, move(): return lax.ppermute(array, AXES, pairs)  4.73 us
    pallas_call x1, Pallas kernels, per_device(): pl.pallas_call(pack_kernel, out_shape=(sds((DEVICES, 64 + EXTRA, BLOCK),...  3.68 us
    all_to_all x1, starting transfers between devices, over_y(): lax.all_to_all(array, 'island', 0, 0, axis_index_groups=[[0, 2, 4, 6], [1...  3.41 us
  transfers between devices with their start and end apart: 15, of which 8 were waited for; matrix products, arithmetic and copies ran while one was open for 1% of the time, Pallas kernels for 22%

profile of v2, /device:TPU:1, one launch (start us, length us, event | category | flops | bytes accessed | tf_op | source)
XLA Modules:
  0.0 71.1 jit_solution(6086201247882338887)
XLA Ops:
  1.3 0.1 pad_add_fusion.pos
  1.4 0.9 %copy-done = f32[16,4096]{1,0:T(8,128)S(1)} copy-done((f32[16,4096]{1,0:T(8,128)S(1)}, f32[16,4096]{1,0:T(8,128)}, u32[]{:S(2)}) %copy-start) | copy-done | bytes 262168
  2.3 0.7 copy-done.1
  3.0 3.7 %pack.1 = (bf16[32,80,128]{2,1,0:T(8,128)(2,1)}, f32[4,4096]{1,0:T(4,128)S(1)}, f32[4,4096]{1,0:T(4,128)S(1)}, f32[4,4096]{1,0:T(4,128)S(1)}, f32[4,4096]{1,0:T(4,128)S(1)}) custom-call(s32[16]{0:T(128)S(1)} %bitcast.13, s32[1]{0:T(128)} %bitcast.9.count, s32[3]{0:T(128)S(1)} %pad_add_fusion.pos, f32[512,4096]{1,0:T(8,128)} %g.9, ...), custom_call_target="tpu_custom_call" | custom-call | flops 2097152 | bytes 4194304 | tf_op jit(solution)/shard_map/pack/pallas_call | solution.py:274
  6.7 8.6 %all-to-all-start = ((bf16[32,80,128]{2,1,0:T(8,128)(2,1)}), bf16[32,80,128]{2,1,0:T(8,128)(2,1)S(1)}, u32[]{:S(2)}, u32[]{:S(2)}) async-start(bf16[32,80,128]{2,1,0:T(8,128)(2,1)} %get-tuple-element.26), calls=%async_computation | async-start | bytes 1310720 | tf_op jit(solution)/shard_map/all_to_all | solution.py:291
  15.3 1.5 %collective-permute-start = (f32[4,4096]{1,0:T(4,128)S(1)}, f32[4,4096]{1,0:T(4,128)S(1)}, u32[]{:S(2)}, u32[]{:S(2)}) collective-permute-start(f32[4,4096]{1,0:T(4,128)S(1)} %get-tuple-element.30), channel_id=1, source_target_pairs={{0,8},{1,9},{2,10},{3,11},{4,12},{5,13},{6,14},{7,15},{8,16},{9,17... | collective-permute-start | bytes 196616 | tf_op jit(solution)/shard_map/ppermute | solution.py:32
  16.7 2.4 %collective-permute-start.1 = (f32[4,4096]{1,0:T(4,128)S(1)}, f32[4,4096]{1,0:T(4,128)S(1)}, u32[]{:S(2)}, u32[]{:S(2)}) collective-permute-start(f32[4,4096]{1,0:T(4,128)S(1)} %get-tuple-element.31), channel_id=1, source_target_pairs={{0,16},{1,17},{2,18},{3,19},{4,20},{5,21},{6,22},{7,23},{8,24},{9,... | collective-permute-start | bytes 196616 | tf_op jit(solution)/shard_map/ppermute | solution.py:32
  19.2 1.1 %collective-permute-start.2 = (f32[4,4096]{1,0:T(4,128)S(1)}, f32[4,4096]{1,0:T(4,128)S(1)}, u32[]{:S(2)}, u32[]{:S(2)}) collective-permute-start(f32[4,4096]{1,0:T(4,128)S(1)} %get-tuple-element.32), channel_id=1, source_target_pairs={{0,24},{1,25},{2,26},{3,27},{4,28},{5,29},{6,30},{7,31},{8,0},{9,1... | collective-permute-start | bytes 196616 | tf_op jit(solution)/shard_map/ppermute | solution.py:32
  20.3 5.7 %error0.1.refs_0_ = f32[512,4096]{1,0:T(8,128)} custom-call(s32[16]{0:T(128)S(1)} %bitcast.14, s32[1]{0:T(128)} %bitcast.10.count, f32[512,4096]{1,0:T(8,128)} %g.9, bf16[512,4096]{1,0:T(8,128)(2,1)} %bitcast.23, f32[512,4096]{1,0:T(8,128)} %bitcast.18), custom_call_target="tpu_custom_call" | custom-call | flops 12582912 | bytes 11010048 | tf_op jit(solution)/shard_map/error0/pallas_call | solution.py:236
  26.0 1.8 %all-to-all-done.recv = bf16[32,80,128]{2,1,0:T(8,128)(2,1)S(1)} async-done(((bf16[32,80,128]{2,1,0:T(8,128)(2,1)}), bf16[32,80,128]{2,1,0:T(8,128)(2,1)S(1)}, u32[]{:S(2)}, u32[]{:S(2)}) %all-to-all-start) | async-done | bytes 655392 | tf_op jit(solution)/shard_map/all_to_all | solution.py:291
  27.8 0.0 collective-permute-done.m1
  27.8 1.1 %collective-permute-done.1.m2 = f32[4,4096]{1,0:T(4,128)S(1)} collective-permute-done((f32[4,4096]{1,0:T(4,128)S(1)}, f32[4,4096]{1,0:T(4,128)S(1)}, u32[]{:S(2)}, u32[]{:S(2)}) %collective-permute-start.1) | collective-permute-done | bytes 65568 | tf_op jit(solution)/shard_map/ppermute | solution.py:32
  28.9 3.0 %share.1 = (bf16[16,4096]{1,0:T(8,128)(2,1)S(1)}, f32[4,4,4096]{2,1,0:T(4,128)}) custom-call(s32[3]{0:T(128)S(1)} %pad_add_fusion.pos, bf16[32,80,128]{2,1,0:T(8,128)(2,1)S(1)} %all-to-all-done.recv, f32[512,4096]{1,0:T(8,128)} %g.9, f32[4,4096]{1,0:T(4,128)S(1)} %get-tuple-element.29.m0, f32[4,4096]{1,0:T(4,128)S(1)} %collective-permute-done.m1, ...), custom_call_target="tpu_custom_call" | custom-call | flops 268435456 | bytes 4194304 | tf_op jit(solution)/shard_map/share/pallas_call | solution.py:299
  31.9 1.3 %collective-permute-start.5 = (bf16[16,4096]{1,0:T(8,128)(2,1)S(1)}, bf16[16,4096]{1,0:T(8,128)(2,1)S(1)}, u32[]{:S(2)}, u32[]{:S(2)}) collective-permute-start(bf16[16,4096]{1,0:T(8,128)(2,1)S(1)} %get-tuple-element.34), channel_id=1, source_target_pairs={{0,3},{1,0},{2,1},{3,2},{4,28},{5,29},{6,30},{7,31},{8,11},{9,8},{... | collective-permute-start | bytes 393224 | tf_op jit(solution)/shard_map/ppermute | solution.py:32
  33.2 0.5 collective-permute-start.4
  33.8 0.1 collective-permute-start.3
  33.9 4.5 %error192.1.refs_0_ = f32[512,4096]{1,0:T(8,128)} custom-call(s32[16]{0:T(128)S(1)} %bitcast.15, s32[1]{0:T(128)} %bitcast.11.count, f32[512,4096]{1,0:T(8,128)} %g.9, bf16[512,4096]{1,0:T(8,128)(2,1)} %bitcast.24, f32[512,4096]{1,0:T(8,128)} %bitcast.19, f32[512,4096]{1,0:T(8,128)} %error0.1.refs_0_), custom_call_target="tpu_custom_call", output_to_operand_aliasing={{}: (5, {})} | custom-call | flops 8388608 | bytes 7340032 | tf_op jit(solution)/shard_map/error192/pallas_call | solution.py:236
  38.5 0.2 collective-permute-done.4
  38.7 1.6 %collective-permute-done.3 = bf16[16,4096]{1,0:T(8,128)(2,1)S(1)} collective-permute-done((bf16[16,4096]{1,0:T(8,128)(2,1)S(1)}, bf16[16,4096]{1,0:T(8,128)(2,1)S(1)}, u32[]{:S(2)}, u32[]{:S(2)}) %collective-permute-start.3) | collective-permute-done | bytes 131104 | tf_op jit(solution)/shard_map/ppermute | solution.py:32
  40.3 3.2 %collective-permute-start.7 = (bf16[64,4096]{1,0:T(8,128)(2,1)S(1)}, bf16[64,4096]{1,0:T(8,128)(2,1)S(1)}, u32[]{:S(2)}, u32[]{:S(2)}) collective-permute-start(bf16[64,4096]{1,0:T(8,128)(2,1)S(1)} %pad_maximum_fusion.refs_0_), channel_id=1, source_target_pairs={{0,4},{1,5},{2,6},{3,7},{4,0},{5,1},{6,2},{7,3},{8,12},{9,13},{10,... | collective-permute-start | bytes 1572872 | tf_op jit(solution)/shard_map/ppermute | solution.py:32
  43.5 2.7 %collective-permute-start.9 = (bf16[64,4096]{1,0:T(8,128)(2,1)S(1)}, bf16[64,4096]{1,0:T(8,128)(2,1)S(1)}, u32[]{:S(2)}, u32[]{:S(2)}) collective-permute-start(bf16[64,4096]{1,0:T(8,128)(2,1)S(1)} %pad_maximum_fusion.refs_0_), channel_id=1, source_target_pairs={{0,24},{1,25},{2,26},{3,27},{4,7},{5,4},{6,5},{7,6},{8,0},{9,1},{1... | collective-permute-start | bytes 1572872 | tf_op jit(solution)/shard_map/ppermute | solution.py:32
  46.2 3.4 %all-to-all-start.1 = ((f32[4,4,4096]{2,1,0:T(4,128)}), f32[4,4,4096]{2,1,0:T(4,128)S(1)}, u32[]{:S(2)}, u32[]{:S(2)}) async-start(f32[4,4,4096]{2,1,0:T(4,128)} %get-tuple-element.42), calls=%async_computation.1 | async-start | bytes 524288 | tf_op jit(solution)/shard_map/all_to_all | solution.py:257
  49.6 5.7 %error320.1 = f32[512,4096]{1,0:T(8,128)} custom-call(s32[16]{0:T(128)S(1)} %bitcast.16, s32[1]{0:T(128)} %bitcast.12.count, f32[512,4096]{1,0:T(8,128)} %g.9, bf16[512,4096]{1,0:T(8,128)(2,1)} %bitcast.25, f32[512,4096]{1,0:T(8,128)} %bitcast.20, f32[512,4096]{1,0:T(8,128)} %error192.1.refs_0_), custom_call_target="tpu_custom_call", output_to_operand_aliasing={{}: (5, {})} | custom-call | flops 12582912 | bytes 11010048 | tf_op jit(solution)/shard_map/error320/pallas_call | solution.py:236
  55.3 5.8 %all-to-all-done.1 = f32[4,4,4096]{2,1,0:T(4,128)S(1)} async-done(((f32[4,4,4096]{2,1,0:T(4,128)}), f32[4,4,4096]{2,1,0:T(4,128)S(1)}, u32[]{:S(2)}, u32[]{:S(2)}) %all-to-all-start.1) | async-done | bytes 262176 | tf_op jit(solution)/shard_map/all_to_all | solution.py:257
  61.1 1.4 %collective-permute-start.12 = (bf16[64,4096]{1,0:T(8,128)(2,1)S(1)}, bf16[64,4096]{1,0:T(8,128)(2,1)S(1)}, u32[]{:S(2)}, u32[]{:S(2)}) collective-permute-start(bf16[64,4096]{1,0:T(8,128)(2,1)S(1)} %collective-permute-done.9.refs_3_), channel_id=1, source_target_pairs={{0,4},{1,5},{2,6},{3,7},{4,0},{5,1},{6,2},{7,3},{8,12},{9,13},{10,... | collective-permute-start | bytes 1572872 | tf_op jit(solution)/shard_map/ppermute | solution.py:32
  62.5 0.1 collective-permute-start.11
  62.6 0.4 collective-permute-start.10
  63.0 0.8 %reshape.33 = f32[16,4096]{1,0:T(8,128)} reshape(f32[4,4,4096]{2,1,0:T(4,128)S(1)} %all-to-all-done.1) | data formatting | bytes 524288 | tf_op jit(solution)/shard_map/reshape | solution.py:340
  63.8 0.2 collective-permute-done.12.refs_7_
  64.0 0.9 %collective-permute-done.11.refs_6_ = bf16[64,4096]{1,0:T(8,128)(2,1)} collective-permute-done((bf16[64,4096]{1,0:T(8,128)(2,1)S(1)}, bf16[64,4096]{1,0:T(8,128)(2,1)}, u32[]{:S(2)}, u32[]{:S(2)}) %collective-permute-start.11) | collective-permute-done | bytes 524320 | tf_op jit(solution)/shard_map/ppermute | solution.py:32
  64.9 0.7 %collective-permute-done.10.refs_5_ = bf16[64,4096]{1,0:T(8,128)(2,1)} collective-permute-done((bf16[64,4096]{1,0:T(8,128)(2,1)S(1)}, bf16[64,4096]{1,0:T(8,128)(2,1)}, u32[]{:S(2)}, u32[]{:S(2)}) %collective-permute-start.10) | collective-permute-done | bytes 524320 | tf_op jit(solution)/shard_map/ppermute | solution.py:32
  65.7 5.3 %spread.1 = f32[4,128,4096]{2,1,0:T(8,128)} custom-call(s32[3]{0:T(128)S(1)} %pad_add_fusion.pos, bf16[64,4096]{1,0:T(8,128)(2,1)S(1)} %pad_maximum_fusion.refs_0_, bf16[64,4096]{1,0:T(8,128)(2,1)S(1)} %collective-permute-done.6.refs_1_, bf16[64,4096]{1,0:T(8,128)(2,1)S(1)} %collective-permute-done.8.refs_2_, ...), custom_call_target="tpu_custom_call" | custom-call | flops 16777216 | bytes 12582912 | tf_op jit(solution)/shard_map/spread/pallas_call | solution.py:327
  (13 shorter events, 0.1 us)
Async XLA Ops:
  1.4 1.0 %copy-start = (f32[16,4096]{1,0:T(8,128)S(1)}, f32[16,4096]{1,0:T(8,128)}, u32[]{:S(2)}) copy-start(f32[16,4096]{1,0:T(8,128)} %mom.1) | copy-start | bytes 786436
  2.3 0.7 copy-start.1
  3.0 17.3 %copy-start.2 = (s32[1,1,1,16]{3,2,1,0:T(1,128)S(1)}, s32[1,1,1,16]{3,2,1,0:T(1,128)}, u32[]{:S(2)}) copy-start(s32[1,1,1,16]{3,2,1,0:T(1,128)} %param.10) | copy-start | bytes 196
  6.7 21.1 %all-to-all-start = ((bf16[32,80,128]{2,1,0:T(8,128)(2,1)}), bf16[32,80,128]{2,1,0:T(8,128)(2,1)S(1)}, u32[]{:S(2)}, u32[]{:S(2)}) async-start(bf16[32,80,128]{2,1,0:T(8,128)(2,1)} %get-tuple-element.26), calls=%async_computation | async-start | bytes 1310720 | tf_op jit(solution)/shard_map/all_to_all | solution.py:291
  15.3 12.5 %collective-permute-start = (f32[4,4096]{1,0:T(4,128)S(1)}, f32[4,4096]{1,0:T(4,128)S(1)}, u32[]{:S(2)}, u32[]{:S(2)}) collective-permute-start(f32[4,4096]{1,0:T(4,128)S(1)} %get-tuple-element.30), channel_id=1, source_target_pairs={{0,8},{1,9},{2,10},{3,11},{4,12},{5,13},{6,14},{7,15},{8,16},{9,17... | collective-permute-start | bytes 196616 | tf_op jit(solution)/shard_map/ppermute | solution.py:32
  16.7 12.1 %collective-permute-start.1 = (f32[4,4096]{1,0:T(4,128)S(1)}, f32[4,4096]{1,0:T(4,128)S(1)}, u32[]{:S(2)}, u32[]{:S(2)}) collective-permute-start(f32[4,4096]{1,0:T(4,128)S(1)} %get-tuple-element.31), channel_id=1, source_target_pairs={{0,16},{1,17},{2,18},{3,19},{4,20},{5,21},{6,22},{7,23},{8,24},{9,... | collective-permute-start | bytes 196616 | tf_op jit(solution)/shard_map/ppermute | solution.py:32
  19.2 9.7 %collective-permute-start.2 = (f32[4,4096]{1,0:T(4,128)S(1)}, f32[4,4096]{1,0:T(4,128)S(1)}, u32[]{:S(2)}, u32[]{:S(2)}) collective-permute-start(f32[4,4096]{1,0:T(4,128)S(1)} %get-tuple-element.32), channel_id=1, source_target_pairs={{0,24},{1,25},{2,26},{3,27},{4,28},{5,29},{6,30},{7,31},{8,0},{9,1... | collective-permute-start | bytes 196616 | tf_op jit(solution)/shard_map/ppermute | solution.py:32
  31.9 6.5 %collective-permute-start.5 = (bf16[16,4096]{1,0:T(8,128)(2,1)S(1)}, bf16[16,4096]{1,0:T(8,128)(2,1)S(1)}, u32[]{:S(2)}, u32[]{:S(2)}) collective-permute-start(bf16[16,4096]{1,0:T(8,128)(2,1)S(1)} %get-tuple-element.34), channel_id=1, source_target_pairs={{0,3},{1,0},{2,1},{3,2},{4,28},{5,29},{6,30},{7,31},{8,11},{9,8},{... | collective-permute-start | bytes 393224 | tf_op jit(solution)/shard_map/ppermute | solution.py:32
  33.2 5.4 %collective-permute-start.4 = (bf16[16,4096]{1,0:T(8,128)(2,1)S(1)}, bf16[16,4096]{1,0:T(8,128)(2,1)S(1)}, u32[]{:S(2)}, u32[]{:S(2)}) collective-permute-start(bf16[16,4096]{1,0:T(8,128)(2,1)S(1)} %get-tuple-element.34), channel_id=1, source_target_pairs={{0,2},{1,3},{2,0},{3,1},{4,20},{5,21},{6,22},{7,23},{8,10},{9,11},... | collective-permute-start | bytes 393224 | tf_op jit(solution)/shard_map/ppermute | solution.py:32
  33.8 6.5 %collective-permute-start.3 = (bf16[16,4096]{1,0:T(8,128)(2,1)S(1)}, bf16[16,4096]{1,0:T(8,128)(2,1)S(1)}, u32[]{:S(2)}, u32[]{:S(2)}) collective-permute-start(bf16[16,4096]{1,0:T(8,128)(2,1)S(1)} %get-tuple-element.34), channel_id=1, source_target_pairs={{0,1},{1,2},{2,3},{3,0},{4,12},{5,13},{6,14},{7,15},{8,9},{9,10},{... | collective-permute-start | bytes 393224 | tf_op jit(solution)/shard_map/ppermute | solution.py:32
  40.3 20.8 %collective-permute-start.7 = (bf16[64,4096]{1,0:T(8,128)(2,1)S(1)}, bf16[64,4096]{1,0:T(8,128)(2,1)S(1)}, u32[]{:S(2)}, u32[]{:S(2)}) collective-permute-start(bf16[64,4096]{1,0:T(8,128)(2,1)S(1)} %pad_maximum_fusion.refs_0_), channel_id=1, source_target_pairs={{0,4},{1,5},{2,6},{3,7},{4,0},{5,1},{6,2},{7,3},{8,12},{9,13},{10,... | collective-permute-start | bytes 1572872 | tf_op jit(solution)/shard_map/ppermute | solution.py:32
  43.5 17.5 %collective-permute-start.6 = (bf16[64,4096]{1,0:T(8,128)(2,1)S(1)}, bf16[64,4096]{1,0:T(8,128)(2,1)S(1)}, u32[]{:S(2)}, u32[]{:S(2)}) collective-permute-start(bf16[64,4096]{1,0:T(8,128)(2,1)S(1)} %pad_maximum_fusion.refs_0_), channel_id=1, source_target_pairs={{0,8},{1,9},{2,10},{3,11},{4,5},{5,6},{6,7},{7,4},{8,16},{9,17},{1... | collective-permute-start | bytes 1572872 | tf_op jit(solution)/shard_map/ppermute | solution.py:32
  43.5 17.5 %collective-permute-start.9 = (bf16[64,4096]{1,0:T(8,128)(2,1)S(1)}, bf16[64,4096]{1,0:T(8,128)(2,1)S(1)}, u32[]{:S(2)}, u32[]{:S(2)}) collective-permute-start(bf16[64,4096]{1,0:T(8,128)(2,1)S(1)} %pad_maximum_fusion.refs_0_), channel_id=1, source_target_pairs={{0,24},{1,25},{2,26},{3,27},{4,7},{5,4},{6,5},{7,6},{8,0},{9,1},{1... | collective-permute-start | bytes 1572872 | tf_op jit(solution)/shard_map/ppermute | solution.py:32
  46.2 16.3 %collective-permute-start.8 = (bf16[64,4096]{1,0:T(8,128)(2,1)S(1)}, bf16[64,4096]{1,0:T(8,128)(2,1)S(1)}, u32[]{:S(2)}, u32[]{:S(2)}) collective-permute-start(bf16[64,4096]{1,0:T(8,128)(2,1)S(1)} %pad_maximum_fusion.refs_0_), channel_id=1, source_target_pairs={{0,16},{1,17},{2,18},{3,19},{4,6},{5,7},{6,4},{7,5},{8,24},{9,25},... | collective-permute-start | bytes 1572872 | tf_op jit(solution)/shard_map/ppermute | solution.py:32
  46.2 14.9 %all-to-all-start.1 = ((f32[4,4,4096]{2,1,0:T(4,128)}), f32[4,4,4096]{2,1,0:T(4,128)S(1)}, u32[]{:S(2)}, u32[]{:S(2)}) async-start(f32[4,4,4096]{2,1,0:T(4,128)} %get-tuple-element.42), calls=%async_computation.1 | async-start | bytes 524288 | tf_op jit(solution)/shard_map/all_to_all | solution.py:257
  61.1 3.0 %collective-permute-start.12 = (bf16[64,4096]{1,0:T(8,128)(2,1)S(1)}, bf16[64,4096]{1,0:T(8,128)(2,1)S(1)}, u32[]{:S(2)}, u32[]{:S(2)}) collective-permute-start(bf16[64,4096]{1,0:T(8,128)(2,1)S(1)} %collective-permute-done.9.refs_3_), channel_id=1, source_target_pairs={{0,4},{1,5},{2,6},{3,7},{4,0},{5,1},{6,2},{7,3},{8,12},{9,13},{10,... | collective-permute-start | bytes 1572872 | tf_op jit(solution)/shard_map/ppermute | solution.py:32
  62.5 2.4 %collective-permute-start.11 = (bf16[64,4096]{1,0:T(8,128)(2,1)S(1)}, bf16[64,4096]{1,0:T(8,128)(2,1)}, u32[]{:S(2)}, u32[]{:S(2)}) collective-permute-start(bf16[64,4096]{1,0:T(8,128)(2,1)S(1)} %collective-permute-done.8.refs_2_), channel_id=1, source_target_pairs={{0,4},{1,5},{2,6},{3,7},{4,0},{5,1},{6,2},{7,3},{8,12},{9,13},{10,... | collective-permute-start | bytes 1572872 | tf_op jit(solution)/shard_map/ppermute | solution.py:32
  62.6 3.1 %collective-permute-start.10 = (bf16[64,4096]{1,0:T(8,128)(2,1)S(1)}, bf16[64,4096]{1,0:T(8,128)(2,1)}, u32[]{:S(2)}, u32[]{:S(2)}) collective-permute-start(bf16[64,4096]{1,0:T(8,128)(2,1)S(1)} %collective-permute-done.6.refs_1_), channel_id=1, source_target_pairs={{0,4},{1,5},{2,6},{3,7},{4,0},{5,1},{6,2},{7,3},{8,12},{9,13},{10,... | collective-permute-start | bytes 1572872 | tf_op jit(solution)/shard_map/ppermute | solution.py:32

commit v3 on v2

v3 whole, which is shorter than its diff:
```python
import functools

import jax
import jax.numpy as jnp
from jax import lax
from jax.experimental import pallas as pl
from jax.experimental.pallas import tpu as pltpu
from jax.sharding import PartitionSpec as P

BLOCK = 128
PARTS = 4
DEVICES = 32
EXTRA = 8
AXES = ("island", "region")
SCALE = 2.0**24
MIB = 2**20
F32 = jnp.float32
BF16 = jnp.bfloat16


def place():
    island = lax.axis_index("island")
    return island // 2, island % 2, lax.axis_index("region")


def move(array, step):
    pairs = []
    for p in range(DEVICES):
        y, c, x = p // 8, p // 4 % 2, p % 4
        y, c, x = step(y, c, x)
        pairs.append((p, 8 * (y % 4) + 4 * (c % 2) + x % 4))
    return lax.ppermute(array, AXES, pairs)


def encode(v):
    v = v * SCALE
    s = v * v
    return jnp.where(v < 0, -(s * s), s * s).astype(BF16)


def decode(code):
    w = code.astype(F32)
    v = lax.rsqrt(lax.rsqrt(jnp.abs(w))) * (1.0 / SCALE)
    return jnp.where(w < 0, -v, v)


def pick(index, choices):
    out = choices[-1]
    for i in range(len(choices) - 2, -1, -1):
        out = jnp.where(index == i, choices[i], out)
    return out


def pack_kernel(kept, counts, g, l, e, mom, pay, m0, m1, m2, m3, gb, lb, eb, mb, sems, msem):
    y, _, x = place()
    ids = [kept[0, 0, 0, k] for k in range(gb.shape[0])]
    held = pltpu.make_async_copy(mom, mb, msem)
    held.start()
    slots = gb.shape[0]
    copies = []
    for k in range(slots):
        rows = pl.ds(pl.multiple_of(ids[k] // 32 * BLOCK, BLOCK), BLOCK)
        cols = pl.ds(pl.multiple_of(ids[k] % 32 * BLOCK, BLOCK), BLOCK)
        copies.append([
            pltpu.make_async_copy(src.at[rows, cols], dst.at[k], sems.at[i, k])
            for i, (src, dst) in enumerate(((g, gb), (l, lb), (e, eb)))
        ])
        for copy in copies[-1]:
            copy.start()
    lane = lax.broadcasted_iota(jnp.int32, (EXTRA, BLOCK), 1)
    vec = jnp.zeros((EXTRA, BLOCK), F32)
    for k in range(slots):
        vec = jnp.where(lane % 64 // 4 == k, ids[k].astype(F32), vec)
    vec = jnp.where(lane // 64 == x % 2, vec, 0.0).astype(BF16)
    for p in range(DEVICES):
        pay[p, 64 : 64 + EXTRA, :] = vec
    for group in range(slots // 4):
        for k in range(4 * group, 4 * group + 4):
            for copy in copies[k]:
                copy.wait()
        for r in range(8):
            rows = slice(16 * r, 16 * r + 16)
            tiles = []
            for k in range(4 * group, 4 * group + 4):
                acc = 0.95 * eb[k, rows, :] + (gb[k, rows, :] - lb[k, rows, :].astype(F32))
                tiles.append(jnp.where(k < counts[0, 0, 0], acc, 0.0))
            for q in range(4):
                tile = jnp.concatenate([t[4 * q : 4 * q + 4] for t in tiles], axis=0)
                pay[8 * q + r, 16 * group : 16 * group + 16, :] = tile.astype(BF16)
    held.wait()
    for d, out in enumerate((m0, m1, m2, m3)):
        out[...] = pick((y + d) % 4, [mb[4 * q : 4 * q + 4, :] for q in range(4)])


def tiles_of(flat, tall):
    out = []
    if flat is not None:
        cols = flat.shape[1] * 4 // 5
        for t in range(0, cols // 4, BLOCK):
            out.append((None, slice(cols + t, cols + t + BLOCK), [i * cols // 4 + t for i in range(4)]))
    if tall is not None:
        wide = tall.shape[1]
        for k in range(4):
            for t in range(0, wide, BLOCK):
                out.append((slice(16 * k, 16 * k + 16), slice(t, t + BLOCK), [(4 * k + i) * wide + t for i in range(4)]))
    return out


def share_kernel(recv, base, m0, m1, m2, m3, c1, c2, c3, t1, t2, t3, n0, mb, nb):
    y, _, _ = place()
    for d, m in enumerate((m0, m1, m2, m3)):
        mb[d] = m[...]
    row = lax.broadcasted_iota(jnp.int32, (512, BLOCK), 0)
    lane = lax.broadcasted_iota(jnp.int32, (512, BLOCK), 1)
    want = (row // 4 % 4 * 32 + row // 16) * 4 + row % 4
    want = (want - lane % 4).astype(F32)
    total = jnp.zeros((512, BLOCK), F32)
    for i in range(0, DEVICES, 4):
        halves = []
        for h in (i, i + 2):
            pair = recv[h, 64 : 64 + EXTRA, :].astype(F32) + recv[h + 1, 64 : 64 + EXTRA, :].astype(F32)
            halves.append((want == 4.0 * pair[0:1, :]).astype(F32).astype(BF16))
        table = jnp.concatenate(halves, axis=1)
        values = jnp.concatenate([recv[i + s, 0:64, :] for s in range(4)], axis=0)
        total = total + jnp.dot(table, values, preferred_element_type=F32)
    for b in range(32):
        cols = slice(BLOCK * b, BLOCK * b + BLOCK)
        average = total[16 * b : 16 * b + 16, :] * (1.0 / DEVICES)
        mom = jnp.concatenate([mb[(y - q) % 4, :, cols] for q in range(4)], axis=0)
        new_mom = 0.9 * mom + average
        code = encode(base[:, cols] - 0.7 * (average + 0.9 * new_mom))
        for out in (c1, c2, c3):
            out[:, cols] = code
        for q in range(4):
            nb[q, :, cols] = new_mom[4 * q : 4 * q + 4, :]
    n0[...] = nb[y]
    for d, (flat, tall) in enumerate(((c1, t1), (c2, t2), (c3, t3)), 1):
        for rows, cols, places in tiles_of(flat, tall):
            tile = encode(jnp.concatenate([nb[(y + d) % 4, :, p : p + BLOCK] for p in places], axis=0))
            (flat if rows is None else tall)[slice(None) if rows is None else rows, cols] = tile


def group_kernel(c1, r1, r2, r3, t1, t2, t3, g1, g2, g3):
    width = g1.shape[1] - t1.shape[1]
    for n, code in enumerate((c1, r1, r2, r3)):
        part = code[:, :width]
        for out in (g1, g2, g3):
            out[16 * n : 16 * n + 16, :width] = part
    for out, tail in ((g1, t1), (g2, t2), (g3, t3)):
        out[:, width:] = tail[...]


def error_kernel(top, kept, counts, g, l, e, *refs):
    gb, lb, eb, mask, sems, done, rb, rsems = refs[-8:]
    out, base = refs[:2] if top == 0 else (refs[1], None)
    chunks, high, _ = gb.shape
    copies = []
    for i in range(chunks):
        rows = pl.ds(top + i * high, high)
        copies.append([
            pltpu.make_async_copy(src.at[rows, :], dst.at[i], sems.at[n, i])
            for n, (src, dst) in enumerate(((g, gb), (l, lb), (e, eb)))
        ])
        for copy in copies[-1]:
            copy.start()
    if base is not None:
        y, c, x = place()
        reads = []
        for q in range(4):
            rows = pl.ds(pl.multiple_of(q * BLOCK + 16 * (4 * c + x), 16), 16)
            reads.append(pltpu.make_async_copy(g.at[rows, :], rb.at[q], rsems.at[q]))
            reads[-1].start()
    for n in range(mask.shape[0]):
        mask[n] = jnp.int32(0)
    for k in range(kept.shape[-1]):

        @pl.when(k < counts[0, 0, 0])
        def _():
            mask[kept[0, 0, 0, k]] = jnp.int32(1)

    back = []
    for i in range(chunks):
        for copy in copies[i]:
            copy.wait()
        first = (top + i * high) // BLOCK * 32

        def body(b, _):
            cols = pl.ds(pl.multiple_of(b * BLOCK, BLOCK), BLOCK)
            acc = 0.95 * eb[i, :, cols] + (gb[i, :, cols] - lb[i, :, cols].astype(F32))
            kept = mask[first + b] > 0
            eb[i, :, cols] = acc - jnp.where(kept, acc.astype(BF16).astype(F32), 0.0)
            return 0

        lax.fori_loop(0, 32, body, 0, unroll=4)
        back.append(pltpu.make_async_copy(eb.at[i], out.at[pl.ds(top + i * high, high), :], done.at[i]))
        back[-1].start()
    if base is not None:
        for q in range(4):
            reads[q].wait()
            base[4 * q : 4 * q + 4, :] = pick(y, [rb[q, 4 * n : 4 * n + 4, :] for n in range(4)])
    for copy in back:
        copy.wait()


def spread_kernel(early, *refs):
    own, other = refs[:3], refs[3:6]
    wide, half, sems = refs[-3:]
    out = refs[6] if early else refs[11]
    y, c, x = place()
    steps = (0, 1, 3) if early else (1, 2, 3)
    width = BLOCK

    def unit(stage, sem, first, parts_of):
        def body(i, _):
            cols = pl.ds(pl.multiple_of(i * width, width), width)
            parts = [decode(part) for part in parts_of(cols)]
            for q in range(4):
                stage[q, :, cols] = jnp.concatenate([p[4 * q : 4 * q + 4, :] for p in parts], axis=0)
            return 0

        lax.fori_loop(0, stage.shape[2] // width, body, 0, unroll=16)
        rows = pl.ds(pl.multiple_of(first, 8), stage.shape[1])
        pltpu.make_async_copy(stage, out.at[:, rows, :], sem).start()

    def shard(ref, index, cols):
        return ref[pl.ds(pl.multiple_of(index * 16, 16), 16), cols]

    for core in range(2):
        groups = dict(zip(steps, own if core == 1 else other))
        groups0 = dict(zip(steps, own if core == 0 else other))

        @pl.when(c == core)
        def _():
            for n, d in enumerate((0, 1, 3) if early else (2,)):
                first = 16 * (4 + (x - d) % 4)
                unit(wide.at[n], sems.at[n], first, lambda cols: [shard(groups[d], (y - q) % 4, cols) for q in range(4)])

        for row in range(4):
            part = row // 2 if early else 1 - row // 2
            pair = (2 * part, 2 * part + 1)

            @pl.when((c == core) & (y == row))
            def _():
                def each(d, _):
                    first = 16 * ((x - d) % 4) + 8 * part
                    unit(half.at[d], sems.at[3 + d], first, lambda cols: [shard(groups0[(row - q) % 4], d, cols) for q in pair])
                    return 0

                lax.fori_loop(0, 4, each, 0)

    if not early:
        flats, n0, new_mom, nb = refs[7:10], refs[10], refs[12], refs[13]
        nb[y] = n0[...]
        full = nb.shape[2]

        def place_piece(d, ref, first, flat, tall):
            for rows, cols, places in tiles_of(flat, tall):
                cols = slice(cols.start + first, cols.stop + first)
                tile = decode(ref[slice(None) if rows is None else rows, cols])
                for n, p in enumerate(places):
                    nb[(y - d) % 4, :, p : p + BLOCK] = tile[4 * n : 4 * n + 4, :]

        @pl.when(c == 1)
        def _():
            for d, flat in enumerate(flats, 1):
                place_piece(d, flat, 0, flat, None)

        @pl.when(c == 0)
        def _():
            for d, group in enumerate(own, 1):
                place_piece(d, group, full, None, jax.ShapeDtypeStruct((64, full // 16), BF16))

        for q in range(4):
            new_mom[4 * q : 4 * q + 4, :] = nb[q]
    for n in range(wide.shape[0]):
        pltpu.make_async_copy(wide.at[n], out.at[:, pl.ds(0, 16), :], sems.at[n]).wait()
    for d in range(4):
        pltpu.make_async_copy(half.at[d], out.at[:, pl.ds(0, 8), :], sems.at[3 + d]).wait()


def smem():
    return pl.BlockSpec(memory_space=pltpu.SMEM)


def vmem():
    return pl.BlockSpec(memory_space=pltpu.VMEM)


def hbm():
    return pl.BlockSpec(memory_space=pl.ANY)


def params(mib):
    return pltpu.CompilerParams(vmem_limit_bytes=mib * MIB)


def in_hbm(array):
    return pltpu.with_memory_space_constraint(array, pltpu.HBM)


def error_rows(top, count_rows, high, kept, counts, g, l, e, before):
    rows, cols = g.shape
    chunks = count_rows // high
    given = [] if before is None else [before]
    return pl.pallas_call(
        functools.partial(error_kernel, top),
        out_shape=[jax.ShapeDtypeStruct((rows, cols), F32)] + [jax.ShapeDtypeStruct((16, cols), F32)] * (1 - len(given)),
        in_specs=[smem(), smem()] + [hbm()] * (3 + len(given)),
        out_specs=[hbm()] + [vmem()] * (1 - len(given)),
        input_output_aliases={5: 0} if given else {},
        scratch_shapes=[
            pltpu.VMEM((chunks, high, cols), F32),
            pltpu.VMEM((chunks, high, cols), BF16),
            pltpu.VMEM((chunks, high, cols), F32),
            pltpu.SMEM((rows // BLOCK * (cols // BLOCK),), jnp.int32),
            pltpu.SemaphoreType.DMA((3, chunks)),
            pltpu.SemaphoreType.DMA((chunks,)),
            pltpu.VMEM((4, 16, cols), F32),
            pltpu.SemaphoreType.DMA((4,)),
        ],
        compiler_params=params(4 + 10 * count_rows * cols // MIB),
        cost_estimate=pl.CostEstimate(flops=16 * count_rows * cols, bytes_accessed=14 * count_rows * cols, transcendentals=0),
        name=f"error{top}",
    )(kept, counts, in_hbm(g), in_hbm(l), in_hbm(e), *given)


def spread(early, own, other, cols, rest=()):
    sds = jax.ShapeDtypeStruct
    late = not early
    return pl.pallas_call(
        functools.partial(spread_kernel, early),
        out_shape=[sds((4, BLOCK, cols), F32)] + [sds((16, cols), F32)] * late,
        in_specs=[vmem()] * 6 + [hbm()] * late + [vmem()] * (len(rest) - late),
        out_specs=[hbm()] + [vmem()] * late,
        input_output_aliases={6: 0} if late else {},
        scratch_shapes=[pltpu.VMEM((4, 4, cols), F32)] * late
        + [
            pltpu.VMEM((3 if early else 1, 4, 16, cols), F32),
            pltpu.VMEM((4, 4, 8, cols), F32),
            pltpu.SemaphoreType.DMA((7,)),
        ],
        compiler_params=params(24),
        cost_estimate=pl.CostEstimate(
            flops=16 * MIB, bytes_accessed=(8 if early else 5) * MIB, transcendentals=(2 if early else 1) * MIB
        ),
        name="spread_early" if early else "spread_late",
    )(*own, *other, *rest)


CUTS = (0, 192, 320, 384, 512)
HIGH = 64


def per_device(global_params, local_params, error_buf, momentum, kept, counts):
    rows, cols = global_params.shape
    local, error = local_params.reshape(rows, cols), error_buf.reshape(rows, cols)
    slots = kept.shape[-1]
    sds = jax.ShapeDtypeStruct

    quarter = sds((4, cols), F32)
    pay, m0, m1, m2, m3 = pl.pallas_call(
        pack_kernel,
        out_shape=(pltpu.VMEM((DEVICES, 64 + EXTRA, BLOCK), BF16),) + (quarter,) * 4,
        in_specs=[smem(), smem(), hbm(), hbm(), hbm(), hbm()],
        out_specs=(vmem(),) * 5,
        scratch_shapes=[
            pltpu.VMEM((slots, BLOCK, BLOCK), F32),
            pltpu.VMEM((slots, BLOCK, BLOCK), BF16),
            pltpu.VMEM((slots, BLOCK, BLOCK), F32),
            pltpu.VMEM(momentum.shape, F32),
            pltpu.SemaphoreType.DMA((3, slots)),
            pltpu.SemaphoreType.DMA,
        ],
        compiler_params=params(16),
        cost_estimate=pl.CostEstimate(flops=2 * MIB, bytes_accessed=4 * MIB, transcendentals=0),
        name="pack",
    )(kept, counts, in_hbm(global_params), in_hbm(local), in_hbm(error), in_hbm(momentum))

    m1, m2, m3 = [move(m, lambda y, c, x, d=d: (y + d, c, x)) for d, m in ((1, m1), (2, m2), (3, m3))]
    recv = lax.all_to_all(pay, AXES, 0, 0, tiled=True)
    def part(n, local, before):
        return error_rows(CUTS[n], CUTS[n + 1] - CUTS[n], HIGH, kept, counts, global_params, local, error, before)

    pay, local = lax.optimization_barrier((pay, local))
    new_error, base = part(0, local, None)
    recv, new_error, base = lax.optimization_barrier((recv, new_error, base))

    flat, tall = sds((16, cols + cols // 4), BF16), sds((64, cols // 16), BF16)
    *codes, t1, t2, t3, n0 = pl.pallas_call(
        share_kernel,
        out_shape=(flat,) * 3 + (tall,) * 3 + (quarter,),
        in_specs=[vmem()] * 6,
        out_specs=(vmem(),) * 7,
        scratch_shapes=[pltpu.VMEM((4, 4, cols), F32)] * 2,
        compiler_params=params(16),
        cost_estimate=pl.CostEstimate(flops=256 * MIB, bytes_accessed=4 * MIB, transcendentals=0),
        name="share",
    )(recv, base, m0, m1, m2, m3)

    codes[0], local = lax.optimization_barrier((codes[0], local))
    new_error, = part(1, local, new_error)
    first = [
        move(code, lambda y, c, x, d=d: (y, c, x + d) if c == 0 else (y + d, c, x)) for d, code in enumerate(codes, 1)
    ]
    first, new_error = lax.optimization_barrier((first, new_error))
    g1, g2, g3 = pl.pallas_call(
        group_kernel,
        out_shape=(sds((64, cols + cols // 16), BF16),) * 3,
        in_specs=[vmem()] * 7,
        out_specs=(vmem(),) * 3,
        compiler_params=params(16),
        cost_estimate=pl.CostEstimate(flops=0, bytes_accessed=2 * MIB, transcendentals=0),
        name="group",
    )(codes[0], *first, t1, t2, t3)

    def send(group, d):
        return move(group, lambda y, c, x: (y + d, c, x) if c == 0 else (y, c, x + d))

    def swap(group):
        return move(group, lambda y, c, x: (y, c + 1, x))

    g1, local = lax.optimization_barrier((g1, local))
    own1, own3, other0 = send(g1, 1), send(g3, 3), swap(g1)
    new_error, = part(2, local, new_error)
    g2, local, new_error = lax.optimization_barrier((g2, local, new_error))
    own2 = send(g2, 2)
    new_error, = part(3, local, new_error)
    own1, own3, other0, new_error = lax.optimization_barrier((own1, own3, other0, new_error))
    other1, other3 = swap(own1), swap(own3)
    own2, other1, other3 = lax.optimization_barrier((own2, other1, other3))
    other2 = swap(own2)
    new_params, = spread(True, [g1, own1, own3], [other0, other1, other3], cols)
    new_params, new_mom = spread(
        False, [own1, own2, own3], [other1, other2, other3], cols, [new_params, *first, n0]
    )
    return (
        new_params.reshape(rows, cols),
        new_error.reshape(1, 1, rows, cols),
        new_mom,
    )


def solution(mesh):
    return jax.shard_map(
        per_device,
        mesh=mesh,
        in_specs=(
            P(None, "tensor"),
            P("region", "island", None, "tensor"),
            P("region", "island", None, "tensor"),
            P(("island", "region"), "tensor"),
            P("region", "island", "tensor", None),
            P("region", "island", "tensor"),
        ),
        out_specs=(
            P(None, "tensor"),
            P("region", "island", None, "tensor"),
            P(("island", "region"), "tensor"),
        ),
        check_vma=False,
    )
```

time: 71.6 us -> 65.2 us (0.911)
  waiting for transfers between devices: 12.3 us -> 7.87 us
  Pallas kernels: 27.9 us -> 30 us
  starting transfers between devices: 26.9 us -> 25 us
  local copies, waits for them, and re-layouts: 2.4 us -> 0.65 us
    all_to_all x1 -> x0, waiting for transfers between devices: 5.75 us -> none  [over_y(): lax.all_to_all(array, 'island', 0, 0, axis_index_groups=[[0, 2, 4, 6], [1...]
    all_to_all x1 -> x0, starting transfers between devices: 3.41 us -> none  [over_y(): lax.all_to_all(array, 'island', 0, 0, axis_index_groups=[[0, 2, 4, 6], [1...]
    ppermute x13, waiting for transfers between devices: 4.73 us -> 6.94 us  [move(): return lax.ppermute(array, AXES, pairs)]
    pallas_call x6 -> x9, Pallas kernels: 27.9 us -> 30 us  [the longest x4 18.9 us: error_rows(): pl.pallas_call(functools.partial(error_kernel, top), out_shape=[jax.Shape...]
    ppermute x13, starting transfers between devices: 14.9 us -> 16.4 us  [move(): return lax.ppermute(array, AXES, pairs)]
    unnamed x6 -> x4, local copies, waits for them, and re-layouts: 1.61 us -> 0.65 us
    all_to_all x1, waiting for transfers between devices: 1.81 us -> 0.93 us  [per_device(): recv = lax.all_to_all(pay, AXES, 0, 0, tiled=True)]
    reshape x1 -> x0, local copies, waits for them, and re-layouts: 0.79 us -> none  [per_device(): new_mom.reshape(16, cols)]
  transfers between devices with their start and end apart: 15 -> 14, of which waited for: 8 -> 7; matrix products, arithmetic and copies ran while one was open for 1% -> 0% of each run, Pallas kernels for 22% -> 34%
where the time goes in v3:
time: 65.2 us; the launch traced here: 64.9 us
  Pallas kernels  30 us (46%)
  starting transfers between devices  25 us (38%)
  waiting for transfers between devices  7.87 us (12%)
  between operations  1.4 us (2%)
    pallas_call x4, Pallas kernels, error_rows(): pl.pallas_call(functools.partial(error_kernel, top), out_shape=[jax.Shape...  18.9 us
    ppermute x13, starting transfers between devices, move(): return lax.ppermute(array, AXES, pairs)  16.4 us
    all_to_all x1, starting transfers between devices, per_device(): recv = lax.all_to_all(pay, AXES, 0, 0, tiled=True)  8.6 us
    ppermute x13, waiting for transfers between devices, move(): return lax.ppermute(array, AXES, pairs)  6.94 us
    pallas_call x2, Pallas kernels, spread(): pl.pallas_call(functools.partial(spread_kernel, early), out_shape=[sds((4...  6.32 us
    pallas_call x1, Pallas kernels, per_device(): pl.pallas_call(pack_kernel, out_shape=(pltpu.VMEM((DEVICES, 64 + EXTRA, B...  3.78 us
  transfers between devices with their start and end apart: 14, of which 7 were waited for; matrix products, arithmetic and copies ran while one was open for 0% of the time, Pallas kernels for 34%

profile of v3, /device:TPU:1, one launch (start us, length us, event | category | flops | bytes accessed | tf_op | source)
XLA Modules:
  0.0 64.9 jit_solution(4011632562181230406)
XLA Ops:
  1.3 0.6 copy-done
  1.9 3.8 %pack.1 = (bf16[32,72,128]{2,1,0:T(8,128)(2,1)}, f32[4,4096]{1,0:T(4,128)S(1)}, f32[4,4096]{1,0:T(4,128)S(1)}, f32[4,4096]{1,0:T(4,128)S(1)}, f32[4,4096]{1,0:T(4,128)S(1)}) custom-call(s32[1,1,1,16]{3,2,1,0:T(1,128)S(1)} %copy-done, s32[1,1,1]{2,1,0:T(1,128)S(6)} %copy.17.counts, f32[512,4096]{1,0:T(8,128)} %g.9, bf16[512,4096]{1,0:T(8,128)(2,1)} %bitcast.9, ...), custom_call_target="tpu_custom_call" | custom-call | flops 2097152 | bytes 4194304 | tf_op jit(solution)/shard_map/pack/pallas_call | solution.py:361
  5.7 8.6 %all-to-all-start = ((bf16[32,72,128]{2,1,0:T(8,128)(2,1)}), bf16[32,72,128]{2,1,0:T(8,128)(2,1)S(1)}, u32[]{:S(2)}, u32[]{:S(2)}) async-start(bf16[32,72,128]{2,1,0:T(8,128)(2,1)} %get-tuple-element.44), calls=%async_computation | async-start | bytes 1179648 | tf_op jit(solution)/shard_map/all_to_all | solution.py:380
  14.3 1.5 %collective-permute-start = (f32[4,4096]{1,0:T(4,128)S(1)}, f32[4,4096]{1,0:T(4,128)S(1)}, u32[]{:S(2)}, u32[]{:S(2)}) collective-permute-start(f32[4,4096]{1,0:T(4,128)S(1)} %get-tuple-element.51), channel_id=1, source_target_pairs={{0,8},{1,9},{2,10},{3,11},{4,12},{5,13},{6,14},{7,15},{8,16},{9,17... | collective-permute-start | bytes 196616 | tf_op jit(solution)/shard_map/ppermute | solution.py:32
  15.8 2.4 %collective-permute-start.1 = (f32[4,4096]{1,0:T(4,128)S(1)}, f32[4,4096]{1,0:T(4,128)S(1)}, u32[]{:S(2)}, u32[]{:S(2)}) collective-permute-start(f32[4,4096]{1,0:T(4,128)S(1)} %get-tuple-element.52), channel_id=1, source_target_pairs={{0,16},{1,17},{2,18},{3,19},{4,20},{5,21},{6,22},{7,23},{8,24},{9,... | collective-permute-start | bytes 196616 | tf_op jit(solution)/shard_map/ppermute | solution.py:32
  18.2 1.1 %collective-permute-start.2 = (f32[4,4096]{1,0:T(4,128)S(1)}, f32[4,4096]{1,0:T(4,128)S(1)}, u32[]{:S(2)}, u32[]{:S(2)}) collective-permute-start(f32[4,4096]{1,0:T(4,128)S(1)} %get-tuple-element.53), channel_id=1, source_target_pairs={{0,24},{1,25},{2,26},{3,27},{4,28},{5,29},{6,30},{7,31},{8,0},{9,1... | collective-permute-start | bytes 196616 | tf_op jit(solution)/shard_map/ppermute | solution.py:32
  19.4 6.0 %error0.1 = (f32[512,4096]{1,0:T(8,128)}, f32[16,4096]{1,0:T(8,128)S(1)}) custom-call(s32[1,1,1,16]{3,2,1,0:T(1,128)S(1)} %copy-done.1, s32[1,1,1]{2,1,0:T(1,128)S(6)} %copy.17.counts, f32[512,4096]{1,0:T(8,128)} %g.9, bf16[512,4096]{1,0:T(8,128)(2,1)} %bitcast.10, f32[512,4096]{1,0:T(8,128)} %bitcast.5), custom_call_target="tpu_custom_call" | custom-call | flops 12582912 | bytes 11010048 | tf_op jit(solution)/shard_map/error0/pallas_call | solution.py:305
  25.4 0.9 %all-to-all-done.recv = bf16[32,72,128]{2,1,0:T(8,128)(2,1)S(1)} async-done(((bf16[32,72,128]{2,1,0:T(8,128)(2,1)}), bf16[32,72,128]{2,1,0:T(8,128)(2,1)S(1)}, u32[]{:S(2)}, u32[]{:S(2)}) %all-to-all-start) | async-done | bytes 589856 | tf_op jit(solution)/shard_map/all_to_all | solution.py:380
  26.3 0.0 collective-permute-done.m1
  26.3 0.9 %collective-permute-done.1.m2 = f32[4,4096]{1,0:T(4,128)S(1)} collective-permute-done((f32[4,4096]{1,0:T(4,128)S(1)}, f32[4,4096]{1,0:T(4,128)S(1)}, u32[]{:S(2)}, u32[]{:S(2)}) %collective-permute-start.1) | collective-permute-done | bytes 65568 | tf_op jit(solution)/shard_map/ppermute | solution.py:32
  27.2 0.9 %share.1 = (bf16[16,5120]{1,0:T(8,128)(2,1)S(1)}, bf16[16,5120]{1,0:T(8,128)(2,1)S(1)}, bf16[16,5120]{1,0:T(8,128)(2,1)S(1)}, bf16[64,256]{1,0:T(8,128)(2,1)S(1)...) custom-call(bf16[32,72,128]{2,1,0:T(8,128)(2,1)S(1)} %all-to-all-done.recv, ...), custom_call_target="tpu_custom_call" | custom-call | flops 268435456 | bytes 4194304 | tf_op jit(solution)/shard_map/share/pallas_call | solution.py:389
  28.1 0.1 collective-permute-start.3
  28.2 2.4 %collective-permute-start.4 = (bf16[16,5120]{1,0:T(8,128)(2,1)S(1)}, bf16[16,5120]{1,0:T(8,128)(2,1)S(1)}, u32[]{:S(2)}, u32[]{:S(2)}) collective-permute-start(bf16[16,5120]{1,0:T(8,128)(2,1)S(1)} %get-tuple-element.56), channel_id=1, source_target_pairs={{0,2},{1,3},{2,0},{3,1},{4,20},{5,21},{6,22},{7,23},{8,10},{9,11},... | collective-permute-start | bytes 491528 | tf_op jit(solution)/shard_map/ppermute | solution.py:32
  30.6 0.9 %collective-permute-start.5 = (bf16[16,5120]{1,0:T(8,128)(2,1)S(1)}, bf16[16,5120]{1,0:T(8,128)(2,1)S(1)}, u32[]{:S(2)}, u32[]{:S(2)}) collective-permute-start(bf16[16,5120]{1,0:T(8,128)(2,1)S(1)} %get-tuple-element.57), channel_id=1, source_target_pairs={{0,3},{1,0},{2,1},{3,2},{4,28},{5,29},{6,30},{7,31},{8,11},{9,8},{... | collective-permute-start | bytes 491528 | tf_op jit(solution)/shard_map/ppermute | solution.py:32
  31.5 4.6 %error192.1.refs_0_ = f32[512,4096]{1,0:T(8,128)} custom-call(s32[1,1,1,16]{3,2,1,0:T(1,128)S(1)} %copy-done.1, s32[1,1,1]{2,1,0:T(1,128)S(6)} %copy.17.counts, f32[512,4096]{1,0:T(8,128)} %g.9, bf16[512,4096]{1,0:T(8,128)(2,1)} %bitcast.11, f32[512,4096]{1,0:T(8,128)} %bitcast.6, f32[512,4096]{1,0:T(8,128)} %get-tuple-element.59.refs_0_), custom_call_target="tpu_custom_call", output_to_operand_aliasing={{}: (5, {})} | custom-call | flops 8388608 | bytes 7340032 | tf_op jit(solution)/shard_map/error192/pallas_call | solution.py:305
  36.1 0.0 collective-permute-done.3.r1.refs_7_
  36.1 0.1 collective-permute-done.5.r3.refs_9_
  36.2 0.1 group.1
  36.3 3.2 %collective-permute-start.8 = (bf16[64,4352]{1,0:T(8,128)(2,1)S(1)}, bf16[64,4352]{1,0:T(8,128)(2,1)S(1)}, u32[]{:S(2)}, u32[]{:S(2)}) collective-permute-start(bf16[64,4352]{1,0:T(8,128)(2,1)S(1)} %get-tuple-element.67.refs_0_), channel_id=1, source_target_pairs={{0,4},{1,5},{2,6},{3,7},{4,0},{5,1},{6,2},{7,3},{8,12},{9,13},{10,... | collective-permute-start | bytes 1671176 | tf_op jit(solution)/shard_map/ppermute | solution.py:32
  39.5 0.7 %collective-permute-start.6 = (bf16[64,4352]{1,0:T(8,128)(2,1)S(1)}, bf16[64,4352]{1,0:T(8,128)(2,1)S(1)}, u32[]{:S(2)}, u32[]{:S(2)}) collective-permute-start(bf16[64,4352]{1,0:T(8,128)(2,1)S(1)} %get-tuple-element.67.refs_0_), channel_id=1, source_target_pairs={{0,8},{1,9},{2,10},{3,11},{4,5},{5,6},{6,7},{7,4},{8,16},{9,17},{1... | collective-permute-start | bytes 1671176 | tf_op jit(solution)/shard_map/ppermute | solution.py:32
  40.1 2.0 %collective-permute-start.7 = (bf16[64,4352]{1,0:T(8,128)(2,1)S(1)}, bf16[64,4352]{1,0:T(8,128)(2,1)S(1)}, u32[]{:S(2)}, u32[]{:S(2)}) collective-permute-start(bf16[64,4352]{1,0:T(8,128)(2,1)S(1)} %get-tuple-element.68), channel_id=1, source_target_pairs={{0,24},{1,25},{2,26},{3,27},{4,7},{5,4},{6,5},{7,6},{8,0},{9,1},{1... | collective-permute-start | bytes 1671176 | tf_op jit(solution)/shard_map/ppermute | solution.py:32
  42.1 3.8 %error320.1.refs_0_ = f32[512,4096]{1,0:T(8,128)} custom-call(s32[1,1,1,16]{3,2,1,0:T(1,128)S(1)} %copy-done.1, s32[1,1,1]{2,1,0:T(1,128)S(6)} %copy.17.counts, f32[512,4096]{1,0:T(8,128)} %g.9, bf16[512,4096]{1,0:T(8,128)(2,1)} %bitcast.12, f32[512,4096]{1,0:T(8,128)} %bitcast.7, f32[512,4096]{1,0:T(8,128)} %error192.1.refs_0_), custom_call_target="tpu_custom_call", output_to_operand_aliasing={{}: (5, {})} | custom-call | flops 4194304 | bytes 3670016 | tf_op jit(solution)/shard_map/error320/pallas_call | solution.py:305
  45.9 0.5 collective-permute-start.9
  46.4 4.6 %error384.1 = f32[512,4096]{1,0:T(8,128)} custom-call(s32[1,1,1,16]{3,2,1,0:T(1,128)S(1)} %copy-done.1, s32[1,1,1]{2,1,0:T(1,128)S(6)} %copy.17.counts, f32[512,4096]{1,0:T(8,128)} %g.9, bf16[512,4096]{1,0:T(8,128)(2,1)} %bitcast.13, f32[512,4096]{1,0:T(8,128)} %bitcast.8, f32[512,4096]{1,0:T(8,128)} %error320.1.refs_0_), custom_call_target="tpu_custom_call", output_to_operand_aliasing={{}: (5, {})} | custom-call | flops 8388608 | bytes 7340032 | tf_op jit(solution)/shard_map/error384/pallas_call | solution.py:305
  51.0 3.5 %collective-permute-done.7.refs_2_ = bf16[64,4352]{1,0:T(8,128)(2,1)S(1)} collective-permute-done((bf16[64,4352]{1,0:T(8,128)(2,1)S(1)}, bf16[64,4352]{1,0:T(8,128)(2,1)S(1)}, u32[]{:S(2)}, u32[]{:S(2)}) %collective-permute-start.7) | collective-permute-done | bytes 557088 | tf_op jit(solution)/shard_map/ppermute | solution.py:32
  54.6 1.2 %collective-permute-start.10 = (bf16[64,4352]{1,0:T(8,128)(2,1)S(1)}, bf16[64,4352]{1,0:T(8,128)(2,1)S(1)}, u32[]{:S(2)}, u32[]{:S(2)}) collective-permute-start(bf16[64,4352]{1,0:T(8,128)(2,1)S(1)} %collective-permute-done.6.refs_1_.refs_0_), channel_id=1, source_target_pairs={{0,4},{1,5},{2,6},{3,7},{4,0},{5,1},{6,2},{7,3},{8,12},{9,13},{10,... | collective-permute-start | bytes 1671176 | tf_op jit(solution)/shard_map/ppermute | solution.py:32
  55.8 0.4 collective-permute-done.9.refs_1_
  56.2 1.2 %collective-permute-done.10.refs_4_.refs_3_ = bf16[64,4352]{1,0:T(8,128)(2,1)S(1)} collective-permute-done((bf16[64,4352]{1,0:T(8,128)(2,1)S(1)}, bf16[64,4352]{1,0:T(8,128)(2,1)S(1)}, u32[]{:S(2)}, u32[]{:S(2)}) %collective-permute-start.10) | collective-permute-done | bytes 557088 | tf_op jit(solution)/shard_map/ppermute | solution.py:32
  57.4 0.8 %collective-permute-done.11.refs_5_ = bf16[64,4352]{1,0:T(8,128)(2,1)S(1)} collective-permute-done((bf16[64,4352]{1,0:T(8,128)(2,1)S(1)}, bf16[64,4352]{1,0:T(8,128)(2,1)S(1)}, u32[]{:S(2)}, u32[]{:S(2)}) %collective-permute-start.11) | collective-permute-done | bytes 557088 | tf_op jit(solution)/shard_map/ppermute | solution.py:32
  58.2 0.4 collective-permute-start.12
  58.6 3.2 %spread_early.1.refs_6_ = f32[4,128,4096]{2,1,0:T(8,128)} custom-call(bf16[64,4352]{1,0:T(8,128)(2,1)S(1)} %get-tuple-element.67.refs_0_, bf16[64,4352]{1,0:T(8,128)(2,1)S(1)} %collective-permute-done.6.refs_1_.refs_0_, bf16[64,4352]{1,0:T(8,128)(2,1)S(1)} %collective-permute-done.7.refs_2_, bf16[64,4352]{1,0:T(8,128)(2,1)S(1)} %collective-permute-done.8.refs_3_, ...), custom_call_target="tpu_custom_call" | custom-call | flops 16777216 | bytes 8388608 | tf_op jit(solution)/shard_map/spread_early/pallas_call | solution.py:330
  61.8 3.1 %spread_late.1 = (f32[4,128,4096]{2,1,0:T(8,128)}, f32[16,4096]{1,0:T(8,128)}) custom-call(bf16[64,4352]{1,0:T(8,128)(2,1)S(1)} %collective-permute-done.6.refs_1_.refs_0_, bf16[64,4352]{1,0:T(8,128)(2,1)S(1)} %collective-permute-done.9.refs_1_, bf16[64,4352]{1,0:T(8,128)(2,1)S(1)} %collective-permute-done.7.refs_2_, ...), custom_call_target="tpu_custom_call", output_to_operand_aliasing={{0}: (6, {})} | custom-call | flops 16777216 | bytes 5242880 | tf_op jit(solution)/shard_map/spread_late/pallas_call | solution.py:330
  (9 shorter events, 0.0 us)
Async XLA Ops:
  1.3 0.7 %copy-start = (s32[1,1,1,16]{3,2,1,0:T(1,128)S(1)}, s32[1,1,1,16]{3,2,1,0:T(1,128)}, u32[]{:S(2)}) copy-start(s32[1,1,1,16]{3,2,1,0:T(1,128)} %kept.9) | copy-start | bytes 196
  1.9 17.4 %copy-start.1 = (s32[1,1,1,16]{3,2,1,0:T(1,128)S(1)}, s32[1,1,1,16]{3,2,1,0:T(1,128)}, u32[]{:S(2)}) copy-start(s32[1,1,1,16]{3,2,1,0:T(1,128)} %kept.9) | copy-start | bytes 196
  5.7 20.6 %all-to-all-start = ((bf16[32,72,128]{2,1,0:T(8,128)(2,1)}), bf16[32,72,128]{2,1,0:T(8,128)(2,1)S(1)}, u32[]{:S(2)}, u32[]{:S(2)}) async-start(bf16[32,72,128]{2,1,0:T(8,128)(2,1)} %get-tuple-element.44), calls=%async_computation | async-start | bytes 1179648 | tf_op jit(solution)/shard_map/all_to_all | solution.py:380
  14.3 12.0 %collective-permute-start = (f32[4,4096]{1,0:T(4,128)S(1)}, f32[4,4096]{1,0:T(4,128)S(1)}, u32[]{:S(2)}, u32[]{:S(2)}) collective-permute-start(f32[4,4096]{1,0:T(4,128)S(1)} %get-tuple-element.51), channel_id=1, source_target_pairs={{0,8},{1,9},{2,10},{3,11},{4,12},{5,13},{6,14},{7,15},{8,16},{9,17... | collective-permute-start | bytes 196616 | tf_op jit(solution)/shard_map/ppermute | solution.py:32
  15.8 11.4 %collective-permute-start.1 = (f32[4,4096]{1,0:T(4,128)S(1)}, f32[4,4096]{1,0:T(4,128)S(1)}, u32[]{:S(2)}, u32[]{:S(2)}) collective-permute-start(f32[4,4096]{1,0:T(4,128)S(1)} %get-tuple-element.52), channel_id=1, source_target_pairs={{0,16},{1,17},{2,18},{3,19},{4,20},{5,21},{6,22},{7,23},{8,24},{9,... | collective-permute-start | bytes 196616 | tf_op jit(solution)/shard_map/ppermute | solution.py:32
  18.2 9.0 %collective-permute-start.2 = (f32[4,4096]{1,0:T(4,128)S(1)}, f32[4,4096]{1,0:T(4,128)S(1)}, u32[]{:S(2)}, u32[]{:S(2)}) collective-permute-start(f32[4,4096]{1,0:T(4,128)S(1)} %get-tuple-element.53), channel_id=1, source_target_pairs={{0,24},{1,25},{2,26},{3,27},{4,28},{5,29},{6,30},{7,31},{8,0},{9,1... | collective-permute-start | bytes 196616 | tf_op jit(solution)/shard_map/ppermute | solution.py:32
  28.1 8.0 %collective-permute-start.3 = (bf16[16,5120]{1,0:T(8,128)(2,1)S(1)}, bf16[16,5120]{1,0:T(8,128)(2,1)S(1)}, u32[]{:S(2)}, u32[]{:S(2)}) collective-permute-start(bf16[16,5120]{1,0:T(8,128)(2,1)S(1)} %get-tuple-element.55.c1), channel_id=1, source_target_pairs={{0,1},{1,2},{2,3},{3,0},{4,12},{5,13},{6,14},{7,15},{8,9},{9,10},{... | collective-permute-start | bytes 491528 | tf_op jit(solution)/shard_map/ppermute | solution.py:32
  28.2 7.9 %collective-permute-start.4 = (bf16[16,5120]{1,0:T(8,128)(2,1)S(1)}, bf16[16,5120]{1,0:T(8,128)(2,1)S(1)}, u32[]{:S(2)}, u32[]{:S(2)}) collective-permute-start(bf16[16,5120]{1,0:T(8,128)(2,1)S(1)} %get-tuple-element.56), channel_id=1, source_target_pairs={{0,2},{1,3},{2,0},{3,1},{4,20},{5,21},{6,22},{7,23},{8,10},{9,11},... | collective-permute-start | bytes 491528 | tf_op jit(solution)/shard_map/ppermute | solution.py:32
  30.6 5.6 %collective-permute-start.5 = (bf16[16,5120]{1,0:T(8,128)(2,1)S(1)}, bf16[16,5120]{1,0:T(8,128)(2,1)S(1)}, u32[]{:S(2)}, u32[]{:S(2)}) collective-permute-start(bf16[16,5120]{1,0:T(8,128)(2,1)S(1)} %get-tuple-element.57), channel_id=1, source_target_pairs={{0,3},{1,0},{2,1},{3,2},{4,28},{5,29},{6,30},{7,31},{8,11},{9,8},{... | collective-permute-start | bytes 491528 | tf_op jit(solution)/shard_map/ppermute | solution.py:32
  36.3 14.7 %collective-permute-start.8 = (bf16[64,4352]{1,0:T(8,128)(2,1)S(1)}, bf16[64,4352]{1,0:T(8,128)(2,1)S(1)}, u32[]{:S(2)}, u32[]{:S(2)}) collective-permute-start(bf16[64,4352]{1,0:T(8,128)(2,1)S(1)} %get-tuple-element.67.refs_0_), channel_id=1, source_target_pairs={{0,4},{1,5},{2,6},{3,7},{4,0},{5,1},{6,2},{7,3},{8,12},{9,13},{10,... | collective-permute-start | bytes 1671176 | tf_op jit(solution)/shard_map/ppermute | solution.py:32
  39.5 11.6 %collective-permute-start.6 = (bf16[64,4352]{1,0:T(8,128)(2,1)S(1)}, bf16[64,4352]{1,0:T(8,128)(2,1)S(1)}, u32[]{:S(2)}, u32[]{:S(2)}) collective-permute-start(bf16[64,4352]{1,0:T(8,128)(2,1)S(1)} %get-tuple-element.67.refs_0_), channel_id=1, source_target_pairs={{0,8},{1,9},{2,10},{3,11},{4,5},{5,6},{6,7},{7,4},{8,16},{9,17},{1... | collective-permute-start | bytes 1671176 | tf_op jit(solution)/shard_map/ppermute | solution.py:32
  40.1 14.5 %collective-permute-start.7 = (bf16[64,4352]{1,0:T(8,128)(2,1)S(1)}, bf16[64,4352]{1,0:T(8,128)(2,1)S(1)}, u32[]{:S(2)}, u32[]{:S(2)}) collective-permute-start(bf16[64,4352]{1,0:T(8,128)(2,1)S(1)} %get-tuple-element.68), channel_id=1, source_target_pairs={{0,24},{1,25},{2,26},{3,27},{4,7},{5,4},{6,5},{7,6},{8,0},{9,1},{1... | collective-permute-start | bytes 1671176 | tf_op jit(solution)/shard_map/ppermute | solution.py:32
  45.9 10.3 %collective-permute-start.9 = (bf16[64,4352]{1,0:T(8,128)(2,1)S(1)}, bf16[64,4352]{1,0:T(8,128)(2,1)S(1)}, u32[]{:S(2)}, u32[]{:S(2)}) collective-permute-start(bf16[64,4352]{1,0:T(8,128)(2,1)S(1)} %get-tuple-element.75), channel_id=1, source_target_pairs={{0,16},{1,17},{2,18},{3,19},{4,6},{5,7},{6,4},{7,5},{8,24},{9,25},... | collective-permute-start | bytes 1671176 | tf_op jit(solution)/shard_map/ppermute | solution.py:32
  54.6 2.8 %collective-permute-start.10 = (bf16[64,4352]{1,0:T(8,128)(2,1)S(1)}, bf16[64,4352]{1,0:T(8,128)(2,1)S(1)}, u32[]{:S(2)}, u32[]{:S(2)}) collective-permute-start(bf16[64,4352]{1,0:T(8,128)(2,1)S(1)} %collective-permute-done.6.refs_1_.refs_0_), channel_id=1, source_target_pairs={{0,4},{1,5},{2,6},{3,7},{4,0},{5,1},{6,2},{7,3},{8,12},{9,13},{10,... | collective-permute-start | bytes 1671176 | tf_op jit(solution)/shard_map/ppermute | solution.py:32
  55.8 2.4 %collective-permute-start.11 = (bf16[64,4352]{1,0:T(8,128)(2,1)S(1)}, bf16[64,4352]{1,0:T(8,128)(2,1)S(1)}, u32[]{:S(2)}, u32[]{:S(2)}) collective-permute-start(bf16[64,4352]{1,0:T(8,128)(2,1)S(1)} %collective-permute-done.7.refs_2_), channel_id=1, source_target_pairs={{0,4},{1,5},{2,6},{3,7},{4,0},{5,1},{6,2},{7,3},{8,12},{9,13},{10,... | collective-permute-start | bytes 1671176 | tf_op jit(solution)/shard_map/ppermute | solution.py:32
  58.2 3.6 %collective-permute-start.12 = (bf16[64,4352]{1,0:T(8,128)(2,1)S(1)}, bf16[64,4352]{1,0:T(8,128)(2,1)S(1)}, u32[]{:S(2)}, u32[]{:S(2)}) collective-permute-start(bf16[64,4352]{1,0:T(8,128)(2,1)S(1)} %collective-permute-done.9.refs_1_), channel_id=1, source_target_pairs={{0,4},{1,5},{2,6},{3,7},{4,0},{5,1},{6,2},{7,3},{8,12},{9,13},{10,... | collective-permute-start | bytes 1671176 | tf_op jit(solution)/shard_map/ppermute | solution.py:32

commit v4 on v3

--- a/solution.py
+++ b/solution.py
@@ -202,54 +202,45 @@
         copy.wait()
 
 
-def spread_kernel(early, *refs):
-    own, other = refs[:3], refs[3:6]
-    wide, half, sems = refs[-3:]
-    out = refs[6] if early else refs[11]
+def spread_kernel(mine, *refs):
+    groups, (stage, sems) = refs[:4], refs[-2:]
+    out = refs[8] if mine else refs[5]
     y, c, x = place()
-    steps = (0, 1, 3) if early else (1, 2, 3)
+    half = c if mine else 1 - c
     width = BLOCK
 
-    def unit(stage, sem, first, parts_of):
+    def unit(slot, tile, parts_of):
         def body(i, _):
             cols = pl.ds(pl.multiple_of(i * width, width), width)
             parts = [decode(part) for part in parts_of(cols)]
             for q in range(4):
-                stage[q, :, cols] = jnp.concatenate([p[4 * q : 4 * q + 4, :] for p in parts], axis=0)
+                stage[slot, q, :, cols] = jnp.concatenate([p[4 * q : 4 * q + 4, :] for p in parts], axis=0)
             return 0
 
-        lax.fori_loop(0, stage.shape[2] // width, body, 0, unroll=16)
-        rows = pl.ds(pl.multiple_of(first, 8), stage.shape[1])
-        pltpu.make_async_copy(stage, out.at[:, rows, :], sem).start()
+        lax.fori_loop(0, stage.shape[3] // width, body, 0, unroll=16)
+        rows = pl.ds(pl.multiple_of(tile * 16, 16), 16)
+        pltpu.make_async_copy(stage.at[slot], out.at[:, rows, :], sems.at[slot]).start()
 
     def shard(ref, index, cols):
         return ref[pl.ds(pl.multiple_of(index * 16, 16), 16), cols]
 
-    for core in range(2):
-        groups = dict(zip(steps, own if core == 1 else other))
-        groups0 = dict(zip(steps, own if core == 0 else other))
-
-        @pl.when(c == core)
+    @pl.when(half == 1)
+    def _():
+        for d in range(4):
+            unit(d, 4 + (x - d) % 4, lambda cols: [shard(groups[d], (y - q) % 4, cols) for q in range(4)])
+
+    for row in range(4):
+
+        @pl.when((half == 0) & (y == row))
         def _():
-            for n, d in enumerate((0, 1, 3) if early else (2,)):
-                first = 16 * (4 + (x - d) % 4)
-                unit(wide.at[n], sems.at[n], first, lambda cols: [shard(groups[d], (y - q) % 4, cols) for q in range(4)])
-
-        for row in range(4):
-            part = row // 2 if early else 1 - row // 2
-            pair = (2 * part, 2 * part + 1)
-
-            @pl.when((c == core) & (y == row))
-            def _():
-                def each(d, _):
-                    first = 16 * ((x - d) % 4) + 8 * part
-                    unit(half.at[d], sems.at[3 + d], first, lambda cols: [shard(groups0[(row - q) % 4], d, cols) for q in pair])
-                    return 0
-
-                lax.fori_loop(0, 4, each, 0)
-
-    if not early:
-        flats, n0, new_mom, nb = refs[7:10], refs[10], refs[12], refs[13]
+            def each(d, _):
+                unit(d, (x - d) % 4, lambda cols: [shard(groups[(row - q) % 4], d, cols) for q in range(4)])
+                return 0
+
+            lax.fori_loop(0, 4, each, 0)
+
+    if mine:
+        flats, n0, new_mom, nb = refs[4:7], refs[7], refs[9], refs[10]
         nb[y] = n0[...]
         full = nb.shape[2]
 
@@ -267,15 +258,13 @@
 
         @pl.when(c == 0)
         def _():
-            for d, group in enumerate(own, 1):
+            for d, group in enumerate(groups[1:], 1):
                 place_piece(d, group, full, None, jax.ShapeDtypeStruct((64, full // 16), BF16))
 
         for q in range(4):
             new_mom[4 * q : 4 * q + 4, :] = nb[q]
-    for n in range(wide.shape[0]):
-        pltpu.make_async_copy(wide.at[n], out.at[:, pl.ds(0, 16), :], sems.at[n]).wait()
-    for d in range(4):
-        pltpu.make_async_copy(half.at[d], out.at[:, pl.ds(0, 8), :], sems.at[3 + d]).wait()
+    for slot in range(4):
+        pltpu.make_async_copy(stage.at[slot], out.at[:, pl.ds(0, 16), :], sems.at[slot]).wait()
 
 
 def smem():
@@ -324,30 +313,24 @@
     )(kept, counts, in_hbm(g), in_hbm(l), in_hbm(e), *given)
 
 
-def spread(early, own, other, cols, rest=()):
+def spread(groups, cols, before=None, rest=()):
     sds = jax.ShapeDtypeStruct
-    late = not early
+    mine = before is None
     return pl.pallas_call(
-        functools.partial(spread_kernel, early),
-        out_shape=[sds((4, BLOCK, cols), F32)] + [sds((16, cols), F32)] * late,
-        in_specs=[vmem()] * 6 + [hbm()] * late + [vmem()] * (len(rest) - late),
-        out_specs=[hbm()] + [vmem()] * late,
-        input_output_aliases={6: 0} if late else {},
-        scratch_shapes=[pltpu.VMEM((4, 4, cols), F32)] * late
-        + [
-            pltpu.VMEM((3 if early else 1, 4, 16, cols), F32),
-            pltpu.VMEM((4, 4, 8, cols), F32),
-            pltpu.SemaphoreType.DMA((7,)),
-        ],
-        compiler_params=params(24),
-        cost_estimate=pl.CostEstimate(
-            flops=16 * MIB, bytes_accessed=(8 if early else 5) * MIB, transcendentals=(2 if early else 1) * MIB
-        ),
-        name="spread_early" if early else "spread_late",
-    )(*own, *other, *rest)
-
-
-CUTS = (0, 192, 320, 384, 512)
+        functools.partial(spread_kernel, mine),
+        out_shape=[sds((4, BLOCK, cols), F32)] + [sds((16, cols), F32)] * mine,
+        in_specs=[vmem()] * (4 + len(rest)) + [hbm()] * (1 - mine),
+        out_specs=[hbm()] + [vmem()] * mine,
+        input_output_aliases={} if mine else {4: 0},
+        scratch_shapes=[pltpu.VMEM((4, 4, cols), F32)] * mine
+        + [pltpu.VMEM((4, 4, 16, cols), F32), pltpu.SemaphoreType.DMA((4,))],
+        compiler_params=params(16),
+        cost_estimate=pl.CostEstimate(flops=8 * MIB, bytes_accessed=6 * MIB, transcendentals=2 * MIB),
+        name="spread_mine" if mine else "spread_other",
+    )(*groups, *rest, *([] if mine else [before]))
+
+
+CUTS = (0, 256, 320, 512)
 HIGH = 64
 
 
@@ -419,20 +402,13 @@
     def swap(group):
         return move(group, lambda y, c, x: (y, c + 1, x))
 
-    g1, local = lax.optimization_barrier((g1, local))
-    own1, own3, other0 = send(g1, 1), send(g3, 3), swap(g1)
+    g1, g2, g3, local = lax.optimization_barrier((g1, g2, g3, local))
+    own = [g1] + [send(g, d) for d, g in enumerate((g1, g2, g3), 1)]
     new_error, = part(2, local, new_error)
-    g2, local, new_error = lax.optimization_barrier((g2, local, new_error))
-    own2 = send(g2, 2)
-    new_error, = part(3, local, new_error)
-    own1, own3, other0, new_error = lax.optimization_barrier((own1, own3, other0, new_error))
-    other1, other3 = swap(own1), swap(own3)
-    own2, other1, other3 = lax.optimization_barrier((own2, other1, other3))
-    other2 = swap(own2)
-    new_params, = spread(True, [g1, own1, own3], [other0, other1, other3], cols)
-    new_params, new_mom = spread(
-        False, [own1, own2, own3], [other1, other2, other3], cols, [new_params, *first, n0]
-    )
+    own, new_error = lax.optimization_barrier((own, new_error))
+    other = [swap(g) for g in own]
+    new_params, new_mom = spread(own, cols, None, [*first, n0])
+    new_params, = spread(other, cols, new_params)
     return (
         new_params.reshape(rows, cols),
         new_error.reshape(1, 1, rows, cols),

time: 65.2 us -> 62.9 us (0.965)
  Pallas kernels: 30 us -> 27.7 us
    pallas_call x4 -> x3, Pallas kernels: 18.9 us -> 16.6 us  [error_rows(): pl.pallas_call(functools.partial(error_kernel, top), out_shape=[jax.Shape...]
    ppermute x13, waiting for transfers between devices: 6.94 us -> 8.12 us  [move(): return lax.ppermute(array, AXES, pairs)]
    all_to_all x1, waiting for transfers between devices: 0.93 us -> 0.01 us  [per_device(): recv = lax.all_to_all(pay, AXES, 0, 0, tiled=True)]
  transfers between devices with their start and end apart: 14 -> 14, of which waited for: 7 -> 4; matrix products, arithmetic and copies ran while one was open for 0% -> 0% of each run, Pallas kernels for 34% -> 32%
where the time goes in v4:
time: 62.9 us; the launch traced here: 62.6 us
  Pallas kernels  27.7 us (44%)
  starting transfers between devices  24.7 us (39%)
  waiting for transfers between devices  8.12 us (13%)
  between operations  1.4 us (2%)
  local copies, waits for them, and re-layouts  0.65 us (1%)
    pallas_call x3, Pallas kernels, error_rows(): pl.pallas_call(functools.partial(error_kernel, top), out_shape=[jax.Shape...  16.6 us
    ppermute x13, starting transfers between devices, move(): return lax.ppermute(array, AXES, pairs)  16.1 us
    all_to_all x1, starting transfers between devices, per_device(): recv = lax.all_to_all(pay, AXES, 0, 0, tiled=True)  8.6 us
    ppermute x13, waiting for transfers between devices, move(): return lax.ppermute(array, AXES, pairs)  8.12 us
    pallas_call x2, Pallas kernels, spread(): pl.pallas_call(functools.partial(spread_kernel, mine), out_shape=[sds((4,...  6.35 us
    pallas_call x1, Pallas kernels, per_device(): pl.pallas_call(pack_kernel, out_shape=(pltpu.VMEM((DEVICES, 64 + EXTRA, B...  3.78 us
  transfers between devices with their start and end apart: 14, of which 4 were waited for; matrix products, arithmetic and copies ran while one was open for 0% of the time, Pallas kernels for 32%

profile of v4, /device:TPU:1, one launch (start us, length us, event | category | flops | bytes accessed | tf_op | source)
XLA Modules:
  0.0 62.6 jit_solution(8198886293741973864)
XLA Ops:
  1.3 0.6 %copy-done = s32[1,1,1,16]{3,2,1,0:T(1,128)S(1)} copy-done((s32[1,1,1,16]{3,2,1,0:T(1,128)S(1)}, s32[1,1,1,16]{3,2,1,0:T(1,128)}, u32[]{:S(2)}) %copy-start) | copy-done | bytes 88
  1.9 3.8 %pack.1 = (bf16[32,72,128]{2,1,0:T(8,128)(2,1)}, f32[4,4096]{1,0:T(4,128)S(1)}, f32[4,4096]{1,0:T(4,128)S(1)}, f32[4,4096]{1,0:T(4,128)S(1)}, f32[4,4096]{1,0:T(4,128)S(1)}) custom-call(s32[1,1,1,16]{3,2,1,0:T(1,128)S(1)} %copy-done, s32[1,1,1]{2,1,0:T(1,128)S(6)} %copy.15.counts, f32[512,4096]{1,0:T(8,128)} %g.7, bf16[512,4096]{1,0:T(8,128)(2,1)} %bitcast.8, ...), custom_call_target="tpu_custom_call" | custom-call | flops 2097152 | bytes 4194304 | tf_op jit(solution)/shard_map/pack/pallas_call | solution.py:344
  5.7 8.6 %all-to-all-start = ((bf16[32,72,128]{2,1,0:T(8,128)(2,1)}), bf16[32,72,128]{2,1,0:T(8,128)(2,1)S(1)}, u32[]{:S(2)}, u32[]{:S(2)}) async-start(bf16[32,72,128]{2,1,0:T(8,128)(2,1)} %get-tuple-element.41), calls=%async_computation | async-start | bytes 1179648 | tf_op jit(solution)/shard_map/all_to_all | solution.py:363
  14.3 1.5 %collective-permute-start = (f32[4,4096]{1,0:T(4,128)S(1)}, f32[4,4096]{1,0:T(4,128)S(1)}, u32[]{:S(2)}, u32[]{:S(2)}) collective-permute-start(f32[4,4096]{1,0:T(4,128)S(1)} %get-tuple-element.48), channel_id=1, source_target_pairs={{0,8},{1,9},{2,10},{3,11},{4,12},{5,13},{6,14},{7,15},{8,16},{9,17... | collective-permute-start | bytes 196616 | tf_op jit(solution)/shard_map/ppermute | solution.py:32
  15.8 2.4 %collective-permute-start.1 = (f32[4,4096]{1,0:T(4,128)S(1)}, f32[4,4096]{1,0:T(4,128)S(1)}, u32[]{:S(2)}, u32[]{:S(2)}) collective-permute-start(f32[4,4096]{1,0:T(4,128)S(1)} %get-tuple-element.49), channel_id=1, source_target_pairs={{0,16},{1,17},{2,18},{3,19},{4,20},{5,21},{6,22},{7,23},{8,24},{9,... | collective-permute-start | bytes 196616 | tf_op jit(solution)/shard_map/ppermute | solution.py:32
  18.2 1.1 %collective-permute-start.2 = (f32[4,4096]{1,0:T(4,128)S(1)}, f32[4,4096]{1,0:T(4,128)S(1)}, u32[]{:S(2)}, u32[]{:S(2)}) collective-permute-start(f32[4,4096]{1,0:T(4,128)S(1)} %get-tuple-element.50), channel_id=1, source_target_pairs={{0,24},{1,25},{2,26},{3,27},{4,28},{5,29},{6,30},{7,31},{8,0},{9,1... | collective-permute-start | bytes 196616 | tf_op jit(solution)/shard_map/ppermute | solution.py:32
  19.4 7.1 %error0.1 = (f32[512,4096]{1,0:T(8,128)}, f32[16,4096]{1,0:T(8,128)S(1)}) custom-call(s32[1,1,1,16]{3,2,1,0:T(1,128)S(1)} %copy-done.1, s32[1,1,1]{2,1,0:T(1,128)S(6)} %copy.15.counts, f32[512,4096]{1,0:T(8,128)} %g.7, bf16[512,4096]{1,0:T(8,128)(2,1)} %bitcast.9, f32[512,4096]{1,0:T(8,128)} %bitcast.5), custom_call_target="tpu_custom_call" | custom-call | flops 16777216 | bytes 14680064 | tf_op jit(solution)/shard_map/error0/pallas_call | solution.py:294
  26.5 0.0 collective-permute-done.m1
  26.6 0.7 %collective-permute-done.1.m2 = f32[4,4096]{1,0:T(4,128)S(1)} collective-permute-done((f32[4,4096]{1,0:T(4,128)S(1)}, f32[4,4096]{1,0:T(4,128)S(1)}, u32[]{:S(2)}, u32[]{:S(2)}) %collective-permute-start.1) | collective-permute-done | bytes 65568 | tf_op jit(solution)/shard_map/ppermute | solution.py:32
  27.2 0.0 collective-permute-done.2.m3
  27.2 0.9 %share.1 = (bf16[16,5120]{1,0:T(8,128)(2,1)S(1)}, bf16[16,5120]{1,0:T(8,128)(2,1)S(1)}, bf16[16,5120]{1,0:T(8,128)(2,1)S(1)}, bf16[64,256]{1,0:T(8,128)(2,1)S(1)...) custom-call(bf16[32,72,128]{2,1,0:T(8,128)(2,1)S(1)} %all-to-all-done.recv, ...), custom_call_target="tpu_custom_call" | custom-call | flops 268435456 | bytes 4194304 | tf_op jit(solution)/shard_map/share/pallas_call | solution.py:372
  28.1 0.1 collective-permute-start.3
  28.2 2.4 %collective-permute-start.4 = (bf16[16,5120]{1,0:T(8,128)(2,1)S(1)}, bf16[16,5120]{1,0:T(8,128)(2,1)S(1)}, u32[]{:S(2)}, u32[]{:S(2)}) collective-permute-start(bf16[16,5120]{1,0:T(8,128)(2,1)S(1)} %get-tuple-element.53), channel_id=1, source_target_pairs={{0,2},{1,3},{2,0},{3,1},{4,20},{5,21},{6,22},{7,23},{8,10},{9,11},... | collective-permute-start | bytes 491528 | tf_op jit(solution)/shard_map/ppermute | solution.py:32
  30.6 0.9 %collective-permute-start.5 = (bf16[16,5120]{1,0:T(8,128)(2,1)S(1)}, bf16[16,5120]{1,0:T(8,128)(2,1)S(1)}, u32[]{:S(2)}, u32[]{:S(2)}) collective-permute-start(bf16[16,5120]{1,0:T(8,128)(2,1)S(1)} %get-tuple-element.54), channel_id=1, source_target_pairs={{0,3},{1,0},{2,1},{3,2},{4,28},{5,29},{6,30},{7,31},{8,11},{9,8},{... | collective-permute-start | bytes 491528 | tf_op jit(solution)/shard_map/ppermute | solution.py:32
  31.5 3.8 %error256.1.refs_0_ = f32[512,4096]{1,0:T(8,128)} custom-call(s32[1,1,1,16]{3,2,1,0:T(1,128)S(1)} %copy-done.1, s32[1,1,1]{2,1,0:T(1,128)S(6)} %copy.15.counts, f32[512,4096]{1,0:T(8,128)} %g.7, bf16[512,4096]{1,0:T(8,128)(2,1)} %bitcast.10, f32[512,4096]{1,0:T(8,128)} %bitcast.6, f32[512,4096]{1,0:T(8,128)} %get-tuple-element.56.refs_0_), custom_call_target="tpu_custom_call", output_to_operand_aliasing={{}: (5, {})} | custom-call | flops 4194304 | bytes 3670016 | tf_op jit(solution)/shard_map/error256/pallas_call | solution.py:294
  35.3 0.0 collective-permute-done.3.r1.refs_4_
  35.3 0.0 collective-permute-done.4.r2.refs_5_
  35.3 0.9 %collective-permute-done.5.r3.refs_6_ = bf16[16,5120]{1,0:T(8,128)(2,1)S(1)} collective-permute-done((bf16[16,5120]{1,0:T(8,128)(2,1)S(1)}, bf16[16,5120]{1,0:T(8,128)(2,1)S(1)}, u32[]{:S(2)}, u32[]{:S(2)}) %collective-permute-start.5) | collective-permute-done | bytes 163872 | tf_op jit(solution)/shard_map/ppermute | solution.py:32
  36.2 0.1 group.1
  36.3 3.0 %collective-permute-start.7 = (bf16[64,4352]{1,0:T(8,128)(2,1)S(1)}, bf16[64,4352]{1,0:T(8,128)(2,1)S(1)}, u32[]{:S(2)}, u32[]{:S(2)}) collective-permute-start(bf16[64,4352]{1,0:T(8,128)(2,1)S(1)} %get-tuple-element.67), channel_id=1, source_target_pairs={{0,16},{1,17},{2,18},{3,19},{4,6},{5,7},{6,4},{7,5},{8,24},{9,25},... | collective-permute-start | bytes 1671176 | tf_op jit(solution)/shard_map/ppermute | solution.py:32
  39.2 0.7 %collective-permute-start.8 = (bf16[64,4352]{1,0:T(8,128)(2,1)S(1)}, bf16[64,4352]{1,0:T(8,128)(2,1)S(1)}, u32[]{:S(2)}, u32[]{:S(2)}) collective-permute-start(bf16[64,4352]{1,0:T(8,128)(2,1)S(1)} %get-tuple-element.68), channel_id=1, source_target_pairs={{0,24},{1,25},{2,26},{3,27},{4,7},{5,4},{6,5},{7,6},{8,0},{9,1},{1... | collective-permute-start | bytes 1671176 | tf_op jit(solution)/shard_map/ppermute | solution.py:32
  39.9 0.8 %collective-permute-start.6 = (bf16[64,4352]{1,0:T(8,128)(2,1)S(1)}, bf16[64,4352]{1,0:T(8,128)(2,1)S(1)}, u32[]{:S(2)}, u32[]{:S(2)}) collective-permute-start(bf16[64,4352]{1,0:T(8,128)(2,1)S(1)} %get-tuple-element.71.refs_0_), channel_id=1, source_target_pairs={{0,8},{1,9},{2,10},{3,11},{4,5},{5,6},{6,7},{7,4},{8,16},{9,17},{1... | collective-permute-start | bytes 1671176 | tf_op jit(solution)/shard_map/ppermute | solution.py:32
  40.7 5.7 %error320.1 = f32[512,4096]{1,0:T(8,128)} custom-call(s32[1,1,1,16]{3,2,1,0:T(1,128)S(1)} %copy-done.1, s32[1,1,1]{2,1,0:T(1,128)S(6)} %copy.15.counts, f32[512,4096]{1,0:T(8,128)} %g.7, bf16[512,4096]{1,0:T(8,128)(2,1)} %bitcast.11, f32[512,4096]{1,0:T(8,128)} %bitcast.7, f32[512,4096]{1,0:T(8,128)} %error256.1.refs_0_), custom_call_target="tpu_custom_call", output_to_operand_aliasing={{}: (5, {})} | custom-call | flops 12582912 | bytes 11010048 | tf_op jit(solution)/shard_map/error320/pallas_call | solution.py:294
  46.4 0.2 collective-permute-done.7.refs_2_
  46.6 6.3 %collective-permute-done.8.refs_3_ = bf16[64,4352]{1,0:T(8,128)(2,1)S(1)} collective-permute-done((bf16[64,4352]{1,0:T(8,128)(2,1)S(1)}, bf16[64,4352]{1,0:T(8,128)(2,1)S(1)}, u32[]{:S(2)}, u32[]{:S(2)}) %collective-permute-start.8) | collective-permute-done | bytes 557088 | tf_op jit(solution)/shard_map/ppermute | solution.py:32
  52.9 0.0 collective-permute-done.6.refs_1_
  52.9 2.8 %collective-permute-start.9 = (bf16[64,4352]{1,0:T(8,128)(2,1)S(1)}, bf16[64,4352]{1,0:T(8,128)(2,1)S(1)}, u32[]{:S(2)}, u32[]{:S(2)}) collective-permute-start(bf16[64,4352]{1,0:T(8,128)(2,1)S(1)} %get-tuple-element.71.refs_0_), channel_id=1, source_target_pairs={{0,4},{1,5},{2,6},{3,7},{4,0},{5,1},{6,2},{7,3},{8,12},{9,13},{10,... | collective-permute-start | bytes 1671176 | tf_op jit(solution)/shard_map/ppermute | solution.py:32
  55.7 0.0 collective-permute-start.10
  55.7 0.5 collective-permute-start.11
  56.2 0.0 collective-permute-start.12
  56.2 3.5 %spread_mine.1 = (f32[4,128,4096]{2,1,0:T(8,128)}, f32[16,4096]{1,0:T(8,128)}) custom-call(bf16[64,4352]{1,0:T(8,128)(2,1)S(1)} %get-tuple-element.71.refs_0_, bf16[64,4352]{1,0:T(8,128)(2,1)S(1)} %collective-permute-done.6.refs_1_, bf16[64,4352]{1,0:T(8,128)(2,1)S(1)} %collective-permute-done.7.refs_2_, ...), custom_call_target="tpu_custom_call" | custom-call | flops 8388608 | bytes 6291456 | tf_op jit(solution)/shard_map/spread_mine/pallas_call | solution.py:319
  59.8 2.9 %spread_other.1 = f32[4,128,4096]{2,1,0:T(8,128)} custom-call(bf16[64,4352]{1,0:T(8,128)(2,1)S(1)} %collective-permute-done.9.refs_0_, bf16[64,4352]{1,0:T(8,128)(2,1)S(1)} %collective-permute-done.10.refs_1_, bf16[64,4352]{1,0:T(8,128)(2,1)S(1)} %collective-permute-done.11.refs_2_, ...), custom_call_target="tpu_custom_call", output_to_operand_aliasing={{}: (4, {})} | custom-call | flops 8388608 | bytes 6291456 | tf_op jit(solution)/shard_map/spread_other/pallas_call | solution.py:319
  (8 shorter events, 0.0 us)
Async XLA Ops:
  1.3 0.7 %copy-start = (s32[1,1,1,16]{3,2,1,0:T(1,128)S(1)}, s32[1,1,1,16]{3,2,1,0:T(1,128)}, u32[]{:S(2)}) copy-start(s32[1,1,1,16]{3,2,1,0:T(1,128)} %kept.7) | copy-start | bytes 196
  1.9 17.4 %copy-start.1 = (s32[1,1,1,16]{3,2,1,0:T(1,128)S(1)}, s32[1,1,1,16]{3,2,1,0:T(1,128)}, u32[]{:S(2)}) copy-start(s32[1,1,1,16]{3,2,1,0:T(1,128)} %kept.7) | copy-start | bytes 196
  5.7 20.8 %all-to-all-start = ((bf16[32,72,128]{2,1,0:T(8,128)(2,1)}), bf16[32,72,128]{2,1,0:T(8,128)(2,1)S(1)}, u32[]{:S(2)}, u32[]{:S(2)}) async-start(bf16[32,72,128]{2,1,0:T(8,128)(2,1)} %get-tuple-element.41), calls=%async_computation | async-start | bytes 1179648 | tf_op jit(solution)/shard_map/all_to_all | solution.py:363
  14.3 12.2 %collective-permute-start = (f32[4,4096]{1,0:T(4,128)S(1)}, f32[4,4096]{1,0:T(4,128)S(1)}, u32[]{:S(2)}, u32[]{:S(2)}) collective-permute-start(f32[4,4096]{1,0:T(4,128)S(1)} %get-tuple-element.48), channel_id=1, source_target_pairs={{0,8},{1,9},{2,10},{3,11},{4,12},{5,13},{6,14},{7,15},{8,16},{9,17... | collective-permute-start | bytes 196616 | tf_op jit(solution)/shard_map/ppermute | solution.py:32
  15.8 11.4 %collective-permute-start.1 = (f32[4,4096]{1,0:T(4,128)S(1)}, f32[4,4096]{1,0:T(4,128)S(1)}, u32[]{:S(2)}, u32[]{:S(2)}) collective-permute-start(f32[4,4096]{1,0:T(4,128)S(1)} %get-tuple-element.49), channel_id=1, source_target_pairs={{0,16},{1,17},{2,18},{3,19},{4,20},{5,21},{6,22},{7,23},{8,24},{9,... | collective-permute-start | bytes 196616 | tf_op jit(solution)/shard_map/ppermute | solution.py:32
  18.2 9.0 %collective-permute-start.2 = (f32[4,4096]{1,0:T(4,128)S(1)}, f32[4,4096]{1,0:T(4,128)S(1)}, u32[]{:S(2)}, u32[]{:S(2)}) collective-permute-start(f32[4,4096]{1,0:T(4,128)S(1)} %get-tuple-element.50), channel_id=1, source_target_pairs={{0,24},{1,25},{2,26},{3,27},{4,28},{5,29},{6,30},{7,31},{8,0},{9,1... | collective-permute-start | bytes 196616 | tf_op jit(solution)/shard_map/ppermute | solution.py:32
  28.1 7.2 %collective-permute-start.3 = (bf16[16,5120]{1,0:T(8,128)(2,1)S(1)}, bf16[16,5120]{1,0:T(8,128)(2,1)S(1)}, u32[]{:S(2)}, u32[]{:S(2)}) collective-permute-start(bf16[16,5120]{1,0:T(8,128)(2,1)S(1)} %get-tuple-element.52.c1), channel_id=1, source_target_pairs={{0,1},{1,2},{2,3},{3,0},{4,12},{5,13},{6,14},{7,15},{8,9},{9,10},{... | collective-permute-start | bytes 491528 | tf_op jit(solution)/shard_map/ppermute | solution.py:32
  28.2 7.1 %collective-permute-start.4 = (bf16[16,5120]{1,0:T(8,128)(2,1)S(1)}, bf16[16,5120]{1,0:T(8,128)(2,1)S(1)}, u32[]{:S(2)}, u32[]{:S(2)}) collective-permute-start(bf16[16,5120]{1,0:T(8,128)(2,1)S(1)} %get-tuple-element.53), channel_id=1, source_target_pairs={{0,2},{1,3},{2,0},{3,1},{4,20},{5,21},{6,22},{7,23},{8,10},{9,11},... | collective-permute-start | bytes 491528 | tf_op jit(solution)/shard_map/ppermute | solution.py:32
  30.6 5.6 %collective-permute-start.5 = (bf16[16,5120]{1,0:T(8,128)(2,1)S(1)}, bf16[16,5120]{1,0:T(8,128)(2,1)S(1)}, u32[]{:S(2)}, u32[]{:S(2)}) collective-permute-start(bf16[16,5120]{1,0:T(8,128)(2,1)S(1)} %get-tuple-element.54), channel_id=1, source_target_pairs={{0,3},{1,0},{2,1},{3,2},{4,28},{5,29},{6,30},{7,31},{8,11},{9,8},{... | collective-permute-start | bytes 491528 | tf_op jit(solution)/shard_map/ppermute | solution.py:32
  36.3 10.3 %collective-permute-start.7 = (bf16[64,4352]{1,0:T(8,128)(2,1)S(1)}, bf16[64,4352]{1,0:T(8,128)(2,1)S(1)}, u32[]{:S(2)}, u32[]{:S(2)}) collective-permute-start(bf16[64,4352]{1,0:T(8,128)(2,1)S(1)} %get-tuple-element.67), channel_id=1, source_target_pairs={{0,16},{1,17},{2,18},{3,19},{4,6},{5,7},{6,4},{7,5},{8,24},{9,25},... | collective-permute-start | bytes 1671176 | tf_op jit(solution)/shard_map/ppermute | solution.py:32
  39.2 13.7 %collective-permute-start.8 = (bf16[64,4352]{1,0:T(8,128)(2,1)S(1)}, bf16[64,4352]{1,0:T(8,128)(2,1)S(1)}, u32[]{:S(2)}, u32[]{:S(2)}) collective-permute-start(bf16[64,4352]{1,0:T(8,128)(2,1)S(1)} %get-tuple-element.68), channel_id=1, source_target_pairs={{0,24},{1,25},{2,26},{3,27},{4,7},{5,4},{6,5},{7,6},{8,0},{9,1},{1... | collective-permute-start | bytes 1671176 | tf_op jit(solution)/shard_map/ppermute | solution.py:32
  39.9 13.0 %collective-permute-start.6 = (bf16[64,4352]{1,0:T(8,128)(2,1)S(1)}, bf16[64,4352]{1,0:T(8,128)(2,1)S(1)}, u32[]{:S(2)}, u32[]{:S(2)}) collective-permute-start(bf16[64,4352]{1,0:T(8,128)(2,1)S(1)} %get-tuple-element.71.refs_0_), channel_id=1, source_target_pairs={{0,8},{1,9},{2,10},{3,11},{4,5},{5,6},{6,7},{7,4},{8,16},{9,17},{1... | collective-permute-start | bytes 1671176 | tf_op jit(solution)/shard_map/ppermute | solution.py:32
  52.9 6.8 %collective-permute-start.9 = (bf16[64,4352]{1,0:T(8,128)(2,1)S(1)}, bf16[64,4352]{1,0:T(8,128)(2,1)S(1)}, u32[]{:S(2)}, u32[]{:S(2)}) collective-permute-start(bf16[64,4352]{1,0:T(8,128)(2,1)S(1)} %get-tuple-element.71.refs_0_), channel_id=1, source_target_pairs={{0,4},{1,5},{2,6},{3,7},{4,0},{5,1},{6,2},{7,3},{8,12},{9,13},{10,... | collective-permute-start | bytes 1671176 | tf_op jit(solution)/shard_map/ppermute | solution.py:32
  55.7 4.0 %collective-permute-start.10 = (bf16[64,4352]{1,0:T(8,128)(2,1)S(1)}, bf16[64,4352]{1,0:T(8,128)(2,1)S(1)}, u32[]{:S(2)}, u32[]{:S(2)}) collective-permute-start(bf16[64,4352]{1,0:T(8,128)(2,1)S(1)} %collective-permute-done.6.refs_1_), channel_id=1, source_target_pairs={{0,4},{1,5},{2,6},{3,7},{4,0},{5,1},{6,2},{7,3},{8,12},{9,13},{10,... | collective-permute-start | bytes 1671176 | tf_op jit(solution)/shard_map/ppermute | solution.py:32
  55.7 4.0 %collective-permute-start.11 = (bf16[64,4352]{1,0:T(8,128)(2,1)S(1)}, bf16[64,4352]{1,0:T(8,128)(2,1)S(1)}, u32[]{:S(2)}, u32[]{:S(2)}) collective-permute-start(bf16[64,4352]{1,0:T(8,128)(2,1)S(1)} %collective-permute-done.7.refs_2_), channel_id=1, source_target_pairs={{0,4},{1,5},{2,6},{3,7},{4,0},{5,1},{6,2},{7,3},{8,12},{9,13},{10,... | collective-permute-start | bytes 1671176 | tf_op jit(solution)/shard_map/ppermute | solution.py:32
  56.2 3.5 %collective-permute-start.12 = (bf16[64,4352]{1,0:T(8,128)(2,1)S(1)}, bf16[64,4352]{1,0:T(8,128)(2,1)S(1)}, u32[]{:S(2)}, u32[]{:S(2)}) collective-permute-start(bf16[64,4352]{1,0:T(8,128)(2,1)S(1)} %collective-permute-done.8.refs_3_), channel_id=1, source_target_pairs={{0,4},{1,5},{2,6},{3,7},{4,0},{5,1},{6,2},{7,3},{8,12},{9,13},{10,... | collective-permute-start | bytes 1671176 | tf_op jit(solution)/shard_map/ppermute | solution.py:32

commit v5 on v4

--- a/solution.py
+++ b/solution.py
@@ -40,8 +40,7 @@
 
 def decode(code):
     w = code.astype(F32)
-    v = lax.rsqrt(lax.rsqrt(jnp.abs(w))) * (1.0 / SCALE)
-    return jnp.where(w < 0, -v, v)
+    return lax.rsqrt(lax.rsqrt(jnp.abs(w))) * jnp.where(w < 0, -1.0 / SCALE, 1.0 / SCALE)
 
 
 def pick(index, choices):
@@ -217,9 +216,12 @@
                 stage[slot, q, :, cols] = jnp.concatenate([p[4 * q : 4 * q + 4, :] for p in parts], axis=0)
             return 0
 
-        lax.fori_loop(0, stage.shape[3] // width, body, 0, unroll=16)
         rows = pl.ds(pl.multiple_of(tile * 16, 16), 16)
-        pltpu.make_async_copy(stage.at[slot], out.at[:, rows, :], sems.at[slot]).start()
+        part = stage.shape[3] // PIECES
+        for n in range(PIECES):
+            lax.fori_loop(n * part // width, (n + 1) * part // width, body, 0, unroll=True)
+            cols = pl.ds(n * part, part)
+            pltpu.make_async_copy(stage.at[slot, :, :, cols], out.at[:, rows, cols], sems.at[slot]).start()
 
     def shard(ref, index, cols):
         return ref[pl.ds(pl.multiple_of(index * 16, 16), 16), cols]
@@ -332,6 +334,7 @@
 
 CUTS = (0, 256, 320, 512)
 HIGH = 64
+PIECES = 4
 
 
 def per_device(global_params, local_params, error_buf, momentum, kept, counts):

time: 62.9 us -> 62.2 us (0.989)
  Pallas kernels: 27.7 us -> 26.3 us
    pallas_call x2, Pallas kernels: 6.35 us -> 4.92 us  [spread(): pl.pallas_call(functools.partial(spread_kernel, mine), out_shape=[sds((4,...]
  transfers between devices with their start and end apart: 14 -> 14, of which waited for: 4 -> 5; matrix products, arithmetic and copies ran while one was open for 0% -> 0% of each run, Pallas kernels for 32% -> 31%
where the time goes in v5:
time: 62.2 us; the launch traced here: 61.9 us
  Pallas kernels  26.3 us (42%)
  starting transfers between devices  24.7 us (40%)
  waiting for transfers between devices  8.74 us (14%)
  between operations  1.56 us (3%)
  local copies, waits for them, and re-layouts  0.65 us (1%)
    pallas_call x3, Pallas kernels, error_rows(): pl.pallas_call(functools.partial(error_kernel, top), out_shape=[jax.Shape...  16.6 us
    ppermute x13, starting transfers between devices, move(): return lax.ppermute(array, AXES, pairs)  16.1 us
    ppermute x13, waiting for transfers between devices, move(): return lax.ppermute(array, AXES, pairs)  8.73 us
    all_to_all x1, starting transfers between devices, per_device(): recv = lax.all_to_all(pay, AXES, 0, 0, tiled=True)  8.6 us
    pallas_call x2, Pallas kernels, spread(): pl.pallas_call(functools.partial(spread_kernel, mine), out_shape=[sds((4,...  4.92 us
    pallas_call x1, Pallas kernels, per_device(): pl.pallas_call(pack_kernel, out_shape=(pltpu.VMEM((DEVICES, 64 + EXTRA, B...  3.78 us
  transfers between devices with their start and end apart: 14, of which 5 were waited for; matrix products, arithmetic and copies ran while one was open for 0% of the time, Pallas kernels for 31%

profile of v5, /device:TPU:1, one launch (start us, length us, event | category | flops | bytes accessed | tf_op | source)
XLA Modules:
  0.0 61.9 jit_solution(648240212276423275)
XLA Ops:
  1.3 0.6 %copy-done = s32[1,1,1,16]{3,2,1,0:T(1,128)S(1)} copy-done((s32[1,1,1,16]{3,2,1,0:T(1,128)S(1)}, s32[1,1,1,16]{3,2,1,0:T(1,128)}, u32[]{:S(2)}) %copy-start) | copy-done | bytes 88
  1.9 3.8 %pack.1 = (bf16[32,72,128]{2,1,0:T(8,128)(2,1)}, f32[4,4096]{1,0:T(4,128)S(1)}, f32[4,4096]{1,0:T(4,128)S(1)}, f32[4,4096]{1,0:T(4,128)S(1)}, f32[4,4096]{1,0:T(4,128)S(1)}) custom-call(s32[1,1,1,16]{3,2,1,0:T(1,128)S(1)} %copy-done, s32[1,1,1]{2,1,0:T(1,128)S(6)} %copy.15.counts, f32[512,4096]{1,0:T(8,128)} %g.7, bf16[512,4096]{1,0:T(8,128)(2,1)} %bitcast.8, ...), custom_call_target="tpu_custom_call" | custom-call | flops 2097152 | bytes 4194304 | tf_op jit(solution)/shard_map/pack/pallas_call | solution.py:347
  5.7 8.6 %all-to-all-start = ((bf16[32,72,128]{2,1,0:T(8,128)(2,1)}), bf16[32,72,128]{2,1,0:T(8,128)(2,1)S(1)}, u32[]{:S(2)}, u32[]{:S(2)}) async-start(bf16[32,72,128]{2,1,0:T(8,128)(2,1)} %get-tuple-element.41), calls=%async_computation | async-start | bytes 1179648 | tf_op jit(solution)/shard_map/all_to_all | solution.py:366
  14.3 1.5 %collective-permute-start = (f32[4,4096]{1,0:T(4,128)S(1)}, f32[4,4096]{1,0:T(4,128)S(1)}, u32[]{:S(2)}, u32[]{:S(2)}) collective-permute-start(f32[4,4096]{1,0:T(4,128)S(1)} %get-tuple-element.48), channel_id=1, source_target_pairs={{0,8},{1,9},{2,10},{3,11},{4,12},{5,13},{6,14},{7,15},{8,16},{9,17... | collective-permute-start | bytes 196616 | tf_op jit(solution)/shard_map/ppermute | solution.py:32
  15.8 2.4 %collective-permute-start.1 = (f32[4,4096]{1,0:T(4,128)S(1)}, f32[4,4096]{1,0:T(4,128)S(1)}, u32[]{:S(2)}, u32[]{:S(2)}) collective-permute-start(f32[4,4096]{1,0:T(4,128)S(1)} %get-tuple-element.49), channel_id=1, source_target_pairs={{0,16},{1,17},{2,18},{3,19},{4,20},{5,21},{6,22},{7,23},{8,24},{9,... | collective-permute-start | bytes 196616 | tf_op jit(solution)/shard_map/ppermute | solution.py:32
  18.2 1.1 %collective-permute-start.2 = (f32[4,4096]{1,0:T(4,128)S(1)}, f32[4,4096]{1,0:T(4,128)S(1)}, u32[]{:S(2)}, u32[]{:S(2)}) collective-permute-start(f32[4,4096]{1,0:T(4,128)S(1)} %get-tuple-element.50), channel_id=1, source_target_pairs={{0,24},{1,25},{2,26},{3,27},{4,28},{5,29},{6,30},{7,31},{8,0},{9,1... | collective-permute-start | bytes 196616 | tf_op jit(solution)/shard_map/ppermute | solution.py:32
  19.4 7.1 %error0.1 = (f32[512,4096]{1,0:T(8,128)}, f32[16,4096]{1,0:T(8,128)S(1)}) custom-call(s32[1,1,1,16]{3,2,1,0:T(1,128)S(1)} %copy-done.1, s32[1,1,1]{2,1,0:T(1,128)S(6)} %copy.15.counts, f32[512,4096]{1,0:T(8,128)} %g.7, bf16[512,4096]{1,0:T(8,128)(2,1)} %bitcast.9, f32[512,4096]{1,0:T(8,128)} %bitcast.5), custom_call_target="tpu_custom_call" | custom-call | flops 16777216 | bytes 14680064 | tf_op jit(solution)/shard_map/error0/pallas_call | solution.py:296
  26.5 0.0 collective-permute-done.m1
  26.6 0.7 %collective-permute-done.1.m2 = f32[4,4096]{1,0:T(4,128)S(1)} collective-permute-done((f32[4,4096]{1,0:T(4,128)S(1)}, f32[4,4096]{1,0:T(4,128)S(1)}, u32[]{:S(2)}, u32[]{:S(2)}) %collective-permute-start.1) | collective-permute-done | bytes 65568 | tf_op jit(solution)/shard_map/ppermute | solution.py:32
  27.2 0.0 collective-permute-done.2.m3
  27.2 0.9 %share.1 = (bf16[16,5120]{1,0:T(8,128)(2,1)S(1)}, bf16[16,5120]{1,0:T(8,128)(2,1)S(1)}, bf16[16,5120]{1,0:T(8,128)(2,1)S(1)}, bf16[64,256]{1,0:T(8,128)(2,1)S(1)...) custom-call(bf16[32,72,128]{2,1,0:T(8,128)(2,1)S(1)} %all-to-all-done.recv, ...), custom_call_target="tpu_custom_call" | custom-call | flops 268435456 | bytes 4194304 | tf_op jit(solution)/shard_map/share/pallas_call | solution.py:375
  28.1 0.1 collective-permute-start.3
  28.2 2.4 %collective-permute-start.4 = (bf16[16,5120]{1,0:T(8,128)(2,1)S(1)}, bf16[16,5120]{1,0:T(8,128)(2,1)S(1)}, u32[]{:S(2)}, u32[]{:S(2)}) collective-permute-start(bf16[16,5120]{1,0:T(8,128)(2,1)S(1)} %get-tuple-element.53), channel_id=1, source_target_pairs={{0,2},{1,3},{2,0},{3,1},{4,20},{5,21},{6,22},{7,23},{8,10},{9,11},... | collective-permute-start | bytes 491528 | tf_op jit(solution)/shard_map/ppermute | solution.py:32
  30.6 0.9 %collective-permute-start.5 = (bf16[16,5120]{1,0:T(8,128)(2,1)S(1)}, bf16[16,5120]{1,0:T(8,128)(2,1)S(1)}, u32[]{:S(2)}, u32[]{:S(2)}) collective-permute-start(bf16[16,5120]{1,0:T(8,128)(2,1)S(1)} %get-tuple-element.54), channel_id=1, source_target_pairs={{0,3},{1,0},{2,1},{3,2},{4,28},{5,29},{6,30},{7,31},{8,11},{9,8},{... | collective-permute-start | bytes 491528 | tf_op jit(solution)/shard_map/ppermute | solution.py:32
  31.5 3.8 %error256.1.refs_0_ = f32[512,4096]{1,0:T(8,128)} custom-call(s32[1,1,1,16]{3,2,1,0:T(1,128)S(1)} %copy-done.1, s32[1,1,1]{2,1,0:T(1,128)S(6)} %copy.15.counts, f32[512,4096]{1,0:T(8,128)} %g.7, bf16[512,4096]{1,0:T(8,128)(2,1)} %bitcast.10, f32[512,4096]{1,0:T(8,128)} %bitcast.6, f32[512,4096]{1,0:T(8,128)} %get-tuple-element.56.refs_0_), custom_call_target="tpu_custom_call", output_to_operand_aliasing={{}: (5, {})} | custom-call | flops 4194304 | bytes 3670016 | tf_op jit(solution)/shard_map/error256/pallas_call | solution.py:296
  35.3 0.0 collective-permute-done.3.r1.refs_4_
  35.3 0.0 collective-permute-done.4.r2.refs_5_
  35.3 0.9 %collective-permute-done.5.r3.refs_6_ = bf16[16,5120]{1,0:T(8,128)(2,1)S(1)} collective-permute-done((bf16[16,5120]{1,0:T(8,128)(2,1)S(1)}, bf16[16,5120]{1,0:T(8,128)(2,1)S(1)}, u32[]{:S(2)}, u32[]{:S(2)}) %collective-permute-start.5) | collective-permute-done | bytes 163872 | tf_op jit(solution)/shard_map/ppermute | solution.py:32
  36.2 0.1 group.1
  36.3 2.9 %collective-permute-start.7 = (bf16[64,4352]{1,0:T(8,128)(2,1)S(1)}, bf16[64,4352]{1,0:T(8,128)(2,1)S(1)}, u32[]{:S(2)}, u32[]{:S(2)}) collective-permute-start(bf16[64,4352]{1,0:T(8,128)(2,1)S(1)} %get-tuple-element.67), channel_id=1, source_target_pairs={{0,16},{1,17},{2,18},{3,19},{4,6},{5,7},{6,4},{7,5},{8,24},{9,25},... | collective-permute-start | bytes 1671176 | tf_op jit(solution)/shard_map/ppermute | solution.py:32
  39.2 0.7 %collective-permute-start.8 = (bf16[64,4352]{1,0:T(8,128)(2,1)S(1)}, bf16[64,4352]{1,0:T(8,128)(2,1)S(1)}, u32[]{:S(2)}, u32[]{:S(2)}) collective-permute-start(bf16[64,4352]{1,0:T(8,128)(2,1)S(1)} %get-tuple-element.68), channel_id=1, source_target_pairs={{0,24},{1,25},{2,26},{3,27},{4,7},{5,4},{6,5},{7,6},{8,0},{9,1},{1... | collective-permute-start | bytes 1671176 | tf_op jit(solution)/shard_map/ppermute | solution.py:32
  39.9 0.8 %collective-permute-start.6 = (bf16[64,4352]{1,0:T(8,128)(2,1)S(1)}, bf16[64,4352]{1,0:T(8,128)(2,1)S(1)}, u32[]{:S(2)}, u32[]{:S(2)}) collective-permute-start(bf16[64,4352]{1,0:T(8,128)(2,1)S(1)} %get-tuple-element.71.refs_0_), channel_id=1, source_target_pairs={{0,8},{1,9},{2,10},{3,11},{4,5},{5,6},{6,7},{7,4},{8,16},{9,17},{1... | collective-permute-start | bytes 1671176 | tf_op jit(solution)/shard_map/ppermute | solution.py:32
  40.7 5.7 %error320.1 = f32[512,4096]{1,0:T(8,128)} custom-call(s32[1,1,1,16]{3,2,1,0:T(1,128)S(1)} %copy-done.1, s32[1,1,1]{2,1,0:T(1,128)S(6)} %copy.15.counts, f32[512,4096]{1,0:T(8,128)} %g.7, bf16[512,4096]{1,0:T(8,128)(2,1)} %bitcast.11, f32[512,4096]{1,0:T(8,128)} %bitcast.7, f32[512,4096]{1,0:T(8,128)} %error256.1.refs_0_), custom_call_target="tpu_custom_call", output_to_operand_aliasing={{}: (5, {})} | custom-call | flops 12582912 | bytes 11010048 | tf_op jit(solution)/shard_map/error320/pallas_call | solution.py:296
  46.4 0.2 collective-permute-done.7.refs_2_
  46.6 6.3 %collective-permute-done.8.refs_3_ = bf16[64,4352]{1,0:T(8,128)(2,1)S(1)} collective-permute-done((bf16[64,4352]{1,0:T(8,128)(2,1)S(1)}, bf16[64,4352]{1,0:T(8,128)(2,1)S(1)}, u32[]{:S(2)}, u32[]{:S(2)}) %collective-permute-start.8) | collective-permute-done | bytes 557088 | tf_op jit(solution)/shard_map/ppermute | solution.py:32
  52.9 2.8 %collective-permute-start.9 = (bf16[64,4352]{1,0:T(8,128)(2,1)S(1)}, bf16[64,4352]{1,0:T(8,128)(2,1)S(1)}, u32[]{:S(2)}, u32[]{:S(2)}) collective-permute-start(bf16[64,4352]{1,0:T(8,128)(2,1)S(1)} %get-tuple-element.71.refs_0_), channel_id=1, source_target_pairs={{0,4},{1,5},{2,6},{3,7},{4,0},{5,1},{6,2},{7,3},{8,12},{9,13},{10,... | collective-permute-start | bytes 1671176 | tf_op jit(solution)/shard_map/ppermute | solution.py:32
  55.7 0.0 collective-permute-start.10
  55.7 0.5 collective-permute-start.11
  56.2 0.0 collective-permute-start.12
  56.2 2.8 %spread_mine.1 = (f32[4,128,4096]{2,1,0:T(8,128)}, f32[16,4096]{1,0:T(8,128)}) custom-call(bf16[64,4352]{1,0:T(8,128)(2,1)S(1)} %get-tuple-element.71.refs_0_, bf16[64,4352]{1,0:T(8,128)(2,1)S(1)} %collective-permute-done.6.refs_1_, bf16[64,4352]{1,0:T(8,128)(2,1)S(1)} %collective-permute-done.7.refs_2_, ...), custom_call_target="tpu_custom_call" | custom-call | flops 8388608 | bytes 6291456 | tf_op jit(solution)/shard_map/spread_mine/pallas_call | solution.py:321
  59.1 0.6 collective-permute-done.12.refs_3_
  59.7 2.1 %spread_other.1 = f32[4,128,4096]{2,1,0:T(8,128)} custom-call(bf16[64,4352]{1,0:T(8,128)(2,1)S(1)} %collective-permute-done.9.refs_0_, bf16[64,4352]{1,0:T(8,128)(2,1)S(1)} %collective-permute-done.10.refs_1_, bf16[64,4352]{1,0:T(8,128)(2,1)S(1)} %collective-permute-done.11.refs_2_, ...), custom_call_target="tpu_custom_call", output_to_operand_aliasing={{}: (4, {})} | custom-call | flops 8388608 | bytes 6291456 | tf_op jit(solution)/shard_map/spread_other/pallas_call | solution.py:321
  (8 shorter events, 0.0 us)
Async XLA Ops:
  1.3 0.7 %copy-start = (s32[1,1,1,16]{3,2,1,0:T(1,128)S(1)}, s32[1,1,1,16]{3,2,1,0:T(1,128)}, u32[]{:S(2)}) copy-start(s32[1,1,1,16]{3,2,1,0:T(1,128)} %kept.7) | copy-start | bytes 196
  1.9 17.4 %copy-start.1 = (s32[1,1,1,16]{3,2,1,0:T(1,128)S(1)}, s32[1,1,1,16]{3,2,1,0:T(1,128)}, u32[]{:S(2)}) copy-start(s32[1,1,1,16]{3,2,1,0:T(1,128)} %kept.7) | copy-start | bytes 196
  5.7 20.8 %all-to-all-start = ((bf16[32,72,128]{2,1,0:T(8,128)(2,1)}), bf16[32,72,128]{2,1,0:T(8,128)(2,1)S(1)}, u32[]{:S(2)}, u32[]{:S(2)}) async-start(bf16[32,72,128]{2,1,0:T(8,128)(2,1)} %get-tuple-element.41), calls=%async_computation | async-start | bytes 1179648 | tf_op jit(solution)/shard_map/all_to_all | solution.py:366
  14.3 12.2 %collective-permute-start = (f32[4,4096]{1,0:T(4,128)S(1)}, f32[4,4096]{1,0:T(4,128)S(1)}, u32[]{:S(2)}, u32[]{:S(2)}) collective-permute-start(f32[4,4096]{1,0:T(4,128)S(1)} %get-tuple-element.48), channel_id=1, source_target_pairs={{0,8},{1,9},{2,10},{3,11},{4,12},{5,13},{6,14},{7,15},{8,16},{9,17... | collective-permute-start | bytes 196616 | tf_op jit(solution)/shard_map/ppermute | solution.py:32
  15.8 11.4 %collective-permute-start.1 = (f32[4,4096]{1,0:T(4,128)S(1)}, f32[4,4096]{1,0:T(4,128)S(1)}, u32[]{:S(2)}, u32[]{:S(2)}) collective-permute-start(f32[4,4096]{1,0:T(4,128)S(1)} %get-tuple-element.49), channel_id=1, source_target_pairs={{0,16},{1,17},{2,18},{3,19},{4,20},{5,21},{6,22},{7,23},{8,24},{9,... | collective-permute-start | bytes 196616 | tf_op jit(solution)/shard_map/ppermute | solution.py:32
  18.2 9.0 %collective-permute-start.2 = (f32[4,4096]{1,0:T(4,128)S(1)}, f32[4,4096]{1,0:T(4,128)S(1)}, u32[]{:S(2)}, u32[]{:S(2)}) collective-permute-start(f32[4,4096]{1,0:T(4,128)S(1)} %get-tuple-element.50), channel_id=1, source_target_pairs={{0,24},{1,25},{2,26},{3,27},{4,28},{5,29},{6,30},{7,31},{8,0},{9,1... | collective-permute-start | bytes 196616 | tf_op jit(solution)/shard_map/ppermute | solution.py:32
  28.1 7.2 %collective-permute-start.3 = (bf16[16,5120]{1,0:T(8,128)(2,1)S(1)}, bf16[16,5120]{1,0:T(8,128)(2,1)S(1)}, u32[]{:S(2)}, u32[]{:S(2)}) collective-permute-start(bf16[16,5120]{1,0:T(8,128)(2,1)S(1)} %get-tuple-element.52.c1), channel_id=1, source_target_pairs={{0,1},{1,2},{2,3},{3,0},{4,12},{5,13},{6,14},{7,15},{8,9},{9,10},{... | collective-permute-start | bytes 491528 | tf_op jit(solution)/shard_map/ppermute | solution.py:32
  28.2 7.1 %collective-permute-start.4 = (bf16[16,5120]{1,0:T(8,128)(2,1)S(1)}, bf16[16,5120]{1,0:T(8,128)(2,1)S(1)}, u32[]{:S(2)}, u32[]{:S(2)}) collective-permute-start(bf16[16,5120]{1,0:T(8,128)(2,1)S(1)} %get-tuple-element.53), channel_id=1, source_target_pairs={{0,2},{1,3},{2,0},{3,1},{4,20},{5,21},{6,22},{7,23},{8,10},{9,11},... | collective-permute-start | bytes 491528 | tf_op jit(solution)/shard_map/ppermute | solution.py:32
  30.6 5.6 %collective-permute-start.5 = (bf16[16,5120]{1,0:T(8,128)(2,1)S(1)}, bf16[16,5120]{1,0:T(8,128)(2,1)S(1)}, u32[]{:S(2)}, u32[]{:S(2)}) collective-permute-start(bf16[16,5120]{1,0:T(8,128)(2,1)S(1)} %get-tuple-element.54), channel_id=1, source_target_pairs={{0,3},{1,0},{2,1},{3,2},{4,28},{5,29},{6,30},{7,31},{8,11},{9,8},{... | collective-permute-start | bytes 491528 | tf_op jit(solution)/shard_map/ppermute | solution.py:32
  36.3 10.3 %collective-permute-start.7 = (bf16[64,4352]{1,0:T(8,128)(2,1)S(1)}, bf16[64,4352]{1,0:T(8,128)(2,1)S(1)}, u32[]{:S(2)}, u32[]{:S(2)}) collective-permute-start(bf16[64,4352]{1,0:T(8,128)(2,1)S(1)} %get-tuple-element.67), channel_id=1, source_target_pairs={{0,16},{1,17},{2,18},{3,19},{4,6},{5,7},{6,4},{7,5},{8,24},{9,25},... | collective-permute-start | bytes 1671176 | tf_op jit(solution)/shard_map/ppermute | solution.py:32
  39.2 13.7 %collective-permute-start.8 = (bf16[64,4352]{1,0:T(8,128)(2,1)S(1)}, bf16[64,4352]{1,0:T(8,128)(2,1)S(1)}, u32[]{:S(2)}, u32[]{:S(2)}) collective-permute-start(bf16[64,4352]{1,0:T(8,128)(2,1)S(1)} %get-tuple-element.68), channel_id=1, source_target_pairs={{0,24},{1,25},{2,26},{3,27},{4,7},{5,4},{6,5},{7,6},{8,0},{9,1},{1... | collective-permute-start | bytes 1671176 | tf_op jit(solution)/shard_map/ppermute | solution.py:32
  39.9 13.0 %collective-permute-start.6 = (bf16[64,4352]{1,0:T(8,128)(2,1)S(1)}, bf16[64,4352]{1,0:T(8,128)(2,1)S(1)}, u32[]{:S(2)}, u32[]{:S(2)}) collective-permute-start(bf16[64,4352]{1,0:T(8,128)(2,1)S(1)} %get-tuple-element.71.refs_0_), channel_id=1, source_target_pairs={{0,8},{1,9},{2,10},{3,11},{4,5},{5,6},{6,7},{7,4},{8,16},{9,17},{1... | collective-permute-start | bytes 1671176 | tf_op jit(solution)/shard_map/ppermute | solution.py:32
  52.9 6.1 %collective-permute-start.9 = (bf16[64,4352]{1,0:T(8,128)(2,1)S(1)}, bf16[64,4352]{1,0:T(8,128)(2,1)S(1)}, u32[]{:S(2)}, u32[]{:S(2)}) collective-permute-start(bf16[64,4352]{1,0:T(8,128)(2,1)S(1)} %get-tuple-element.71.refs_0_), channel_id=1, source_target_pairs={{0,4},{1,5},{2,6},{3,7},{4,0},{5,1},{6,2},{7,3},{8,12},{9,13},{10,... | collective-permute-start | bytes 1671176 | tf_op jit(solution)/shard_map/ppermute | solution.py:32
  55.7 3.3 %collective-permute-start.10 = (bf16[64,4352]{1,0:T(8,128)(2,1)S(1)}, bf16[64,4352]{1,0:T(8,128)(2,1)S(1)}, u32[]{:S(2)}, u32[]{:S(2)}) collective-permute-start(bf16[64,4352]{1,0:T(8,128)(2,1)S(1)} %collective-permute-done.6.refs_1_), channel_id=1, source_target_pairs={{0,4},{1,5},{2,6},{3,7},{4,0},{5,1},{6,2},{7,3},{8,12},{9,13},{10,... | collective-permute-start | bytes 1671176 | tf_op jit(solution)/shard_map/ppermute | solution.py:32
  55.7 3.4 %collective-permute-start.11 = (bf16[64,4352]{1,0:T(8,128)(2,1)S(1)}, bf16[64,4352]{1,0:T(8,128)(2,1)S(1)}, u32[]{:S(2)}, u32[]{:S(2)}) collective-permute-start(bf16[64,4352]{1,0:T(8,128)(2,1)S(1)} %collective-permute-done.7.refs_2_), channel_id=1, source_target_pairs={{0,4},{1,5},{2,6},{3,7},{4,0},{5,1},{6,2},{7,3},{8,12},{9,13},{10,... | collective-permute-start | bytes 1671176 | tf_op jit(solution)/shard_map/ppermute | solution.py:32
  56.2 3.5 %collective-permute-start.12 = (bf16[64,4352]{1,0:T(8,128)(2,1)S(1)}, bf16[64,4352]{1,0:T(8,128)(2,1)S(1)}, u32[]{:S(2)}, u32[]{:S(2)}) collective-permute-start(bf16[64,4352]{1,0:T(8,128)(2,1)S(1)} %collective-permute-done.8.refs_3_), channel_id=1, source_target_pairs={{0,4},{1,5},{2,6},{3,7},{4,0},{5,1},{6,2},{7,3},{8,12},{9,13},{10,... | collective-permute-start | bytes 1671176 | tf_op jit(solution)/shard_map/ppermute | solution.py:32

commit v6 on v5

--- a/solution.py
+++ b/solution.py
@@ -332,7 +332,7 @@
     )(*groups, *rest, *([] if mine else [before]))
 
 
-CUTS = (0, 256, 320, 512)
+CUTS = (0, 256, 320, 448, 512)
 HIGH = 64
 PIECES = 4
 
@@ -362,7 +362,7 @@
         name="pack",
     )(kept, counts, in_hbm(global_params), in_hbm(local), in_hbm(error), in_hbm(momentum))
 
-    m1, m2, m3 = [move(m, lambda y, c, x, d=d: (y + d, c, x)) for d, m in ((1, m1), (2, m2), (3, m3))]
+    m2, m1, m3 = [move(m, lambda y, c, x, d=d: (y + d, c, x)) for d, m in ((2, m2), (1, m1), (3, m3))]
     recv = lax.all_to_all(pay, AXES, 0, 0, tiled=True)
     def part(n, local, before):
         return error_rows(CUTS[n], CUTS[n + 1] - CUTS[n], HIGH, kept, counts, global_params, local, error, before)
@@ -408,8 +408,11 @@
     g1, g2, g3, local = lax.optimization_barrier((g1, g2, g3, local))
     own = [g1] + [send(g, d) for d, g in enumerate((g1, g2, g3), 1)]
     new_error, = part(2, local, new_error)
-    own, new_error = lax.optimization_barrier((own, new_error))
-    other = [swap(g) for g in own]
+    own[2], local, new_error = lax.optimization_barrier((own[2], local, new_error))
+    other0, other2 = swap(own[0]), swap(own[2])
+    new_error, = part(3, local, new_error)
+    own[1], own[3], other0, other2, new_error = lax.optimization_barrier((own[1], own[3], other0, other2, new_error))
+    other = [other0, swap(own[1]), other2, swap(own[3])]
     new_params, new_mom = spread(own, cols, None, [*first, n0])
     new_params, = spread(other, cols, new_params)
     return (

time: 62.2 us -> 61.4 us (0.987)
  waiting for transfers between devices: 8.74 us -> 1.62 us
  starting transfers between devices: 24.7 us -> 28 us
  Pallas kernels: 26.3 us -> 29.2 us
    ppermute x13, waiting for transfers between devices: 8.73 us -> 1.62 us  [move(): return lax.ppermute(array, AXES, pairs)]
    ppermute x13, starting transfers between devices: 16.1 us -> 19.4 us  [move(): return lax.ppermute(array, AXES, pairs)]
    pallas_call x3 -> x4, Pallas kernels: 16.6 us -> 19.3 us  [error_rows(): pl.pallas_call(functools.partial(error_kernel, top), out_shape=[jax.Shape...]
  transfers between devices with their start and end apart: 14 -> 14, of which waited for: 5 -> 2; matrix products, arithmetic and copies ran while one was open for 0% -> 0% of each run, Pallas kernels for 31% -> 36%
where the time goes in v6:
time: 61.4 us; the launch traced here: 61 us
  Pallas kernels  29.2 us (48%)
  starting transfers between devices  28 us (46%)
  waiting for transfers between devices  1.62 us (3%)
  between operations  1.59 us (3%)
  local copies, waits for them, and re-layouts  0.65 us (1%)
    ppermute x13, starting transfers between devices, move(): return lax.ppermute(array, AXES, pairs)  19.4 us
    pallas_call x4, Pallas kernels, error_rows(): pl.pallas_call(functools.partial(error_kernel, top), out_shape=[jax.Shape...  19.3 us
    all_to_all x1, starting transfers between devices, per_device(): recv = lax.all_to_all(pay, AXES, 0, 0, tiled=True)  8.6 us
    pallas_call x2, Pallas kernels, spread(): pl.pallas_call(functools.partial(spread_kernel, mine), out_shape=[sds((4,...  5.13 us
    pallas_call x1, Pallas kernels, per_device(): pl.pallas_call(pack_kernel, out_shape=(pltpu.VMEM((DEVICES, 64 + EXTRA, B...  3.78 us
    ppermute x13, waiting for transfers between devices, move(): return lax.ppermute(array, AXES, pairs)  1.62 us
  transfers between devices with their start and end apart: 14, of which 2 were waited for; matrix products, arithmetic and copies ran while one was open for 0% of the time, Pallas kernels for 36%

profile of v6, /device:TPU:1, one launch (start us, length us, event | category | flops | bytes accessed | tf_op | source)
XLA Modules:
  0.0 61.0 jit_solution(5069086394254139809)
XLA Ops:
  1.3 0.6 %copy-done = s32[1,1,1,16]{3,2,1,0:T(1,128)S(1)} copy-done((s32[1,1,1,16]{3,2,1,0:T(1,128)S(1)}, s32[1,1,1,16]{3,2,1,0:T(1,128)}, u32[]{:S(2)}) %copy-start) | copy-done | bytes 88
  1.9 3.8 %pack.1 = (bf16[32,72,128]{2,1,0:T(8,128)(2,1)}, f32[4,4096]{1,0:T(4,128)S(1)}, f32[4,4096]{1,0:T(4,128)S(1)}, f32[4,4096]{1,0:T(4,128)S(1)}, f32[4,4096]{1,0:T(4,128)S(1)}) custom-call(s32[1,1,1,16]{3,2,1,0:T(1,128)S(1)} %copy-done, s32[1,1,1]{2,1,0:T(1,128)S(6)} %copy.17.counts, f32[512,4096]{1,0:T(8,128)} %g.9, bf16[512,4096]{1,0:T(8,128)(2,1)} %bitcast.9, ...), custom_call_target="tpu_custom_call" | custom-call | flops 2097152 | bytes 4194304 | tf_op jit(solution)/shard_map/pack/pallas_call | solution.py:347
  5.7 8.6 %all-to-all-start = ((bf16[32,72,128]{2,1,0:T(8,128)(2,1)}), bf16[32,72,128]{2,1,0:T(8,128)(2,1)S(1)}, u32[]{:S(2)}, u32[]{:S(2)}) async-start(bf16[32,72,128]{2,1,0:T(8,128)(2,1)} %get-tuple-element.44), calls=%async_computation | async-start | bytes 1179648 | tf_op jit(solution)/shard_map/all_to_all | solution.py:366
  14.3 1.5 %collective-permute-start = (f32[4,4096]{1,0:T(4,128)S(1)}, f32[4,4096]{1,0:T(4,128)S(1)}, u32[]{:S(2)}, u32[]{:S(2)}) collective-permute-start(f32[4,4096]{1,0:T(4,128)S(1)} %get-tuple-element.51), channel_id=1, source_target_pairs={{0,8},{1,9},{2,10},{3,11},{4,12},{5,13},{6,14},{7,15},{8,16},{9,17... | collective-permute-start | bytes 196616 | tf_op jit(solution)/shard_map/ppermute | solution.py:32
  15.8 2.4 %collective-permute-start.1 = (f32[4,4096]{1,0:T(4,128)S(1)}, f32[4,4096]{1,0:T(4,128)S(1)}, u32[]{:S(2)}, u32[]{:S(2)}) collective-permute-start(f32[4,4096]{1,0:T(4,128)S(1)} %get-tuple-element.52), channel_id=1, source_target_pairs={{0,16},{1,17},{2,18},{3,19},{4,20},{5,21},{6,22},{7,23},{8,24},{9,... | collective-permute-start | bytes 196616 | tf_op jit(solution)/shard_map/ppermute | solution.py:32
  18.2 1.1 %collective-permute-start.2 = (f32[4,4096]{1,0:T(4,128)S(1)}, f32[4,4096]{1,0:T(4,128)S(1)}, u32[]{:S(2)}, u32[]{:S(2)}) collective-permute-start(f32[4,4096]{1,0:T(4,128)S(1)} %get-tuple-element.53), channel_id=1, source_target_pairs={{0,24},{1,25},{2,26},{3,27},{4,28},{5,29},{6,30},{7,31},{8,0},{9,1... | collective-permute-start | bytes 196616 | tf_op jit(solution)/shard_map/ppermute | solution.py:32
  19.4 7.1 %error0.1 = (f32[512,4096]{1,0:T(8,128)}, f32[16,4096]{1,0:T(8,128)S(1)}) custom-call(s32[1,1,1,16]{3,2,1,0:T(1,128)S(1)} %copy-done.1, s32[1,1,1]{2,1,0:T(1,128)S(6)} %copy.17.counts, f32[512,4096]{1,0:T(8,128)} %g.9, bf16[512,4096]{1,0:T(8,128)(2,1)} %bitcast.10, f32[512,4096]{1,0:T(8,128)} %bitcast.5), custom_call_target="tpu_custom_call" | custom-call | flops 16777216 | bytes 14680064 | tf_op jit(solution)/shard_map/error0/pallas_call | solution.py:296
  26.5 0.0 all-to-all-done.recv
  26.6 0.7 %collective-permute-done.1.m2 = f32[4,4096]{1,0:T(4,128)S(1)} collective-permute-done((f32[4,4096]{1,0:T(4,128)S(1)}, f32[4,4096]{1,0:T(4,128)S(1)}, u32[]{:S(2)}, u32[]{:S(2)}) %collective-permute-start.1) | collective-permute-done | bytes 65568 | tf_op jit(solution)/shard_map/ppermute | solution.py:32
  27.2 0.9 %share.1 = (bf16[16,5120]{1,0:T(8,128)(2,1)S(1)}, bf16[16,5120]{1,0:T(8,128)(2,1)S(1)}, bf16[16,5120]{1,0:T(8,128)(2,1)S(1)}, bf16[64,256]{1,0:T(8,128)(2,1)S(1)...) custom-call(bf16[32,72,128]{2,1,0:T(8,128)(2,1)S(1)} %all-to-all-done.recv, ...), custom_call_target="tpu_custom_call" | custom-call | flops 268435456 | bytes 4194304 | tf_op jit(solution)/shard_map/share/pallas_call | solution.py:375
  28.1 0.1 collective-permute-start.3
  28.2 2.4 %collective-permute-start.4 = (bf16[16,5120]{1,0:T(8,128)(2,1)S(1)}, bf16[16,5120]{1,0:T(8,128)(2,1)S(1)}, u32[]{:S(2)}, u32[]{:S(2)}) collective-permute-start(bf16[16,5120]{1,0:T(8,128)(2,1)S(1)} %get-tuple-element.56), channel_id=1, source_target_pairs={{0,2},{1,3},{2,0},{3,1},{4,20},{5,21},{6,22},{7,23},{8,10},{9,11},... | collective-permute-start | bytes 491528 | tf_op jit(solution)/shard_map/ppermute | solution.py:32
  30.6 0.9 %collective-permute-start.5 = (bf16[16,5120]{1,0:T(8,128)(2,1)S(1)}, bf16[16,5120]{1,0:T(8,128)(2,1)S(1)}, u32[]{:S(2)}, u32[]{:S(2)}) collective-permute-start(bf16[16,5120]{1,0:T(8,128)(2,1)S(1)} %get-tuple-element.57), channel_id=1, source_target_pairs={{0,3},{1,0},{2,1},{3,2},{4,28},{5,29},{6,30},{7,31},{8,11},{9,8},{... | collective-permute-start | bytes 491528 | tf_op jit(solution)/shard_map/ppermute | solution.py:32
  31.5 3.8 %error256.1.refs_0_ = f32[512,4096]{1,0:T(8,128)} custom-call(s32[1,1,1,16]{3,2,1,0:T(1,128)S(1)} %copy-done.1, s32[1,1,1]{2,1,0:T(1,128)S(6)} %copy.17.counts, f32[512,4096]{1,0:T(8,128)} %g.9, bf16[512,4096]{1,0:T(8,128)(2,1)} %bitcast.11, f32[512,4096]{1,0:T(8,128)} %bitcast.6, f32[512,4096]{1,0:T(8,128)} %get-tuple-element.59.refs_0_), custom_call_target="tpu_custom_call", output_to_operand_aliasing={{}: (5, {})} | custom-call | flops 4194304 | bytes 3670016 | tf_op jit(solution)/shard_map/error256/pallas_call | solution.py:296
  35.3 0.0 collective-permute-done.3.r1.refs_4_
  35.3 0.0 collective-permute-done.4.r2.refs_5_
  35.3 0.9 %collective-permute-done.5.r3.refs_6_ = bf16[16,5120]{1,0:T(8,128)(2,1)S(1)} collective-permute-done((bf16[16,5120]{1,0:T(8,128)(2,1)S(1)}, bf16[16,5120]{1,0:T(8,128)(2,1)S(1)}, u32[]{:S(2)}, u32[]{:S(2)}) %collective-permute-start.5) | collective-permute-done | bytes 163872 | tf_op jit(solution)/shard_map/ppermute | solution.py:32
  36.2 0.1 group.1
  36.3 2.9 %collective-permute-start.9 = (bf16[64,4352]{1,0:T(8,128)(2,1)S(1)}, bf16[64,4352]{1,0:T(8,128)(2,1)S(1)}, u32[]{:S(2)}, u32[]{:S(2)}) collective-permute-start(bf16[64,4352]{1,0:T(8,128)(2,1)S(1)} %get-tuple-element.71), channel_id=1, source_target_pairs={{0,16},{1,17},{2,18},{3,19},{4,6},{5,7},{6,4},{7,5},{8,24},{9,25},... | collective-permute-start | bytes 1671176 | tf_op jit(solution)/shard_map/ppermute | solution.py:32
  39.2 0.7 %collective-permute-start.8 = (bf16[64,4352]{1,0:T(8,128)(2,1)S(1)}, bf16[64,4352]{1,0:T(8,128)(2,1)S(1)}, u32[]{:S(2)}, u32[]{:S(2)}) collective-permute-start(bf16[64,4352]{1,0:T(8,128)(2,1)S(1)} %get-tuple-element.69.refs_0_), channel_id=1, source_target_pairs={{0,4},{1,5},{2,6},{3,7},{4,0},{5,1},{6,2},{7,3},{8,12},{9,13},{10,... | collective-permute-start | bytes 1671176 | tf_op jit(solution)/shard_map/ppermute | solution.py:32
  39.9 1.7 %collective-permute-start.6 = (bf16[64,4352]{1,0:T(8,128)(2,1)S(1)}, bf16[64,4352]{1,0:T(8,128)(2,1)S(1)}, u32[]{:S(2)}, u32[]{:S(2)}) collective-permute-start(bf16[64,4352]{1,0:T(8,128)(2,1)S(1)} %get-tuple-element.69.refs_0_), channel_id=1, source_target_pairs={{0,8},{1,9},{2,10},{3,11},{4,5},{5,6},{6,7},{7,4},{8,16},{9,17},{1... | collective-permute-start | bytes 1671176 | tf_op jit(solution)/shard_map/ppermute | solution.py:32
  41.6 1.0 %collective-permute-start.7 = (bf16[64,4352]{1,0:T(8,128)(2,1)S(1)}, bf16[64,4352]{1,0:T(8,128)(2,1)S(1)}, u32[]{:S(2)}, u32[]{:S(2)}) collective-permute-start(bf16[64,4352]{1,0:T(8,128)(2,1)S(1)} %get-tuple-element.70), channel_id=1, source_target_pairs={{0,24},{1,25},{2,26},{3,27},{4,7},{5,4},{6,5},{7,6},{8,0},{9,1},{1... | collective-permute-start | bytes 1671176 | tf_op jit(solution)/shard_map/ppermute | solution.py:32
  42.6 4.7 %error320.1.refs_0_ = f32[512,4096]{1,0:T(8,128)} custom-call(s32[1,1,1,16]{3,2,1,0:T(1,128)S(1)} %copy-done.1, s32[1,1,1]{2,1,0:T(1,128)S(6)} %copy.17.counts, f32[512,4096]{1,0:T(8,128)} %g.9, bf16[512,4096]{1,0:T(8,128)(2,1)} %bitcast.12, f32[512,4096]{1,0:T(8,128)} %bitcast.7, f32[512,4096]{1,0:T(8,128)} %error256.1.refs_0_), custom_call_target="tpu_custom_call", output_to_operand_aliasing={{}: (5, {})} | custom-call | flops 8388608 | bytes 7340032 | tf_op jit(solution)/shard_map/error320/pallas_call | solution.py:296
  47.3 0.0 collective-permute-done.9.refs_2_
  47.3 2.5 %collective-permute-start.10 = (bf16[64,4352]{1,0:T(8,128)(2,1)S(1)}, bf16[64,4352]{1,0:T(8,128)(2,1)S(1)}, u32[]{:S(2)}, u32[]{:S(2)}) collective-permute-start(bf16[64,4352]{1,0:T(8,128)(2,1)S(1)} %collective-permute-done.9.refs_2_), channel_id=1, source_target_pairs={{0,4},{1,5},{2,6},{3,7},{4,0},{5,1},{6,2},{7,3},{8,12},{9,13},{10,... | collective-permute-start | bytes 1671176 | tf_op jit(solution)/shard_map/ppermute | solution.py:32
  49.8 3.8 %error448.1 = f32[512,4096]{1,0:T(8,128)} custom-call(s32[1,1,1,16]{3,2,1,0:T(1,128)S(1)} %copy-done.1, s32[1,1,1]{2,1,0:T(1,128)S(6)} %copy.17.counts, f32[512,4096]{1,0:T(8,128)} %g.9, bf16[512,4096]{1,0:T(8,128)(2,1)} %bitcast.13, f32[512,4096]{1,0:T(8,128)} %bitcast.8, f32[512,4096]{1,0:T(8,128)} %error320.1.refs_0_), custom_call_target="tpu_custom_call", output_to_operand_aliasing={{}: (5, {})} | custom-call | flops 4194304 | bytes 3670016 | tf_op jit(solution)/shard_map/error448/pallas_call | solution.py:296
  53.6 0.0 collective-permute-done.6.refs_1_
  53.6 2.1 %collective-permute-start.11 = (bf16[64,4352]{1,0:T(8,128)(2,1)S(1)}, bf16[64,4352]{1,0:T(8,128)(2,1)S(1)}, u32[]{:S(2)}, u32[]{:S(2)}) collective-permute-start(bf16[64,4352]{1,0:T(8,128)(2,1)S(1)} %collective-permute-done.6.refs_1_), channel_id=1, source_target_pairs={{0,4},{1,5},{2,6},{3,7},{4,0},{5,1},{6,2},{7,3},{8,12},{9,13},{10,... | collective-permute-start | bytes 1671176 | tf_op jit(solution)/shard_map/ppermute | solution.py:32
  55.7 0.0 collective-permute-start.12
  55.7 2.8 %spread_mine.1 = (f32[4,128,4096]{2,1,0:T(8,128)}, f32[16,4096]{1,0:T(8,128)}) custom-call(bf16[64,4352]{1,0:T(8,128)(2,1)S(1)} %get-tuple-element.69.refs_0_, bf16[64,4352]{1,0:T(8,128)(2,1)S(1)} %collective-permute-done.6.refs_1_, bf16[64,4352]{1,0:T(8,128)(2,1)S(1)} %collective-permute-done.9.refs_2_, ...), custom_call_target="tpu_custom_call" | custom-call | flops 8388608 | bytes 6291456 | tf_op jit(solution)/shard_map/spread_mine/pallas_call | solution.py:321
  58.5 0.0 collective-permute-done.11.refs_1_
  58.5 2.3 %spread_other.1 = f32[4,128,4096]{2,1,0:T(8,128)} custom-call(bf16[64,4352]{1,0:T(8,128)(2,1)S(1)} %collective-permute-done.8.refs_0_, bf16[64,4352]{1,0:T(8,128)(2,1)S(1)} %collective-permute-done.11.refs_1_, bf16[64,4352]{1,0:T(8,128)(2,1)S(1)} %collective-permute-done.10.refs_2_, ...), custom_call_target="tpu_custom_call", output_to_operand_aliasing={{}: (4, {})} | custom-call | flops 8388608 | bytes 6291456 | tf_op jit(solution)/shard_map/spread_other/pallas_call | solution.py:321
  (9 shorter events, 0.0 us)
Async XLA Ops:
  1.3 0.7 %copy-start = (s32[1,1,1,16]{3,2,1,0:T(1,128)S(1)}, s32[1,1,1,16]{3,2,1,0:T(1,128)}, u32[]{:S(2)}) copy-start(s32[1,1,1,16]{3,2,1,0:T(1,128)} %kept.9) | copy-start | bytes 196
  1.9 17.4 %copy-start.1 = (s32[1,1,1,16]{3,2,1,0:T(1,128)S(1)}, s32[1,1,1,16]{3,2,1,0:T(1,128)}, u32[]{:S(2)}) copy-start(s32[1,1,1,16]{3,2,1,0:T(1,128)} %kept.9) | copy-start | bytes 196
  5.7 20.8 %all-to-all-start = ((bf16[32,72,128]{2,1,0:T(8,128)(2,1)}), bf16[32,72,128]{2,1,0:T(8,128)(2,1)S(1)}, u32[]{:S(2)}, u32[]{:S(2)}) async-start(bf16[32,72,128]{2,1,0:T(8,128)(2,1)} %get-tuple-element.44), calls=%async_computation | async-start | bytes 1179648 | tf_op jit(solution)/shard_map/all_to_all | solution.py:366
  14.3 12.2 %collective-permute-start = (f32[4,4096]{1,0:T(4,128)S(1)}, f32[4,4096]{1,0:T(4,128)S(1)}, u32[]{:S(2)}, u32[]{:S(2)}) collective-permute-start(f32[4,4096]{1,0:T(4,128)S(1)} %get-tuple-element.51), channel_id=1, source_target_pairs={{0,8},{1,9},{2,10},{3,11},{4,12},{5,13},{6,14},{7,15},{8,16},{9,17... | collective-permute-start | bytes 196616 | tf_op jit(solution)/shard_map/ppermute | solution.py:32
  15.8 11.4 %collective-permute-start.1 = (f32[4,4096]{1,0:T(4,128)S(1)}, f32[4,4096]{1,0:T(4,128)S(1)}, u32[]{:S(2)}, u32[]{:S(2)}) collective-permute-start(f32[4,4096]{1,0:T(4,128)S(1)} %get-tuple-element.52), channel_id=1, source_target_pairs={{0,16},{1,17},{2,18},{3,19},{4,20},{5,21},{6,22},{7,23},{8,24},{9,... | collective-permute-start | bytes 196616 | tf_op jit(solution)/shard_map/ppermute | solution.py:32
  18.2 9.0 %collective-permute-start.2 = (f32[4,4096]{1,0:T(4,128)S(1)}, f32[4,4096]{1,0:T(4,128)S(1)}, u32[]{:S(2)}, u32[]{:S(2)}) collective-permute-start(f32[4,4096]{1,0:T(4,128)S(1)} %get-tuple-element.53), channel_id=1, source_target_pairs={{0,24},{1,25},{2,26},{3,27},{4,28},{5,29},{6,30},{7,31},{8,0},{9,1... | collective-permute-start | bytes 196616 | tf_op jit(solution)/shard_map/ppermute | solution.py:32
  28.1 7.2 %collective-permute-start.3 = (bf16[16,5120]{1,0:T(8,128)(2,1)S(1)}, bf16[16,5120]{1,0:T(8,128)(2,1)S(1)}, u32[]{:S(2)}, u32[]{:S(2)}) collective-permute-start(bf16[16,5120]{1,0:T(8,128)(2,1)S(1)} %get-tuple-element.55.c1), channel_id=1, source_target_pairs={{0,1},{1,2},{2,3},{3,0},{4,12},{5,13},{6,14},{7,15},{8,9},{9,10},{... | collective-permute-start | bytes 491528 | tf_op jit(solution)/shard_map/ppermute | solution.py:32
  28.2 7.1 %collective-permute-start.4 = (bf16[16,5120]{1,0:T(8,128)(2,1)S(1)}, bf16[16,5120]{1,0:T(8,128)(2,1)S(1)}, u32[]{:S(2)}, u32[]{:S(2)}) collective-permute-start(bf16[16,5120]{1,0:T(8,128)(2,1)S(1)} %get-tuple-element.56), channel_id=1, source_target_pairs={{0,2},{1,3},{2,0},{3,1},{4,20},{5,21},{6,22},{7,23},{8,10},{9,11},... | collective-permute-start | bytes 491528 | tf_op jit(solution)/shard_map/ppermute | solution.py:32
  30.6 5.6 %collective-permute-start.5 = (bf16[16,5120]{1,0:T(8,128)(2,1)S(1)}, bf16[16,5120]{1,0:T(8,128)(2,1)S(1)}, u32[]{:S(2)}, u32[]{:S(2)}) collective-permute-start(bf16[16,5120]{1,0:T(8,128)(2,1)S(1)} %get-tuple-element.57), channel_id=1, source_target_pairs={{0,3},{1,0},{2,1},{3,2},{4,28},{5,29},{6,30},{7,31},{8,11},{9,8},{... | collective-permute-start | bytes 491528 | tf_op jit(solution)/shard_map/ppermute | solution.py:32
  36.3 11.0 %collective-permute-start.9 = (bf16[64,4352]{1,0:T(8,128)(2,1)S(1)}, bf16[64,4352]{1,0:T(8,128)(2,1)S(1)}, u32[]{:S(2)}, u32[]{:S(2)}) collective-permute-start(bf16[64,4352]{1,0:T(8,128)(2,1)S(1)} %get-tuple-element.71), channel_id=1, source_target_pairs={{0,16},{1,17},{2,18},{3,19},{4,6},{5,7},{6,4},{7,5},{8,24},{9,25},... | collective-permute-start | bytes 1671176 | tf_op jit(solution)/shard_map/ppermute | solution.py:32
  39.2 14.4 %collective-permute-start.8 = (bf16[64,4352]{1,0:T(8,128)(2,1)S(1)}, bf16[64,4352]{1,0:T(8,128)(2,1)S(1)}, u32[]{:S(2)}, u32[]{:S(2)}) collective-permute-start(bf16[64,4352]{1,0:T(8,128)(2,1)S(1)} %get-tuple-element.69.refs_0_), channel_id=1, source_target_pairs={{0,4},{1,5},{2,6},{3,7},{4,0},{5,1},{6,2},{7,3},{8,12},{9,13},{10,... | collective-permute-start | bytes 1671176 | tf_op jit(solution)/shard_map/ppermute | solution.py:32
  39.9 13.7 %collective-permute-start.6 = (bf16[64,4352]{1,0:T(8,128)(2,1)S(1)}, bf16[64,4352]{1,0:T(8,128)(2,1)S(1)}, u32[]{:S(2)}, u32[]{:S(2)}) collective-permute-start(bf16[64,4352]{1,0:T(8,128)(2,1)S(1)} %get-tuple-element.69.refs_0_), channel_id=1, source_target_pairs={{0,8},{1,9},{2,10},{3,11},{4,5},{5,6},{6,7},{7,4},{8,16},{9,17},{1... | collective-permute-start | bytes 1671176 | tf_op jit(solution)/shard_map/ppermute | solution.py:32
  41.6 12.0 %collective-permute-start.7 = (bf16[64,4352]{1,0:T(8,128)(2,1)S(1)}, bf16[64,4352]{1,0:T(8,128)(2,1)S(1)}, u32[]{:S(2)}, u32[]{:S(2)}) collective-permute-start(bf16[64,4352]{1,0:T(8,128)(2,1)S(1)} %get-tuple-element.70), channel_id=1, source_target_pairs={{0,24},{1,25},{2,26},{3,27},{4,7},{5,4},{6,5},{7,6},{8,0},{9,1},{1... | collective-permute-start | bytes 1671176 | tf_op jit(solution)/shard_map/ppermute | solution.py:32
  47.3 6.3 %collective-permute-start.10 = (bf16[64,4352]{1,0:T(8,128)(2,1)S(1)}, bf16[64,4352]{1,0:T(8,128)(2,1)S(1)}, u32[]{:S(2)}, u32[]{:S(2)}) collective-permute-start(bf16[64,4352]{1,0:T(8,128)(2,1)S(1)} %collective-permute-done.9.refs_2_), channel_id=1, source_target_pairs={{0,4},{1,5},{2,6},{3,7},{4,0},{5,1},{6,2},{7,3},{8,12},{9,13},{10,... | collective-permute-start | bytes 1671176 | tf_op jit(solution)/shard_map/ppermute | solution.py:32
  53.6 4.9 %collective-permute-start.11 = (bf16[64,4352]{1,0:T(8,128)(2,1)S(1)}, bf16[64,4352]{1,0:T(8,128)(2,1)S(1)}, u32[]{:S(2)}, u32[]{:S(2)}) collective-permute-start(bf16[64,4352]{1,0:T(8,128)(2,1)S(1)} %collective-permute-done.6.refs_1_), channel_id=1, source_target_pairs={{0,4},{1,5},{2,6},{3,7},{4,0},{5,1},{6,2},{7,3},{8,12},{9,13},{10,... | collective-permute-start | bytes 1671176 | tf_op jit(solution)/shard_map/ppermute | solution.py:32
  55.7 2.8 %collective-permute-start.12 = (bf16[64,4352]{1,0:T(8,128)(2,1)S(1)}, bf16[64,4352]{1,0:T(8,128)(2,1)S(1)}, u32[]{:S(2)}, u32[]{:S(2)}) collective-permute-start(bf16[64,4352]{1,0:T(8,128)(2,1)S(1)} %collective-permute-done.7.refs_3_), channel_id=1, source_target_pairs={{0,4},{1,5},{2,6},{3,7},{4,0},{5,1},{6,2},{7,3},{8,12},{9,13},{10,... | collective-permute-start | bytes 1671176 | tf_op jit(solution)/shard_map/ppermute | solution.py:32
